TPU v7x, 128 devices: a whole 4x4x4 slice. The times are simulated.
128 devices in a mesh: dp: 32 (over z_lo, x, y), tensor: 4 (over z_hi, core).
Axes of the slice: x: 4, y: 4, z: 4 (z_hi: 2, z_lo: 2; z = z_hi * 2 + z_lo), core: 2. Of those that a mesh axis runs over, the one named last changes fastest.
Arguments:
- hidden_in: bfloat16 [16384, 2048], P('dp'), may hold values from -6 to 6
- segment_ids: int32 [16384], P('dp'), may hold values from 0 to 3, as said below
- positions: int32 [16384], P('dp'), may hold values from 0 to 508, as said below
- ln1_gain: float32 [2048], replicated, may hold values from 0.1 to 1.9
- ln1_bias: float32 [2048], replicated, may hold values from -3 to 3
- qkv_weight: bfloat16 [2048, 6144], P(None, 'tensor'), may hold values from -0.125 to 0.125
- qkv_bias: float32 [8, 768], P('tensor'), may hold values from -3 to 3
- dense_weight: bfloat16 [2048, 2048], P('tensor'), may hold values from -0.5 to 0.5
- dense_bias: float32 [2048], replicated, may hold values from -3 to 3
- ln2_gain: float32 [2048], replicated, may hold values from 0.1 to 1.9
- ln2_bias: float32 [2048], replicated, may hold values from -3 to 3
- fc1_weight: bfloat16 [2048, 8192], P(None, 'tensor'), may hold values from -0.125 to 0.125
- fc1_bias: float32 [64, 128], P('tensor'), may hold values from -3 to 3
- fc2_weight: bfloat16 [8192, 2048], P('tensor'), may hold values from -0.0625 to 0.0625
- fc2_bias: float32 [2048], replicated, may hold values from -3 to 3
- cotangent: bfloat16 [16384, 2048], P('dp'), may hold values from -6 to 6
Outputs:
- output: float32 [16384, 2048], P('dp')
- input_grad: float32 [16384, 2048], P('dp')
- ln1_gain_grad: float32 [2048], P('dp')
- ln1_bias_grad: float32 [2048], P('dp')
- qkv_weight_grad: float32 [2048, 6144], P('dp', 'tensor')
- qkv_bias_grad: float32 [8, 768], P('tensor', 'dp')
- dense_weight_grad: float32 [2048, 2048], P('tensor', 'dp')
- dense_bias_grad: float32 [2048], P('dp')
- ln2_gain_grad: float32 [2048], P('dp')
- ln2_bias_grad: float32 [2048], P('dp')
- fc1_weight_grad: float32 [2048, 8192], P('dp', 'tensor')
- fc1_bias_grad: float32 [64, 128], P('tensor', 'dp')
- fc2_weight_grad: float32 [8192, 2048], P('tensor', 'dp')
- fc2_bias_grad: float32 [2048], P('dp')
Inputs may be any that keep to these rules, and one draw needn't show every extreme that they name: `segment_ids`: within each sequence of 512 tokens the segment numbers start at 0, never fall, and take each of the 4 values. `positions`: A token's index in its sequence minus the index of its document's first token.
All inputs are finite; a program needn't handle non-finite values.
Results may differ from a plain program's by a relative error of at most 0.011.
Values sent between devices are 32-bit elements; how exact they have to be, the bound alone decides.
No kernel may reach another device: no remote copies, remote signals or barrier semaphores. Data moves between devices by JAX's collectives and lax.ppermute only.
A program may use at most 256 MiB of HBM per device.

v0:
```python
from functools import partial
import math

import jax
import jax.numpy as jnp
from jax import lax
from jax.experimental import pallas as pl
from jax.experimental.pallas import tpu as pltpu
from jax.sharding import Mesh, PartitionSpec as P

HD = 256
ROT = 64
TOK = 512
D = 2048
EPSILON = 1e-05
NEGATIVE = -1000000000.0
SIZES = {"zl": 2, "x": 4, "y": 4, "zh": 2, "c": 2}
DP = ("zl", "x", "y")
TENSOR = ("zh", "c")
F32 = jnp.float32
BF16 = jnp.bfloat16


def send(value, axis, step=1):
    n = SIZES[axis]
    return lax.ppermute(value, axis, [(i, (i + step) % n) for i in range(n)])


def swap(value, axis, bit):
    return lax.ppermute(value, axis, [(i, i ^ bit) for i in range(SIZES[axis])])


def plain_dot(left, right):
    return jnp.dot(left, right, preferred_element_type=F32)


def contract_cols(left, right):
    return lax.dot_general(left, right, (((1,), (1,)), ((), ())), preferred_element_type=F32)


VMEM = 56 * 1024 * 1024
COST = pl.CostEstimate(flops=1000000, bytes_accessed=1000000, transcendentals=0)


def whole(shape):
    return pl.BlockSpec(shape, lambda *_: (0,) * len(shape), pipeline_mode=pl.Buffered(1))


def put_turned(target, rows):
    for z in range(2):
        for pair in range(8):
            start = z * 1024 + pair * 128
            block = rows[:, start : start + 128].T.astype(BF16)
            target[2 * pair, z] = block[:64]
            target[2 * pair + 1, z] = block[64:]


def normalise(hidden):
    average = jnp.mean(hidden, axis=-1, keepdims=True)
    centred = hidden - average
    inv_std = lax.rsqrt(jnp.mean(centred * centred, axis=-1, keepdims=True) + EPSILON)
    return centred * inv_std, inv_std


def second_kernel(hidden, cot, gain, shift, second_out, cot_turned):
    normed, _ = normalise(hidden[...].astype(F32))
    second_out[...] = (normed * gain[...] + shift[...]).astype(BF16)
    put_turned(cot_turned, cot[...].astype(F32))


def first_kernel(hidden, gain, shift, gain_two, shift_two, first_out, first_turned, second_turned):
    normed, _ = normalise(hidden[...].astype(F32))
    first = normed * gain[...] + shift[...]
    first_out[...] = first.astype(BF16)
    put_turned(first_turned, first)
    put_turned(second_turned, normed * gain_two[...] + shift_two[...])


def far_kernel(near, other, gain, shift, gain_two, shift_two, *refs):
    first_out, second_out, cot_out, first_turned, second_turned, cot_turned = refs[3:]

    def step(rows):
        cot = rows[1]
        normed, _ = normalise(rows[0])
        first = normed * gain[...] + shift[...]
        second = normed * gain_two[...] + shift_two[...]
        first_out[...] = first.astype(BF16)
        second_out[...] = second.astype(BF16)
        cot_out[...] = cot.astype(BF16)
        put_turned(first_turned, first)
        put_turned(second_turned, second)
        put_turned(cot_turned, cot)

    @pl.when(pl.program_id(0) < 2)
    def _():
        step(near)

    @pl.when(pl.program_id(0) >= 2)
    def _():
        step(other)


TURNED = (16, 2, 64, 2 * TOK)


def norm_call(kernel, rows, n_rows, n_plain, n_turned, params, far=()):
    steps = TOK // rows
    plain = pl.BlockSpec((rows, D), lambda i: (i, 0))
    shift = steps if far else 0
    turned = pl.BlockSpec((16, 2, 64, rows), lambda i: (0, 0, 0, i + shift))
    if far:
        picks = (lambda i: (0, lax.min(i, 1), 0), lambda i: (0, lax.max(i - 2, 0), 0))
        specs = [pl.BlockSpec((2, rows, D), p) for p in picks]
    else:
        specs = [plain] * len(n_rows)
    operands = list(n_rows) + [p.reshape(1, D) for p in params]
    aliases = {len(operands) + i: n_plain + i for i in range(len(far))}
    return pl.pallas_call(
        kernel,
        grid=(steps,),
        in_specs=specs + [whole((1, D))] * len(params) + [pl.BlockSpec(memory_space=pl.ANY)] * len(far),
        out_specs=[plain] * n_plain + [turned] * n_turned,
        out_shape=[jax.ShapeDtypeStruct((TOK, D), BF16)] * n_plain
        + [jax.ShapeDtypeStruct(TURNED, BF16)] * n_turned,
        input_output_aliases=aliases,
        compiler_params=pltpu.CompilerParams(vmem_limit_bytes=VMEM),
        cost_estimate=COST,
    )(*operands, *far)


def phi(upward):
    return 0.5 * (1.0 + lax.erf(upward * math.sqrt(0.5)))


def gelu_slope(upward, below):
    return below + upward * (jnp.exp(-0.5 * upward * upward) * (1.0 / math.sqrt(2.0 * math.pi)))


def feed_kernel(second, cot_turned, weight, bias, act_out, slope_out, down_grad):
    upward = plain_dot(second[...], weight[...]) + bias[...]
    below = phi(upward)
    act = (upward * below).astype(BF16)
    act_out[...] = act
    slope_out[...] = gelu_slope(upward, below)
    down_grad[...] = plain_dot(cot_turned[...].reshape(D, TOK), act).reshape(16, 128, -1)


def feed(second, cot_turned, weight, bias):
    units, width = weight.shape[1], 512
    column = pl.BlockSpec((TOK, width), lambda j: (0, j))
    return pl.pallas_call(
        feed_kernel,
        grid=(units // width,),
        in_specs=[
            whole((TOK, D)),
            whole((16, 2, 64, TOK)),
            pl.BlockSpec((D, width), lambda j: (0, j)),
            pl.BlockSpec((1, width), lambda j: (0, j)),
        ],
        out_specs=[column, column, pl.BlockSpec((16, 128, width), lambda j: (0, 0, j))],
        out_shape=[
            jax.ShapeDtypeStruct((TOK, units), BF16),
            jax.ShapeDtypeStruct((TOK, units), F32),
            jax.ShapeDtypeStruct((16, 128, units), F32),
        ],
        compiler_params=pltpu.CompilerParams(vmem_limit_bytes=VMEM),
        cost_estimate=COST,
    )(second, cot_turned, weight, bias.reshape(1, -1))


def feed_back_kernel(cot, weight, slope, up_grad):
    up_grad[...] = (contract_cols(cot[...], weight[...]) * slope[...]).astype(BF16)


def feed_back(cot, weight, slope):
    units, width = weight.shape[0], 512
    column = pl.BlockSpec((TOK, width), lambda j: (0, j))
    return pl.pallas_call(
        feed_back_kernel,
        grid=(units // width,),
        in_specs=[whole((TOK, D)), pl.BlockSpec((width, D), lambda j: (j, 0)), column],
        out_specs=column,
        out_shape=jax.ShapeDtypeStruct((TOK, units), BF16),
        compiler_params=pltpu.CompilerParams(vmem_limit_bytes=VMEM),
        cost_estimate=COST,
    )(cot, weight, slope)


def feed_far_kernel(side, second, cot, up_weight, up_bias, down_weight, up_grad):
    upward = plain_dot(second[...], up_weight[...]) + up_bias[...]
    slope = gelu_slope(upward, phi(upward))
    up_grad[...] = (contract_cols(cot[...], down_weight[...]) * slope).astype(BF16)


def feed_far(side, second, cot, up_weight, up_bias, down_weight):
    width = 256
    units = up_weight.shape[1] // 2
    steps = units // width
    return pl.pallas_call(
        feed_far_kernel,
        grid_spec=pltpu.PrefetchScalarGridSpec(
            num_scalar_prefetch=1,
            grid=(steps,),
            in_specs=[
                whole((TOK, D)),
                whole((TOK, D)),
                pl.BlockSpec((D, width), lambda j, s: (0, s[0] * steps + j)),
                pl.BlockSpec((1, width), lambda j, s: (0, s[0] * steps + j)),
                pl.BlockSpec((width, D), lambda j, s: (s[0] * steps + j, 0)),
            ],
            out_specs=pl.BlockSpec((TOK, width), lambda j, s: (0, j)),
        ),
        out_shape=jax.ShapeDtypeStruct((TOK, units), BF16),
        compiler_params=pltpu.CompilerParams(vmem_limit_bytes=VMEM),
        cost_estimate=COST,
    )(side, second, cot, up_weight, up_bias.reshape(1, -1), down_weight)


def turn(values, tables, sign):
    first = values[:, :128]
    cosine, rising, falling = tables
    first = (
        first * cosine[...]
        + (pltpu.roll(first, 32, 1) * rising[...] + pltpu.roll(first, 96, 1) * falling[...]) * sign
    )
    return jnp.concatenate([first, values[:, 128:]], axis=1)


def attend_kernel(
    side, first, cot, weight, bias, dense, cosine, rising, falling, marks, marks_too, mixed_out, grad_out
):
    tables = (cosine, rising, falling)
    scale = 1.0 / math.sqrt(HD)
    packed = plain_dot(first[...], weight[...]) + bias[0]
    queries = turn(packed[:, :HD], tables, 1.0).astype(BF16)
    keys = turn(packed[:, HD : 2 * HD], tables, 1.0).astype(BF16)
    values = packed[:, 2 * HD :].astype(BF16)
    scores = contract_cols(queries, keys) * scale
    allowed = (marks[:, 0:1] == marks_too[0:1, :]) & (marks[:, 1:2] >= marks_too[1:2, :])
    scores = jnp.where(allowed, scores, NEGATIVE)
    top = jnp.max(scores, axis=-1, keepdims=True)
    weights = jnp.exp(scores - top)
    probs = weights / jnp.sum(weights, axis=-1, keepdims=True)
    probs_low = probs.astype(BF16)
    mixed_out[...] = plain_dot(probs_low, values).astype(BF16)
    grad_mixed = contract_cols(cot[...], dense[...]).astype(BF16)
    grad_probs = contract_cols(grad_mixed, values)
    along = jnp.sum(probs * grad_probs, axis=-1, keepdims=True)
    grad_scores = (probs * (grad_probs - along)).astype(BF16)
    grad_query = plain_dot(grad_scores, keys) * scale
    grad_key = plain_dot(grad_scores.T, queries) * scale
    grad_value = plain_dot(probs_low.T, grad_mixed)
    grad_out[:, :HD] = turn(grad_query, tables, -1.0).astype(BF16)
    grad_out[:, HD : 2 * HD] = turn(grad_key, tables, -1.0).astype(BF16)
    grad_out[:, 2 * HD :] = grad_value.astype(BF16)


def attend(side, heads, first, cot, weight, bias, dense, segments, positions, order):
    halves = jnp.arange(ROT // 2, dtype=F32)
    inverse = 10000.0 ** (-2.0 * halves / ROT)
    angles = positions.astype(F32)[:, None] * inverse
    cosine, sine = jnp.cos(angles), jnp.sin(angles)
    none, rest = jnp.zeros((TOK, 32), F32), jnp.zeros((TOK, 64), F32)
    tables = (
        jnp.concatenate([cosine, cosine, rest + 1.0], axis=1),
        jnp.concatenate([none, sine, rest], axis=1),
        jnp.concatenate([-sine, none, rest], axis=1),
    )
    marks = jnp.stack([segments, order], axis=1)
    at = (lambda h, s: h) if heads == 2 else (lambda h, s: s[0])
    return pl.pallas_call(
        attend_kernel,
        grid_spec=pltpu.PrefetchScalarGridSpec(
            num_scalar_prefetch=1,
            grid=(heads,),
            in_specs=[
                whole((TOK, D)),
                whole((TOK, D)),
                pl.BlockSpec((D, 3 * HD), lambda h, s: (0, at(h, s))),
                pl.BlockSpec((1, 1, 3 * HD), lambda h, s: (at(h, s), 0, 0)),
                pl.BlockSpec((HD, D), lambda h, s: (at(h, s), 0)),
            ]
            + [whole((TOK, 128))] * 3
            + [whole((TOK, 2)), whole((2, TOK))],
            out_specs=[
                pl.BlockSpec((TOK, HD), lambda h, s: (0, h)),
                pl.BlockSpec((TOK, 3 * HD), lambda h, s: (0, h)),
            ],
        ),
        out_shape=[
            jax.ShapeDtypeStruct((TOK, heads * HD), BF16),
            jax.ShapeDtypeStruct((TOK, heads * 3 * HD), BF16),
        ],
        compiler_params=pltpu.CompilerParams(vmem_limit_bytes=VMEM),
        cost_estimate=COST,
    )(
        side,
        first,
        cot,
        weight,
        bias.reshape(-1, 1, 3 * HD),
        dense,
        *tables,
        marks,
        marks.T,
    )


def joint_kernel(side, *refs):
    lefts, rights, target = refs[:3], refs[3:9], refs[9]
    step = pl.program_id(0)
    for k, (start, stop) in enumerate(((0, 4), (4, 5), (5, 8))):

        @pl.when((step >= start) & (step < stop))
        def _(k=k):
            right = jnp.concatenate([rights[2 * k][...], rights[2 * k + 1][...]], axis=0)
            total = plain_dot(lefts[k][...].reshape(D, 2 * TOK), right)
            target[...] = total.reshape(16, 128, -1)


def joint(side, lefts, rights):
    width = 256
    specs = [whole(TURNED)] * 3
    for start, n in ((0, 4), (4, 1), (5, 3)):

        def near(j, s, start=start, n=n):
            return (0, s[0] * n + jnp.clip(j - start, 0, n - 1))

        def far(j, s, start=start, n=n):
            return (0, jnp.clip(j - start, 0, n - 1))

        specs += [pl.BlockSpec((TOK, width), near), pl.BlockSpec((TOK, width), far)]
    return pl.pallas_call(
        joint_kernel,
        grid_spec=pltpu.PrefetchScalarGridSpec(
            num_scalar_prefetch=1,
            grid=(8,),
            in_specs=specs,
            out_specs=pl.BlockSpec((16, 128, width), lambda j, s: (0, 0, j)),
        ),
        out_shape=jax.ShapeDtypeStruct((16, 128, 8 * width), F32),
        compiler_params=pltpu.CompilerParams(vmem_limit_bytes=VMEM),
        cost_estimate=COST,
    )(side, *lefts, *rights)


def body(
    hidden_in,
    segment_ids,
    positions,
    ln1_gain,
    ln1_bias,
    qkv_weight,
    qkv_bias,
    dense_weight,
    dense_bias,
    ln2_gain,
    ln2_bias,
    fc1_weight,
    fc1_bias,
    fc2_weight,
    fc2_bias,
    cotangent,
):
    core = lax.axis_index("c")
    side = lax.axis_index("zl")
    at_side = side.astype(jnp.int32).reshape(1)
    half_rows = TOK // 2
    after = lax.optimization_barrier
    params = (ln1_gain, ln1_bias, ln2_gain, ln2_bias)

    def of_core(values, which):
        return lax.dynamic_slice_in_dim(values, which * half_rows, half_rows, 0)

    def both_cores(mine):
        theirs = send(mine, "c")
        filled = jnp.zeros((TOK,) + mine.shape[1:], mine.dtype)
        filled = lax.dynamic_update_slice_in_dim(filled, mine, core * half_rows, 0)
        return lax.dynamic_update_slice_in_dim(filled, theirs, (1 - core) * half_rows, 0)

    sent = jnp.stack([of_core(hidden_in, core).astype(F32), of_core(cotangent, core).astype(F32)])
    pair_rows = lax.all_gather(sent, "zl")

    second_in, cot_turned = norm_call(
        second_kernel, 256, (hidden_in, cotangent), 1, 1, (ln2_gain, ln2_bias)
    )
    act_low, slope, down_grad = feed(second_in, cot_turned, fc1_weight, fc1_bias)
    down_sum = after(lax.psum_scatter(down_grad, ("x", "y"), scatter_dimension=0, tiled=True))
    _, cotangent, hidden_in = after((down_grad, cotangent, hidden_in))

    first_in, first_turned, second_turned = norm_call(
        first_kernel, 256, (hidden_in,), 1, 2, (ln1_gain, ln1_bias, ln2_gain, ln2_bias)
    )
    mixed_low, grad_packed = attend(
        at_side,
        2,
        first_in,
        cotangent,
        qkv_weight,
        qkv_bias,
        dense_weight,
        segment_ids,
        positions,
        jnp.arange(TOK, dtype=jnp.int32),
    )
    grad_up = feed_back(cotangent, fc2_weight, slope)

    def branch_half(which):
        return plain_dot(of_core(mixed_low, which), dense_weight) + plain_dot(
            of_core(act_low, which), fc2_weight
        )

    hidden = hidden_in.astype(F32)
    normed, inv_std = normalise(hidden)
    branch = branch_half(core) + send(branch_half(1 - core), "c")
    first_part = contract_cols(grad_packed, qkv_weight)
    second_part = contract_cols(grad_up, fc1_weight)
    combined = first_part * ln1_gain + second_part * ln2_gain
    combined = of_core(combined, core) + send(of_core(combined, 1 - core), "c")
    norms = jnp.stack(
        [
            jnp.sum(first_part * normed, axis=0),
            jnp.sum(first_part, axis=0),
            jnp.sum(second_part * normed, axis=0),
            jnp.sum(second_part, axis=0),
        ]
    )

    branch, combined, norms, pair_rows = after((branch, combined, norms, pair_rows))
    branch = lax.psum(branch, "zh")
    combined = lax.psum(combined, "zh")
    _, marks = after((pair_rows, jnp.stack([segment_ids, positions])))
    marks_got = send(marks, "zl")
    far_rows = lax.dynamic_index_in_dim(pair_rows, 1 - side, 0, keepdims=False)
    first_far, second_far, cot_far, first_turned, second_turned, cot_turned = norm_call(
        far_kernel,
        128,
        (far_rows, send(far_rows, "c")),
        3,
        3,
        params,
        (first_turned, second_turned, cot_turned),
    )
    grad_up_far = feed_far(at_side, second_far, cot_far, fc1_weight, fc1_bias, fc2_weight)
    marks_far = jnp.concatenate(
        [lax.dynamic_slice_in_dim(marks_got, w * half_rows, half_rows, 1) for w in (core, 1 - core)],
        axis=1,
    )
    mixed_far, grad_packed_far = attend(
        at_side,
        1,
        first_far,
        cot_far,
        qkv_weight,
        qkv_bias,
        dense_weight,
        marks_far[0],
        marks_far[1],
        (jnp.arange(TOK, dtype=jnp.int32) + core.astype(jnp.int32) * half_rows) % TOK,
    )
    joint_grad = joint(
        at_side,
        (second_turned, cot_turned, first_turned),
        (grad_up, grad_up_far, mixed_low, mixed_far, grad_packed, grad_packed_far),
    )
    joint_grad, down_sum = after((joint_grad, down_sum))
    joint_sum = after(lax.psum_scatter(joint_grad, ("x", "y"), scatter_dimension=0, tiled=True))
    _, norms, grad_packed, grad_up, cotangent, down_sum = after(
        (joint_grad, norms, grad_packed, grad_up, cotangent, down_sum)
    )

    norms = norms.reshape(4, 32, 64).transpose(1, 0, 2).reshape(32, 256)
    norms = norms + send(norms, "c")
    norms = norms + send(norms, "zh")
    grad_out = cotangent.astype(F32)
    bias_sum = jnp.sum(grad_out, axis=0)
    qkv_bias_sum = jnp.sum(grad_packed.astype(F32), axis=0)
    up_bias_grad = jnp.sum(grad_up.astype(F32), axis=0)
    small = jnp.concatenate(
        [
            norms,
            bias_sum.reshape(32, 64),
            qkv_bias_sum.reshape(2, 32, 24).transpose(1, 0, 2).reshape(32, 48),
            up_bias_grad.reshape(16, 32, 4).transpose(1, 0, 2).reshape(32, 64),
            jnp.zeros((32, 80), F32),
        ],
        axis=1,
    )
    for axis in ("x", "y"):
        small = small + swap(small, axis, 1)
        small = small + swap(small, axis, 2)
    block = lax.axis_index("x") * 4 + lax.axis_index("y")
    own_small = lax.dynamic_slice_in_dim(small, side * 16 + block, 1, 0)
    far_small = lax.dynamic_slice_in_dim(small, (1 - side) * 16 + block, 1, 0)
    small = (own_small + send(far_small, "zl")).reshape(-1)

    small, branch, combined = after((small, branch, combined))
    norms = small[:256].reshape(4, 64)
    bias_total = small[256:320]
    output = both_cores(of_core(hidden, core) + branch + dense_bias + fc2_bias)
    normed_half = of_core(normed, core)
    input_half = of_core(grad_out, core) + of_core(inv_std, core) * (
        combined
        - jnp.mean(combined, axis=-1, keepdims=True)
        - normed_half * jnp.mean(combined * normed_half, axis=-1, keepdims=True)
    )
    input_grad = both_cores(input_half)

    def of_side(values, which):
        return lax.dynamic_slice_in_dim(values[0], which * 64, 64, 0)

    down_sum = of_side(down_sum, side) + send(of_side(down_sum, 1 - side), "zl")
    near = of_side(joint_sum, side)
    far = send(of_side(joint_sum, 1 - side), "zl")
    low = jnp.where(side == 0, near, far)
    high = jnp.where(side == 0, far, near)
    sums = []
    start = 0
    for width in (1024, 256, 768):
        stop = start + width
        sums.append(jnp.concatenate([low[:, start:stop], high[:, start:stop]], axis=1))
        start = stop
    up_sum, dense_sum, qkv_sum = sums
    return (
        output,
        input_grad,
        norms[0],
        norms[1],
        qkv_sum,
        small[320:368].reshape(2, 24),
        dense_sum.T,
        bias_total,
        norms[2],
        norms[3],
        up_sum,
        small[368:432].reshape(16, 4),
        down_sum.T,
        bias_total,
    )


def solution(mesh):
    fine = Mesh(mesh.devices.reshape(tuple(SIZES.values())), tuple(SIZES))
    return jax.shard_map(
        body,
        mesh=fine,
        in_specs=(
            P(DP, None),
            P(DP),
            P(DP),
            P(),
            P(),
            P(None, TENSOR),
            P(TENSOR, None),
            P(TENSOR, None),
            P(),
            P(),
            P(),
            P(None, TENSOR),
            P(TENSOR, None),
            P(TENSOR, None),
            P(),
            P(DP, None),
        ),
        out_specs=(
            P(DP, None),
            P(DP, None),
            P(DP),
            P(DP),
            P(DP, TENSOR),
            P(TENSOR, DP),
            P(TENSOR, DP),
            P(DP),
            P(DP),
            P(DP),
            P(DP, TENSOR),
            P(TENSOR, DP),
            P(TENSOR, DP),
            P(DP),
        ),
        check_vma=False,
    )
```

profile of v0, /device:TPU:0, one launch (start us, length us, event | category | flops | bytes accessed | tf_op | source)
XLA Modules:
  0.0 321.1 jit_solution(17566848676375226361)
XLA Ops:
  9.7 2.3 maximum_convert_fusion
  12.1 4.7 %shard_map.263 = (bf16[512,2048]{1,0:T(8,128)(2,1)}, bf16[16,2,64,1024]{3,2,1,0:T(8,128)(2,1)}) custom-call(bf16[512,2048]{1,0:T(8,128)(2,1)} %hidden.2, bf16[512,2048]{1,0:T(8,128)(2,1)} %cot.3, f32[1,2048]{1,0:T(1,128)} %bitcast.65, f32[1,2048]{1,0:T(1,128)} %bitcast.68), custom_call_target="tpu_custom_call" | custom-call | flops 1000000 | bytes 1000000 | tf_op jit(solution)/shard_map/pallas_call | solution.py:118
  16.9 17.0 %shard_map.264 = (bf16[512,2048]{1,0:T(8,128)(2,1)}, f32[512,2048]{1,0:T(8,128)}, f32[16,128,2048]{2,1,0:T(8,128)}) custom-call(bf16[512,2048]{1,0:T(8,128)(2,1)} %get-tuple-element.49.second, bf16[16,2,64,1024]{3,2,1,0:T(8,128)(2,1)} %get-tuple-element.50.cot_turned.refs_2_, bf16[2048,2048]{1,0:T(8,128)(2,1)} %up_weight.1, f32[1,2048]{1,0:T(1,128)} %bitcast.75), custom_call_target="tpu_custom_call" | custom-call | flops 1000000 | bytes 1000000 | tf_op jit(solution)/shard_map/pallas_call | solution.py:151
  36.7 5.3 %shard_map.265 = (bf16[512,2048]{1,0:T(8,128)(2,1)}, bf16[16,2,64,1024]{3,2,1,0:T(8,128)(2,1)}, bf16[16,2,64,1024]{3,2,1,0:T(8,128)(2,1)}) custom-call(bf16[512,2048]{1,0:T(8,128)(2,1)} %hidden.2, f32[1,2048]{1,0:T(1,128)} %bitcast.71, f32[1,2048]{1,0:T(1,128)} %bitcast.73, f32[1,2048]{1,0:T(1,128)} %bitcast.66, f32[1,2048]{1,0:T(1,128)} %bitcast.69), custom_call_target="tpu_custom_call" | custom-call | flops 1000000 | bytes 1000000 | tf_op jit(solution)/shard_map/pallas_call | solution.py:118
  44.2 15.1 %shard_map.266 = (bf16[512,512]{1,0:T(8,128)(2,1)}, bf16[512,1536]{1,0:T(8,128)(2,1)}) custom-call(s32[1]{0:T(128)} %bitcast.3.side, bf16[512,2048]{1,0:T(8,128)(2,1)} %get-tuple-element.53.first, bf16[512,2048]{1,0:T(8,128)(2,1)} %cot.3, bf16[2048,1536]{1,0:T(8,128)(2,1)} %weight.7, f32[2,1,768]{2,1,0:T(1,128)} %reshape.203.bias, bf16[512,2048]{1,0:T(8,128)(2,1)} %dense.3, ...), custom_call_target="tpu_custom_call" | custom-call | flops 1000000 | bytes 1000000 | tf_op jit(solution)/shard_map/pallas_call | solution.py:271
  59.3 6.0 %fusion.1 = f32[256,2048]{1,0:T(8,128)S(1)} fusion(bf16[2048,2048]{1,0:T(8,128)(2,1)} %down_weight.1, bf16[512,2048]{1,0:T(8,128)(2,1)S(1)} %copy-done.28, s32[]{:T(128)S(6)} %select_n.67), kind=kOutput, calls=%fused_computation.20 | convolution fusion | flops 2147483648 | bytes 11534340 | tf_op jit(solution)/shard_map/dot_general | solution.py:34
  67.6 10.5 %shard_map.267.refs_3_ = bf16[512,2048]{1,0:T(8,128)(2,1)} custom-call(bf16[512,2048]{1,0:T(8,128)(2,1)} %cot.3, bf16[2048,2048]{1,0:T(8,128)(2,1)} %down_weight.1, f32[512,2048]{1,0:T(8,128)} %get-tuple-element.58.slope), custom_call_target="tpu_custom_call" | custom-call | flops 1000000 | bytes 1000000 | tf_op jit(solution)/shard_map/pallas_call | solution.py:178
  79.7 7.6 %fusion.27 = f32[512,2048]{1,0:T(8,128)S(1)} fusion(bf16[512,2048]{1,0:T(8,128)(2,1)S(1)} %copy-done.4, bf16[2048,2048]{1,0:T(8,128)(2,1)} %up_weight.1), kind=kOutput, calls=%fused_computation.88 | convolution fusion | flops 4294967296 | bytes 14680064 | tf_op jit(solution)/shard_map/dot_general | solution.py:38
  87.3 5.6 %multiply_reduce_fusion.1 = (f32[2048]{0:T(1024)S(1)}, f32[2048]{0:T(1024)S(1)}, f32[2048]{0:T(1024)S(1)}, f32[2048]{0:T(1024)S(1)}, f32[512,2048]{1,0:T(8,128)S(1)}, /*index=5*/f32[512,2048]{1,0:T(8,128)}) fusion(f32[512]{0:T(512)S(1)} %add_rsqrt_fusion, f32[512]{0:T(512)S(1)} %broadcast_multiply_fusion, bf16[512,2048]{1,0:T(8,128)(2,1)S(1)} %copy-done, ...), kind=kOutput, calls=%fused_computation.3 | convolution fusion | flops 3233800192 | bytes 22597632 | tf_op jit(solution)/shard_map/dot_general | solution.py:38
  96.6 6.8 %fusion.3 = f32[256,2048]{1,0:T(8,128)S(1)} fusion(bf16[2048,2048]{1,0:T(8,128)(2,1)} %down_weight.1, bf16[512,2048]{1,0:T(8,128)(2,1)} %get-tuple-element.56, s32[]{:T(128)S(6)} %select_n.66), kind=kOutput, calls=%fused_computation.22 | convolution fusion | flops 2147483648 | bytes 11534340 | tf_op jit(solution)/shard_map/dot_general | solution.py:34
  103.5 4.0 %fusion = f32[256,2048]{1,0:T(8,128)} fusion(f32[256,2048]{1,0:T(8,128)} %collective-permute-done, f32[256,2048]{1,0:T(8,128)S(1)} %fusion.3, bf16[512,2048]{1,0:T(8,128)(2,1)S(1)} %copy-done.3, bf16[512,512]{1,0:T(8,128)(2,1)S(1)} %copy-done.17, s32[]{:T(128)S(6)} %select_n.66), kind=kOutput, calls=%fused_computation.11 | convolution fusion | flops 537919488 | bytes 8650756 | tf_op jit(solution)/shard_map/dot_general | solution.py:34
  107.5 3.3 %dynamic-slice_add_fusion = f32[256,2048]{1,0:T(8,128)} fusion(f32[256,2048]{1,0:T(8,128)} %collective-permute-done.1, f32[512,2048]{1,0:T(8,128)S(1)} %copy-done.11, s32[]{:T(128)S(6)} %select_n.66), kind=kLoop, calls=%fused_computation.16 | loop fusion | flops 524288 | bytes 6291460 | tf_op jit(solution)/shard_map/add | solution.py:419
  110.8 10.5 %all-gather.3.cloned.1.call-done = f32[4,256,2048]{2,1,0:T(8,128)} async-done(((f32[2,256,2048]{2,1,0:T(8,128)}), f32[4,256,2048]{2,1,0:T(8,128)}) %all-gather.3.cloned.1.call-update) | async-done | bytes 8388624 | tf_op jit(solution)/shard_map/all_gather | solution.py:382
  121.3 4.9 %dynamic-slice_bitcast_fusion.near = f32[2,256,2048]{2,1,0:T(8,128)} fusion(f32[2,2,256,2048]{3,2,1,0:T(8,128)} %bitcast.59, s32[]{:T(128)S(6)} %select_n.68), kind=kLoop, calls=%fused_computation.1 | loop fusion | bytes 8388612 | tf_op jit(solution)/shard_map/jit(dynamic_index_in_dim)/squeeze | solution.py:434
  126.6 3.5 %collective-permute-done.3 = s32[2,512]{1,0:T(2,128)S(1)} collective-permute-done((s32[2,512]{1,0:T(2,128)S(1)}, s32[2,512]{1,0:T(2,128)S(1)}, u32[]{:S(2)}, u32[]{:S(2)}) %collective-permute-start.3) | collective-permute-done | bytes 4128 | tf_op jit(solution)/shard_map/ppermute | solution.py:26
  134.5 10.9 %shard_map.268 = (bf16[512,2048]{1,0:T(8,128)(2,1)}, bf16[512,2048]{1,0:T(8,128)(2,1)}, bf16[512,2048]{1,0:T(8,128)(2,1)}, bf16[16,2,64,1024]{3,2,1,0:T(8,128)(2...) custom-call(f32[2,256,2048]{2,1,0:T(8,128)} %dynamic-slice_bitcast_f, ...), custom_call_target="tpu_custom_call", output_to_operand_aliasing={{3}: (6, {}), {4}: (7, {}), {5}: (8, {})} | custom-call | flops 1000000 | bytes 1000000 | tf_op jit(solution)/shard_map/pallas_call | solution.py:118
  145.3 10.1 %shard_map.269.refs_4_ = bf16[512,1024]{1,0:T(8,128)(2,1)} custom-call(s32[1]{0:T(128)} %bitcast.3.side, bf16[512,2048]{1,0:T(8,128)(2,1)} %get-tuple-element.65.second, bf16[512,2048]{1,0:T(8,128)(2,1)} %get-tuple-element.66.cot, bf16[2048,2048]{1,0:T(8,128)(2,1)} %up_weight.1, f32[1,2048]{1,0:T(1,128)} %bitcast.76, bf16[2048,2048]{1,0:T(8,128)(2,1)} %down_weight.1), custom_call_target="tpu_custom_call" | custom-call | flops 1000000 | bytes 1000000 | tf_op jit(solution)/shard_map/pallas_call | solution.py:199
  155.5 9.6 %shard_map.270 = (bf16[512,256]{1,0:T(8,128)(2,1)}, bf16[512,768]{1,0:T(8,128)(2,1)}) custom-call(s32[1]{0:T(128)} %bitcast.3.side, bf16[512,2048]{1,0:T(8,128)(2,1)} %get-tuple-element.67.first, bf16[512,2048]{1,0:T(8,128)(2,1)} %get-tuple-element.66.cot, bf16[2048,1536]{1,0:T(8,128)(2,1)} %weight.7, f32[2,1,768]{2,1,0:T(1,128)} %reshape.203.bias, ...), custom_call_target="tpu_custom_call" | custom-call | flops 1000000 | bytes 1000000 | tf_op jit(solution)/shard_map/pallas_call | solution.py:271
  165.0 17.6 %shard_map.271 = f32[16,128,2048]{2,1,0:T(8,128)} custom-call(s32[1]{0:T(128)} %bitcast.3.side, bf16[16,2,64,1024]{3,2,1,0:T(8,128)(2,1)} %get-tuple-element.62.refs_0_, bf16[16,2,64,1024]{3,2,1,0:T(8,128)(2,1)} %get-tuple-element.63.refs_1_, bf16[16,2,64,1024]{3,2,1,0:T(8,128)(2,1)} %get-tuple-element.64.refs_2_, bf16[512,2048]{1,0:T(8,128)(2,1)} %shard_map.267.refs_3_, ...), custom_call_target="tpu_custom_call" | custom-call | flops 1000000 | bytes 1000000 | tf_op jit(solution)/shard_map/pallas_call | solution.py:333
  192.9 4.0 %collective-permute-done.6 = f32[32,512]{1,0:T(8,128)S(1)} collective-permute-done((f32[32,512]{1,0:T(8,128)S(1)}, f32[32,512]{1,0:T(8,128)S(1)}, u32[]{:S(2)}, u32[]{:S(2)}) %collective-permute-start.6) | collective-permute-done | bytes 65568 | tf_op jit(solution)/shard_map/ppermute | solution.py:30
  196.9 3.0 collective-permute-start.7
  199.9 4.2 %collective-permute-done.7 = f32[32,512]{1,0:T(8,128)S(1)} collective-permute-done((f32[32,512]{1,0:T(8,128)S(1)}, f32[32,512]{1,0:T(8,128)S(1)}, u32[]{:S(2)}, u32[]{:S(2)}) %collective-permute-start.7) | collective-permute-done | bytes 65568 | tf_op jit(solution)/shard_map/ppermute | solution.py:30
  205.5 4.1 %collective-permute-done.8 = f32[32,512]{1,0:T(8,128)S(1)} collective-permute-done((f32[32,512]{1,0:T(8,128)S(1)}, f32[32,512]{1,0:T(8,128)S(1)}, u32[]{:S(2)}, u32[]{:S(2)}) %collective-permute-start.8) | collective-permute-done | bytes 65568 | tf_op jit(solution)/shard_map/ppermute | solution.py:30
  209.6 3.3 %collective-permute-start.9 = (f32[32,512]{1,0:T(8,128)S(1)}, f32[32,512]{1,0:T(8,128)S(1)}, u32[]{:S(2)}, u32[]{:S(2)}) collective-permute-start(f32[32,512]{1,0:T(8,128)S(1)} %add.178), channel_id=1, source_target_pairs={{0,8},{4,12},{8,0},{12,4},{1,9},{5,13},{9,1},{13,5},{2,10},{6,14},... | collective-permute-start | bytes 196616 | tf_op jit(solution)/shard_map/ppermute | solution.py:30
  212.9 3.9 %collective-permute-done.9 = f32[32,512]{1,0:T(8,128)S(1)} collective-permute-done((f32[32,512]{1,0:T(8,128)S(1)}, f32[32,512]{1,0:T(8,128)S(1)}, u32[]{:S(2)}, u32[]{:S(2)}) %collective-permute-start.9) | collective-permute-done | bytes 65568 | tf_op jit(solution)/shard_map/ppermute | solution.py:30
  217.1 2.5 convert_element_type.27
  219.6 4.1 %convert_element_type.31 = f32[512,2048]{1,0:T(8,128)} convert(bf16[512,2048]{1,0:T(8,128)(2,1)} %cot.3) | non-fusion elementwise | flops 1048576 | bytes 6291456 | tf_op jit(solution)/shard_map/convert_element_type | solution.py:475
  223.8 20.1 %all-reduce.5.cloned.1.call-done = (f32[256,2048]{1,0:T(8,128)}, f32[256,2048]{1,0:T(8,128)}) async-done(((f32[256,2048]{1,0:T(8,128)}, f32[256,2048]{1,0:T(8,128)}), (f32[256,2048]{1,0:T(8,128)}, f32[256,2048]{1,0:T(8,128)})) %all-reduce.5.cloned.1.call-update) | async-done | bytes 4194320 | tf_op jit(solution)/shard_map/psum | solution.py:430
  246.0 3.7 %constant_dynamic-update-slice_fusion.3 = (f32[512,2048]{1,0:T(8,128)S(1)}, f32[256,2048]{1,0:T(8,128)}) fusion(f32[512,2048]{1,0:T(8,128)S(1)} %broadcast.128.clone, s32[]{:T(128)S(6)} %select_n.66, f32[2048]{0:T(1024)S(1)} %copy-done.24, f32[2048]{0:T(1024)S(1)} %copy-done.25, f32[256,2048]{1,0:T(8,128)} %get-tuple-element.80, f32[512,2048]{1,0:T(8,128)S(1)} %copy-done.6), kind=kLoop, calls=%fused_computation.58 | loop fusion | flops 1572864 | bytes 8404996 | tf_op jit(solution)/shard_map/dynamic_update_slice | solution.py:378
  261.8 11.7 %collective-permute-done.14 = f32[64,2048]{1,0:T(8,128)} collective-permute-done((f32[64,2048]{1,0:T(8,128)}, f32[64,2048]{1,0:T(8,128)}, u32[]{:S(2)}, u32[]{:S(2)}) %collective-permute-start.14) | collective-permute-done | bytes 524320 | tf_op jit(solution)/shard_map/ppermute | solution.py:26
  275.4 20.7 %reduce-scatter.9.cloned.1.call-done = f32[1,128,2048]{2,1,0:T(8,128)} async-done(((f32[16,128,2048]{2,1,0:T(8,128)}), f32[1,128,2048]{2,1,0:T(8,128)}) %reduce-scatter.9.cloned.1.call-update) | async-done | bytes 1048592
  303.6 6.8 %collective-permute-done.13 = f32[64,2048]{1,0:T(8,128)S(1)} collective-permute-done((f32[64,2048]{1,0:T(8,128)S(1)}, f32[64,2048]{1,0:T(8,128)S(1)}, u32[]{:S(2)}, u32[]{:S(2)}) %collective-permute-start.13) | collective-permute-done | bytes 524320 | tf_op jit(solution)/shard_map/ppermute | solution.py:26
  (174 shorter events, 57.5 us)
Async XLA Ops:
  8.0 113.3 %all-gather.3.cloned.1.call-start = ((), (), s32[]{:S(2)}) async-start(), calls=%async_computation.2 | async-start | bytes 12582912 | tf_op jit(solution)/shard_map/all_gather | solution.py:382
  12.1 170.6 %reduce-scatter.7.cloned.1.call-start = ((), (), s32[]{:S(2)}) async-start(), calls=%async_computation.3 | async-start | bytes 17825792
  33.9 209.9 %all-reduce.5.cloned.1.call-start = ((), (), s32[]{:S(2)}) async-start(), calls=%async_computation.5 | async-start | bytes 8388608 | tf_op jit(solution)/shard_map/psum | solution.py:430
  44.2 15.1 %copy-start.28 = (bf16[512,2048]{1,0:T(8,128)(2,1)S(1)}, bf16[512,2048]{1,0:T(8,128)(2,1)}, u32[]{:S(2)}) copy-start(bf16[512,2048]{1,0:T(8,128)(2,1)} %get-tuple-element.56) | copy-start | bytes 6291460
  67.4 36.0 %collective-permute-start = (f32[256,2048]{1,0:T(8,128)}, f32[256,2048]{1,0:T(8,128)}, u32[]{:S(2)}, u32[]{:S(2)}) collective-permute-start(f32[256,2048]{1,0:T(8,128)} %convolution_add_fusion), channel_id=1, source_target_pairs={{0,1},{1,0},{2,3},{3,2},{4,5},{5,4},{6,7},{7,6},{8,9},{9,8},{10,11... | collective-permute-start | bytes 6291464 | tf_op jit(solution)/shard_map/ppermute | solution.py:26
  67.6 10.5 %copy-start = (bf16[512,2048]{1,0:T(8,128)(2,1)S(1)}, bf16[512,2048]{1,0:T(8,128)(2,1)}, u32[]{:S(2)}) copy-start(bf16[512,2048]{1,0:T(8,128)(2,1)} %hidden.2) | copy-start | bytes 6291460
  78.4 8.9 %slice-start = ((s8[6291456]{0:T(1024)(128)(4,1)}), s8[4194304]{0:T(1024)(128)(4,1)S(1)}, s32[]{:S(2)}) async-start(s8[6291456]{0:T(1024)(128)(4,1)} %bitcast.57), calls=%async_computation.6 | async-start | bytes 8388608
  79.7 7.6 %slice-start.1 = ((s8[6291456]{0:T(1024)(128)(4,1)}), s8[2097152]{0:T(1024)(128)(4,1)S(1)}, s32[]{:S(2)}) async-start(s8[6291456]{0:T(1024)(128)(4,1)} %bitcast.57), calls=%async_computation.7 | async-start | bytes 4194304
  79.7 7.6 %copy-start.8 = (bf16[512,1536]{1,0:T(8,128)(2,1)S(1)}, bf16[512,1536]{1,0:T(8,128)(2,1)}, u32[]{:S(2)}) copy-start(bf16[512,1536]{1,0:T(8,128)(2,1)} %get-tuple-element.76.refs_7_) | copy-start | bytes 4718596
  79.7 7.6 %copy-start.20 = (f32[2048]{0:T(1024)S(1)}, f32[2048]{0:T(1024)}, u32[]{:S(2)}) copy-start(f32[2048]{0:T(1024)} %param.25) | copy-start | bytes 24580
  79.7 7.7 %copy-start.21 = (f32[2048]{0:T(1024)S(1)}, f32[2048]{0:T(1024)}, u32[]{:S(2)}) copy-start(f32[2048]{0:T(1024)} %param.19) | copy-start | bytes 24580
  95.6 11.8 %collective-permute-start.1 = (f32[256,2048]{1,0:T(8,128)}, f32[256,2048]{1,0:T(8,128)}, u32[]{:S(2)}, u32[]{:S(2)}) collective-permute-start(f32[256,2048]{1,0:T(8,128)} %constant_dynamic-slice_fusion.4), channel_id=1, source_target_pairs={{0,1},{1,0},{2,3},{3,2},{4,5},{5,4},{6,7},{7,6},{8,9},{9,8},{10,11... | collective-permute-start | bytes 6291464 | tf_op jit(solution)/shard_map/ppermute | solution.py:26
  96.6 6.8 %copy-start.3 = (bf16[512,2048]{1,0:T(8,128)(2,1)S(1)}, bf16[512,2048]{1,0:T(8,128)(2,1)}, u32[]{:S(2)}) copy-start(bf16[512,2048]{1,0:T(8,128)(2,1)} %dense.3) | copy-start | bytes 6291460
  126.2 8.3 %collective-permute-start.2 = (f32[2,256,2048]{2,1,0:T(8,128)}, f32[2,256,2048]{2,1,0:T(8,128)}, u32[]{:S(2)}, u32[]{:S(2)}) collective-permute-start(f32[2,256,2048]{2,1,0:T(8,128)} %dynamic-slice_bitcast_fusion.near), channel_id=1, source_target_pairs={{0,1},{1,0},{2,3},{3,2},{4,5},{5,4},{6,7},{7,6},{8,9},{9,8},{10,11... | collective-permute-start | bytes 12582920 | tf_op jit(solution)/shard_map/ppermute | solution.py:26
  126.2 169.8 %reduce-scatter.9.cloned.1.call-start = ((), (), s32[]{:S(2)}) async-start(), calls=%async_computation.4 | async-start | bytes 17825792
  126.2 3.9 %collective-permute-start.3 = (s32[2,512]{1,0:T(2,128)S(1)}, s32[2,512]{1,0:T(2,128)S(1)}, u32[]{:S(2)}, u32[]{:S(2)}) collective-permute-start(s32[2,512]{1,0:T(2,128)S(1)} %pad_add_fusion.1), channel_id=1, source_target_pairs={{0,64},{64,0},{1,65},{65,1},{2,66},{66,2},{3,67},{67,3},{4,68},{68... | collective-permute-start | bytes 12296 | tf_op jit(solution)/shard_map/ppermute | solution.py:26
  182.9 2.9 collective-permute-start.4
  185.8 5.5 %collective-permute-start.5 = (f32[32,256]{1,0:T(8,128)S(1)}, f32[32,256]{1,0:T(8,128)S(1)}, u32[]{:S(2)}, u32[]{:S(2)}) collective-permute-start(f32[32,256]{1,0:T(8,128)S(1)} %add.174), channel_id=1, source_target_pairs={{0,2},{2,0},{1,3},{3,1},{4,6},{6,4},{5,7},{7,5},{8,10},{10,8},{9,1... | collective-permute-start | bytes 98312 | tf_op jit(solution)/shard_map/ppermute | solution.py:26
  191.4 5.4 %collective-permute-start.6 = (f32[32,512]{1,0:T(8,128)S(1)}, f32[32,512]{1,0:T(8,128)S(1)}, u32[]{:S(2)}, u32[]{:S(2)}) collective-permute-start(f32[32,512]{1,0:T(8,128)S(1)} %concatenate.40), channel_id=1, source_target_pairs={{0,16},{16,0},{32,48},{48,32},{1,17},{17,1},{33,49},{49,33},{2,18}... | collective-permute-start | bytes 196616 | tf_op jit(solution)/shard_map/ppermute | solution.py:30
  196.9 7.2 %collective-permute-start.7 = (f32[32,512]{1,0:T(8,128)S(1)}, f32[32,512]{1,0:T(8,128)S(1)}, u32[]{:S(2)}, u32[]{:S(2)}) collective-permute-start(f32[32,512]{1,0:T(8,128)S(1)} %add.176), channel_id=1, source_target_pairs={{0,32},{16,48},{32,0},{48,16},{1,33},{17,49},{33,1},{49,17},{2,34}... | collective-permute-start | bytes 196616 | tf_op jit(solution)/shard_map/ppermute | solution.py:30
  204.1 5.5 %collective-permute-start.8 = (f32[32,512]{1,0:T(8,128)S(1)}, f32[32,512]{1,0:T(8,128)S(1)}, u32[]{:S(2)}, u32[]{:S(2)}) collective-permute-start(f32[32,512]{1,0:T(8,128)S(1)} %add.177), channel_id=1, source_target_pairs={{0,4},{4,0},{8,12},{12,8},{1,5},{5,1},{9,13},{13,9},{2,6},{6,2},{1... | collective-permute-start | bytes 196616 | tf_op jit(solution)/shard_map/ppermute | solution.py:30
  209.6 7.2 %collective-permute-start.9 = (f32[32,512]{1,0:T(8,128)S(1)}, f32[32,512]{1,0:T(8,128)S(1)}, u32[]{:S(2)}, u32[]{:S(2)}) collective-permute-start(f32[32,512]{1,0:T(8,128)S(1)} %add.178), channel_id=1, source_target_pairs={{0,8},{4,12},{8,0},{12,4},{1,9},{5,13},{9,1},{13,5},{2,10},{6,14},... | collective-permute-start | bytes 196616 | tf_op jit(solution)/shard_map/ppermute | solution.py:30
  216.9 6.9 %collective-permute-start.10 = (f32[1,512]{1,0:T(1,128)S(1)}, f32[1,512]{1,0:T(1,128)S(1)}, u32[]{:S(2)}, u32[]{:S(2)}) collective-permute-start(f32[1,512]{1,0:T(1,128)S(1)} %constant_dynamic-slice_fusion), channel_id=1, source_target_pairs={{0,64},{64,0},{1,65},{65,1},{2,66},{66,2},{3,67},{67,3},{4,68},{68... | collective-permute-start | bytes 6152 | tf_op jit(solution)/shard_map/ppermute | solution.py:26
  219.6 24.7 %copy-start.24 = (f32[2048]{0:T(1024)S(1)}, f32[2048]{0:T(1024)}, u32[]{:S(2)}) copy-start(f32[2048]{0:T(1024)} %param.30) | copy-start | bytes 24580
  219.6 24.7 %copy-start.25 = (f32[2048]{0:T(1024)S(1)}, f32[2048]{0:T(1024)}, u32[]{:S(2)}) copy-start(f32[2048]{0:T(1024)} %param.24) | copy-start | bytes 24580
  249.7 49.1 %collective-permute-start.11 = (f32[256,2048]{1,0:T(8,128)}, f32[256,2048]{1,0:T(8,128)S(1)}, u32[]{:S(2)}, u32[]{:S(2)}) collective-permute-start(f32[256,2048]{1,0:T(8,128)} %get-tuple-element.153), channel_id=1, source_target_pairs={{0,1},{1,0},{2,3},{3,2},{4,5},{5,4},{6,7},{7,6},{8,9},{9,8},{10,11... | collective-permute-start | bytes 6291464 | tf_op jit(solution)/shard_map/ppermute | solution.py:26
  258.0 42.3 %collective-permute-start.12 = (f32[256,2048]{1,0:T(8,128)}, f32[256,2048]{1,0:T(8,128)}, u32[]{:S(2)}, u32[]{:S(2)}) collective-permute-start(f32[256,2048]{1,0:T(8,128)} %get-tuple-element.151), channel_id=1, source_target_pairs={{0,1},{1,0},{2,3},{3,2},{4,5},{5,4},{6,7},{7,6},{8,9},{9,8},{10,11... | collective-permute-start | bytes 6291464 | tf_op jit(solution)/shard_map/ppermute | solution.py:26
  258.9 14.5 %collective-permute-start.14 = (f32[64,2048]{1,0:T(8,128)}, f32[64,2048]{1,0:T(8,128)}, u32[]{:S(2)}, u32[]{:S(2)}) collective-permute-start(f32[64,2048]{1,0:T(8,128)} %dynamic-slice_bitcast_fusion.3), channel_id=1, source_target_pairs={{0,64},{64,0},{1,65},{65,1},{2,66},{66,2},{3,67},{67,3},{4,68},{68... | collective-permute-start | bytes 1572872 | tf_op jit(solution)/shard_map/ppermute | solution.py:26
  261.0 51.9 %copy-start.27 = (f32[64]{0:T(128)}, f32[64]{0:T(128)S(1)}, u32[]{:S(2)}) copy-start(f32[64]{0:T(128)S(1)} %get-tuple-element.212) | copy-start | bytes 772
  297.1 13.3 %collective-permute-start.13 = (f32[64,2048]{1,0:T(8,128)S(1)}, f32[64,2048]{1,0:T(8,128)S(1)}, u32[]{:S(2)}, u32[]{:S(2)}) collective-permute-start(f32[64,2048]{1,0:T(8,128)S(1)} %dynamic-slice_bitcast_fusion.4), channel_id=1, source_target_pairs={{0,64},{64,0},{1,65},{65,1},{2,66},{66,2},{3,67},{67,3},{4,68},{68... | collective-permute-start | bytes 1572872 | tf_op jit(solution)/shard_map/ppermute | solution.py:26
  301.7 8.7 %copy-start.19 = (f32[1,128,2048]{2,1,0:T(8,128)S(1)}, f32[1,128,2048]{2,1,0:T(8,128)}, u32[]{:S(2)}) copy-start(f32[1,128,2048]{2,1,0:T(8,128)} %reduce-scatter.9.cloned.1.call-done) | copy-start | bytes 3145732
  303.6 9.9 %copy-start.14 = (f32[512,2048]{1,0:T(8,128)}, f32[512,2048]{1,0:T(8,128)S(1)}, u32[]{:S(2)}) copy-start(f32[512,2048]{1,0:T(8,128)S(1)} %constant_dynamic-update-slice_fusion) | copy-start | bytes 12582916
  (18 other events, 54.8 us)
Sparse Core Ops, SparseCore 0:
  12.2 109.0 all-gather.2
  126.3 117.4 all-reduce.4
Sparse Core Ops, SparseCore 1:
  34.0 112.6 reduce-scatter.6
  182.8 113.2 reduce-scatter.8
where the time goes:
time: 325 us; the launch traced here: 321 us
  Pallas kernels  101 us (31%)
  waiting for transfers between devices  91.8 us (28%)
  other arithmetic  32.8 us (10%)
  matrix products  32.1 us (10%)
  local copies, waits for them, and re-layouts  30.7 us (9%)
  starting transfers between devices  16.7 us (5%)
  between operations  16.3 us (5%)
    pallas_call x2, Pallas kernels, attend(): pl.pallas_call(attend_kernel, grid_spec=pltpu.PrefetchScalarGridSpec(num_...  24.6 us
    ppermute x11, waiting for transfers between devices, send(): return lax.ppermute(value, axis, [(i, (i + step) % n) for i in range(n)])  24.3 us
    pallas_call x3, Pallas kernels, norm_call(): pl.pallas_call(kernel, grid=(steps,), in_specs=specs + [whole((1, D))] *...  20.9 us
    unnamed x5, waiting for transfers between devices  20.7 us
    psum x1, waiting for transfers between devices, body(): branch = lax.psum(branch, 'zh')  20.1 us
    dot_general x4, matrix products, plain_dot(): return jnp.dot(left, right, preferred_element_type=F32)  18.9 us
    pallas_call x1, Pallas kernels, joint(): pl.pallas_call(joint_kernel, grid_spec=pltpu.PrefetchScalarGridSpec(num_s...  17.6 us
    pallas_call x1, Pallas kernels, feed(): pl.pallas_call(feed_kernel, grid=(units // width,), in_specs=[whole((TOK,...  17 us
  transfers between devices with their start and end apart: 19, of which 11 were waited for; matrix products, arithmetic and copies ran while one was open for 24% of the time, Pallas kernels for 31%

commit v1 on v0

v1 whole, which is shorter than its diff:
```python
from functools import partial
import math

import jax
import jax.numpy as jnp
import numpy as np
from jax import lax
from jax.experimental import pallas as pl
from jax.experimental.pallas import tpu as pltpu
from jax.sharding import Mesh, PartitionSpec as P

HD = 256
ROT = 64
TOK = 512
D = 2048
EPSILON = 1e-05
NEGATIVE = -1000000000.0
SIZES = {"zl": 2, "x": 4, "y": 4, "zh": 2, "c": 2}
DP = ("zl", "x", "y")
TENSOR = ("zh", "c")
F32 = jnp.float32
BF16 = jnp.bfloat16


def send(value, axis, step=1):
    n = SIZES[axis]
    return lax.ppermute(value, axis, [(i, (i + step) % n) for i in range(n)])


def swap(value, axis, bit):
    return lax.ppermute(value, axis, [(i, i ^ bit) for i in range(SIZES[axis])])


def plain_dot(left, right):
    return jnp.dot(left, right, preferred_element_type=F32)


def contract_cols(left, right):
    return lax.dot_general(left, right, (((1,), (1,)), ((), ())), preferred_element_type=F32)


VMEM = 56 * 1024 * 1024
COST = pl.CostEstimate(flops=1000000, bytes_accessed=1000000, transcendentals=0)


def whole(shape):
    return pl.BlockSpec(shape, lambda *_: (0,) * len(shape), pipeline_mode=pl.Buffered(1))


def put_turned(target, rows):
    for z in range(2):
        for pair in range(8):
            start = z * 1024 + pair * 128
            block = rows[:, start : start + 128].T.astype(BF16)
            target[2 * pair, z] = block[:64]
            target[2 * pair + 1, z] = block[64:]


def normalise(hidden):
    average = jnp.mean(hidden, axis=-1, keepdims=True)
    centred = hidden - average
    inv_std = lax.rsqrt(jnp.mean(centred * centred, axis=-1, keepdims=True) + EPSILON)
    return centred * inv_std, inv_std


def second_kernel(hidden, cot, gain, shift, second_out, cot_turned, stats):
    rows = hidden[...].astype(F32)
    average = jnp.mean(rows, axis=-1, keepdims=True)
    centred = rows - average
    inv_std = lax.rsqrt(jnp.mean(centred * centred, axis=-1, keepdims=True) + EPSILON)
    second_out[...] = (centred * inv_std * gain[...] + shift[...]).astype(BF16)
    put_turned(cot_turned, cot[...].astype(F32))
    lane = lax.broadcasted_iota(jnp.int32, (rows.shape[0], 128), 1)
    stats[...] = jnp.where(lane < 64, average, inv_std)


def first_kernel(hidden, gain, shift, gain_two, shift_two, first_out, first_turned, second_turned):
    normed, _ = normalise(hidden[...].astype(F32))
    first = normed * gain[...] + shift[...]
    first_out[...] = first.astype(BF16)
    put_turned(first_turned, first)
    put_turned(second_turned, normed * gain_two[...] + shift_two[...])


def first_far_kernel(near, other, gain, shift, gain_two, shift_two, *refs):
    first_out, second_out, first_turned, second_turned = refs[2:]

    def step(rows):
        normed, _ = normalise(rows)
        first = normed * gain[...] + shift[...]
        second = normed * gain_two[...] + shift_two[...]
        first_out[...] = first.astype(BF16)
        second_out[...] = second.astype(BF16)
        put_turned(first_turned, first)
        put_turned(second_turned, second)

    @pl.when(pl.program_id(0) < 2)
    def _():
        step(near[...])

    @pl.when(pl.program_id(0) >= 2)
    def _():
        step(other[...])


def cot_far_kernel(*refs):
    cot_out, cot_turned = refs[5:]
    for k in range(4):

        @pl.when(pl.program_id(0) == k)
        def _(k=k):
            rows = refs[k][...]
            cot_out[...] = rows.astype(BF16)
            put_turned(cot_turned, rows)


TURNED = (16, 2, 64, 2 * TOK)


def norm_call(kernel, rows, n_rows, n_plain, n_turned, params, far=(), stats=False):
    steps = TOK // rows
    plain = pl.BlockSpec((rows, D), lambda i: (i, 0))
    shift = steps if far else 0
    turned = pl.BlockSpec((16, 2, 64, rows), lambda i: (0, 0, 0, i + shift))
    if len(n_rows) == 4:
        specs = [whole((rows, D))] * 4
    elif far:
        picks = (lambda i: (lax.min(i, 1), 0), lambda i: (lax.max(i - 2, 0), 0))
        specs = [pl.BlockSpec((rows, D), p) for p in picks]
    else:
        specs = [plain] * len(n_rows)
    operands = list(n_rows) + [p.reshape(1, D) for p in params]
    aliases = {len(operands) + i: n_plain + i for i in range(len(far))}
    return pl.pallas_call(
        kernel,
        grid=(steps,),
        in_specs=specs + [whole((1, D))] * len(params) + [pl.BlockSpec(memory_space=pl.ANY)] * len(far),
        out_specs=[plain] * n_plain
        + [turned] * n_turned
        + [pl.BlockSpec((rows, 128), lambda i: (i, 0))] * stats,
        out_shape=[jax.ShapeDtypeStruct((TOK, D), BF16)] * n_plain
        + [jax.ShapeDtypeStruct(TURNED, BF16)] * n_turned
        + [jax.ShapeDtypeStruct((TOK, 128), F32)] * stats,
        input_output_aliases=aliases,
        compiler_params=pltpu.CompilerParams(vmem_limit_bytes=VMEM),
        cost_estimate=COST,
    )(*operands, *far)


def phi(upward):
    return 0.5 * (1.0 + lax.erf(upward * math.sqrt(0.5)))


def gelu_slope(upward, below):
    return below + upward * (jnp.exp(-0.5 * upward * upward) * (1.0 / math.sqrt(2.0 * math.pi)))


def as_row(block):
    return jnp.concatenate([block[i : i + 1, :] for i in range(block.shape[0])], axis=1)


def feed_kernel(second, cot_turned, weight, bias, act_out, slope_out, down_grad):
    upward = plain_dot(second[...], weight[...]) + as_row(bias[0])
    below = phi(upward)
    act = (upward * below).astype(BF16)
    act_out[...] = act
    slope_out[...] = gelu_slope(upward, below)
    down_grad[...] = plain_dot(cot_turned[...].reshape(D, TOK), act).reshape(16, 128, -1)


def feed(second, cot_turned, weight, bias):
    units, width = weight.shape[1], 512
    column = pl.BlockSpec((TOK, width), lambda j: (0, j))
    return pl.pallas_call(
        feed_kernel,
        grid=(units // width,),
        in_specs=[
            whole((TOK, D)),
            whole((16, 2, 64, TOK)),
            pl.BlockSpec((D, width), lambda j: (0, j)),
            pl.BlockSpec((1, width // 128, 128), lambda j: (j, 0, 0)),
        ],
        out_specs=[column, column, pl.BlockSpec((16, 128, width), lambda j: (0, 0, j))],
        out_shape=[
            jax.ShapeDtypeStruct((TOK, units), BF16),
            jax.ShapeDtypeStruct((TOK, units), F32),
            jax.ShapeDtypeStruct((16, 128, units), F32),
        ],
        compiler_params=pltpu.CompilerParams(vmem_limit_bytes=VMEM),
        cost_estimate=COST,
    )(second, cot_turned, weight, bias.reshape(-1, width // 128, 128))


def feed_back_kernel(side, cot, weight, slope, up_grad):
    up_grad[...] = (contract_cols(cot[...], weight[...]) * slope[...]).astype(BF16)


def feed_back(side, cot, weight, slope):
    units, width = slope.shape[1], 512
    steps = units // width
    far = units < weight.shape[0]
    column = pl.BlockSpec((TOK, width), lambda j, s: (0, j))
    return pl.pallas_call(
        feed_back_kernel,
        grid_spec=pltpu.PrefetchScalarGridSpec(
            num_scalar_prefetch=1,
            grid=(steps,),
            in_specs=[
                whole((TOK, D)),
                pl.BlockSpec((width, D), lambda j, s: (s[0] * steps * far + j, 0)),
                column,
            ],
            out_specs=column,
        ),
        out_shape=jax.ShapeDtypeStruct((TOK, units), BF16),
        compiler_params=pltpu.CompilerParams(vmem_limit_bytes=VMEM),
        cost_estimate=COST,
    )(side, cot, weight, slope)


def slope_far_kernel(side, second, weight, bias, slope):
    upward = plain_dot(second[...], weight[...]) + as_row(bias[0])
    slope[...] = gelu_slope(upward, phi(upward))


def slope_far(side, second, weight, bias):
    units, width = weight.shape[1] // 2, 512
    steps = units // width
    return pl.pallas_call(
        slope_far_kernel,
        grid_spec=pltpu.PrefetchScalarGridSpec(
            num_scalar_prefetch=1,
            grid=(steps,),
            in_specs=[
                whole((TOK, D)),
                pl.BlockSpec((D, width), lambda j, s: (0, s[0] * steps + j)),
                pl.BlockSpec((1, width // 128, 128), lambda j, s: (s[0] * steps + j, 0, 0)),
            ],
            out_specs=pl.BlockSpec((TOK, width), lambda j, s: (0, j)),
        ),
        out_shape=jax.ShapeDtypeStruct((TOK, units), F32),
        compiler_params=pltpu.CompilerParams(vmem_limit_bytes=VMEM),
        cost_estimate=COST,
    )(side, second, weight, bias.reshape(-1, width // 128, 128))


def turn(values, tables, sign):
    first = values[:, :128]
    cosine, rising, falling = tables
    first = (
        first * cosine[...]
        + (pltpu.roll(first, 32, 1) * rising[...] + pltpu.roll(first, 96, 1) * falling[...]) * sign
    )
    return jnp.concatenate([first, values[:, 128:]], axis=1)


def as_column(row):
    return jnp.broadcast_to(row, (8, row.shape[1])).T[:, 0:1]


def project_kernel(place, first, weight, bias, marks, inverse, queries, keys, values, *tables):
    @pl.when(pl.program_id(0) == 0)
    def _():
        lane = lax.broadcasted_iota(jnp.int32, (TOK, 128), 1)
        angles = as_column(marks[1:2, :]) * inverse[...]
        sine = jnp.sin(angles)
        tables[0][...] = jnp.where(lane < ROT, jnp.cos(angles), 1.0)
        tables[1][...] = jnp.where((lane >= ROT // 2) & (lane < ROT), sine, 0.0)
        tables[2][...] = jnp.where(lane < ROT // 2, -sine, 0.0)

    head = pl.program_id(0) + place[0] * (2 - pl.num_programs(0))
    packed = plain_dot(first[...], weight[...]) + bias[pl.ds(head, 1), :]
    queries[...] = turn(packed[:, :HD], tables, 1.0).astype(BF16)
    keys[...] = turn(packed[:, HD : 2 * HD], tables, 1.0).astype(BF16)
    values[...] = packed[:, 2 * HD :].astype(BF16)


def project(place, heads, first, weight, bias, marks):
    inverse = (10000.0 ** (-2.0 * (np.arange(128) % (ROT // 2)) / ROT)).astype(np.float32)
    inverse = jnp.asarray(inverse.reshape(1, 128))
    at = (lambda h, s: h) if heads == 2 else (lambda h, s: s[0])
    column = pl.BlockSpec((TOK, HD), lambda h, s: (0, h))
    return pl.pallas_call(
        project_kernel,
        grid_spec=pltpu.PrefetchScalarGridSpec(
            num_scalar_prefetch=1,
            grid=(heads,),
            in_specs=[
                whole((TOK, D)),
                pl.BlockSpec((D, 3 * HD), lambda h, s: (0, at(h, s))),
                whole((2, 3 * HD)),
                whole((2, TOK)),
                whole((1, 128)),
            ],
            out_specs=[column] * 3 + [pl.BlockSpec((TOK, 128), lambda h, s: (0, 0))] * 3,
        ),
        out_shape=[jax.ShapeDtypeStruct((TOK, heads * HD), BF16)] * 3
        + [jax.ShapeDtypeStruct((TOK, 128), F32)] * 3,
        compiler_params=pltpu.CompilerParams(vmem_limit_bytes=VMEM),
        cost_estimate=COST,
    )(place, first, weight, bias, marks, inverse)


def attend_kernel(
    place, queries, keys, values, cosine, rising, falling, cot, dense, marks, mixed_out, grad_out
):
    tables = (cosine, rising, falling)
    scale = 1.0 / math.sqrt(HD)
    queries, keys, values = queries[...], keys[...], values[...]
    segments = marks[0:1, :]

    def order(axis):
        return lax.rem(lax.broadcasted_iota(jnp.int32, (TOK, TOK), axis) + place[1], TOK)

    allowed = (as_column(segments) == segments) & (order(0) >= order(1))
    scores = jnp.where(allowed, contract_cols(queries, keys) * scale, NEGATIVE)
    top = jnp.max(scores, axis=-1, keepdims=True)
    weights = jnp.exp(scores - top)
    probs = weights / jnp.sum(weights, axis=-1, keepdims=True)
    probs_low = probs.astype(BF16)
    mixed_out[...] = plain_dot(probs_low, values).astype(BF16)
    grad_mixed = contract_cols(cot[...], dense[...]).astype(BF16)
    grad_probs = contract_cols(grad_mixed, values)
    along = jnp.sum(probs * grad_probs, axis=-1, keepdims=True)
    grad_scores = (probs * (grad_probs - along)).astype(BF16)
    grad_query = plain_dot(grad_scores, keys) * scale
    grad_key = plain_dot(grad_scores.T, queries) * scale
    grad_value = plain_dot(probs_low.T, grad_mixed)
    grad_out[:, :HD] = turn(grad_query, tables, -1.0).astype(BF16)
    grad_out[:, HD : 2 * HD] = turn(grad_key, tables, -1.0).astype(BF16)
    grad_out[:, 2 * HD :] = grad_value.astype(BF16)


def attend(place, heads, projected, cot, dense, marks):
    at = (lambda h, s: h) if heads == 2 else (lambda h, s: s[0])
    column = pl.BlockSpec((TOK, HD), lambda h, s: (0, h))
    return pl.pallas_call(
        attend_kernel,
        grid_spec=pltpu.PrefetchScalarGridSpec(
            num_scalar_prefetch=1,
            grid=(heads,),
            in_specs=[column] * 3
            + [whole((TOK, 128))] * 3
            + [whole((TOK, D)), pl.BlockSpec((HD, D), lambda h, s: (at(h, s), 0)), whole((2, TOK))],
            out_specs=[column, pl.BlockSpec((TOK, 3 * HD), lambda h, s: (0, h))],
        ),
        out_shape=[
            jax.ShapeDtypeStruct((TOK, heads * HD), BF16),
            jax.ShapeDtypeStruct((TOK, heads * 3 * HD), BF16),
        ],
        compiler_params=pltpu.CompilerParams(vmem_limit_bytes=VMEM),
        cost_estimate=COST,
    )(place, *projected, cot, dense, marks)


def put_halves(core, values, scratch, mine, other):
    scratch[...] = values
    half = TOK // 2
    mine[...] = scratch[pl.ds(pl.multiple_of(core[0] * half, half), half), :]
    other[...] = scratch[pl.ds(pl.multiple_of((1 - core[0]) * half, half), half), :]


def branch_kernel(core, mixed, act, dense, down, mine, other, scratch):
    total = plain_dot(act[...], down[...]) + plain_dot(mixed[...], dense[...])
    put_halves(core, total, scratch, mine, other)


def back_kernel(
    core, packed, up_grad, qkv, up, hidden, stats, gain, gain_two, mine, other, sums, scratch
):
    first = contract_cols(packed[...], qkv[...])
    second = contract_cols(up_grad[...], up[...])
    put_halves(core, first * gain[...] + second * gain_two[...], scratch, mine, other)
    normed = (hidden[...].astype(F32) - stats[:, 0:1]) * stats[:, 64:65]
    rows = [
        jnp.sum(v, axis=0, keepdims=True) for v in (first * normed, first, second * normed, second)
    ]
    sums[...] = jnp.concatenate(rows + [jnp.zeros((4, first.shape[1]), F32)], axis=0)


def halves_call(kernel, core, operands, specs, with_sums):
    width = 512
    half = pl.BlockSpec((TOK // 2, width), lambda j, s: (0, j))
    return pl.pallas_call(
        kernel,
        grid_spec=pltpu.PrefetchScalarGridSpec(
            num_scalar_prefetch=1,
            grid=(D // width,),
            in_specs=specs,
            out_specs=[half, half] + [pl.BlockSpec((8, width), lambda j, s: (0, j))] * with_sums,
            scratch_shapes=[pltpu.VMEM((TOK, width), F32)],
        ),
        out_shape=[jax.ShapeDtypeStruct((TOK // 2, D), F32)] * 2
        + [jax.ShapeDtypeStruct((8, D), F32)] * with_sums,
        compiler_params=pltpu.CompilerParams(vmem_limit_bytes=VMEM),
        cost_estimate=COST,
    )(core, *operands)


def branch_halves(core, mixed, act, dense, down):
    specs = [whole(mixed.shape), whole(act.shape)]
    specs += [pl.BlockSpec((w.shape[0], 512), lambda j, s: (0, j)) for w in (dense, down)]
    return halves_call(branch_kernel, core, (mixed, act, dense, down), specs, False)


def back_halves(core, packed, up_grad, qkv, up, hidden, stats, gain, gain_two):
    specs = [whole(packed.shape), whole(up_grad.shape)]
    specs += [pl.BlockSpec((512, w.shape[1]), lambda j, s: (j, 0)) for w in (qkv, up)]
    specs += [pl.BlockSpec((TOK, 512), lambda j, s: (0, j)), whole((TOK, 128))]
    specs += [pl.BlockSpec((1, 512), lambda j, s: (0, j))] * 2
    operands = (packed, up_grad, qkv, up, hidden, stats, gain.reshape(1, D), gain_two.reshape(1, D))
    return halves_call(back_kernel, core, operands, specs, True)


def joint_kernel(side, *refs):
    lefts, rights, target, held, arrived = refs[:3], refs[3:9], refs[9], refs[10:13], refs[13]
    step = pl.program_id(0)
    copies = [pltpu.make_async_copy(lefts[k], held[k], arrived.at[k]) for k in range(3)]

    @pl.when(step == 0)
    def _():
        for copy in copies:
            copy.start()

    for k, (start, stop) in enumerate(((0, 4), (4, 5), (5, 8))):

        @pl.when(step == start)
        def _(k=k):
            copies[k].wait()

        @pl.when((step >= start) & (step < stop))
        def _(k=k):
            right = jnp.concatenate([rights[2 * k][...], rights[2 * k + 1][...]], axis=0)
            total = plain_dot(held[k][...].reshape(D, 2 * TOK), right)
            target[...] = total.reshape(16, 128, -1)


def joint(side, lefts, rights):
    width = 256
    specs = [pl.BlockSpec(memory_space=pl.ANY)] * 3
    for start, n in ((0, 4), (4, 1), (5, 3)):

        def near(j, s, start=start, n=n):
            return (0, s[0] * n + jnp.clip(j - start, 0, n - 1))

        def far(j, s, start=start, n=n):
            return (0, jnp.clip(j - start, 0, n - 1))

        specs += [pl.BlockSpec((TOK, width), near), pl.BlockSpec((TOK, width), far)]
    return pl.pallas_call(
        joint_kernel,
        grid_spec=pltpu.PrefetchScalarGridSpec(
            num_scalar_prefetch=1,
            grid=(8,),
            in_specs=specs,
            out_specs=pl.BlockSpec((16, 128, width), lambda j, s: (0, 0, j)),
            scratch_shapes=[pltpu.VMEM(TURNED, BF16)] * 3 + [pltpu.SemaphoreType.DMA((3,))],
        ),
        out_shape=jax.ShapeDtypeStruct((16, 128, 8 * width), F32),
        compiler_params=pltpu.CompilerParams(vmem_limit_bytes=VMEM),
        cost_estimate=COST,
    )(side, *lefts, *rights)


def body(
    hidden_in,
    segment_ids,
    positions,
    ln1_gain,
    ln1_bias,
    qkv_weight,
    qkv_bias,
    dense_weight,
    dense_bias,
    ln2_gain,
    ln2_bias,
    fc1_weight,
    fc1_bias,
    fc2_weight,
    fc2_bias,
    cotangent,
):
    core = lax.axis_index("c")
    side = lax.axis_index("zl")
    half_rows = TOK // 2
    at_side = side.astype(jnp.int32).reshape(1)
    at_core = core.astype(jnp.int32).reshape(1)
    own_place = jnp.zeros((2,), jnp.int32)
    far_place = jnp.stack([side, core * half_rows]).astype(jnp.int32)
    after = lax.optimization_barrier
    params = (ln1_gain, ln1_bias, ln2_gain, ln2_bias)

    def of_core(values, which):
        return lax.dynamic_slice_in_dim(values, which * half_rows, half_rows, 0)

    def both_cores(mine):
        theirs = send(mine, "c")
        filled = jnp.zeros((TOK,) + mine.shape[1:], mine.dtype)
        filled = lax.dynamic_update_slice_in_dim(filled, mine, core * half_rows, 0)
        return lax.dynamic_update_slice_in_dim(filled, theirs, (1 - core) * half_rows, 0)

    marks = jnp.concatenate([segment_ids, positions]).astype(F32).reshape(1, 2 * TOK)
    hidden_sent = jnp.concatenate(
        [of_core(hidden_in, core).astype(F32), jnp.pad(marks, ((0, 7), (0, D - 2 * TOK)))], axis=0
    )
    hidden_pair = lax.all_gather(hidden_sent, "zl")

    second_in, cot_turned, stats = norm_call(
        second_kernel, 256, (hidden_in, cotangent), 1, 1, (ln2_gain, ln2_bias), stats=True
    )
    act_low, slope, down_grad = feed(second_in, cot_turned, fc1_weight, fc1_bias)
    down_sum = after(lax.psum_scatter(down_grad, ("x", "y"), scatter_dimension=0, tiled=True))
    _, cotangent, hidden_in = after((down_grad, cotangent, hidden_in))
    cot_sent = of_core(cotangent, core).astype(F32)
    cot_got = send(cot_sent[:128], "zl")

    own_marks = marks.reshape(2, TOK)

    def own_step(hidden_in, cotangent, act_low, slope):
        first_in, first_turned, second_turned = norm_call(
            first_kernel, 256, (hidden_in,), 1, 2, params
        )
        projected = project(own_place, 2, first_in, qkv_weight, qkv_bias, own_marks)
        mixed_low, grad_packed = attend(
            own_place, 2, projected, cotangent, dense_weight, own_marks
        )
        grad_up = feed_back(at_side, cotangent, fc2_weight, slope)
        branches = branch_halves(at_core, mixed_low, act_low, dense_weight, fc2_weight)
        backs = back_halves(
            at_core,
            grad_packed,
            grad_up,
            qkv_weight,
            fc1_weight,
            hidden_in,
            stats,
            ln1_gain,
            ln2_gain,
        )
        return (first_turned, second_turned, mixed_low, grad_packed, grad_up, *branches, *backs)

    (
        first_turned,
        second_turned,
        mixed_low,
        grad_packed,
        grad_up,
        branch,
        branch_other,
        combined,
        combined_other,
        norms,
    ) = lax.cond(core == 0, own_step, own_step, hidden_in, cotangent, act_low, slope)
    hidden_pair, branch_other, combined_other, cot_got, cot_sent = after(
        (hidden_pair, branch_other, combined_other, cot_got, cot_sent)
    )
    cot_got_too = send(cot_sent[128:], "zl")
    branch = branch + send(branch_other, "c")
    combined = combined + send(combined_other, "c")
    hidden_got = lax.dynamic_index_in_dim(hidden_pair, 1 - side, 0, keepdims=False)

    def far_step(hidden_got, hidden_too, first_turned, second_turned):
        first_far, second_far, first_turned, second_turned = norm_call(
            first_far_kernel,
            128,
            (hidden_got, hidden_too),
            2,
            2,
            params,
            (first_turned, second_turned),
        )
        slope_side = slope_far(at_side, second_far, fc1_weight, fc1_bias)
        marks_got = hidden_got[half_rows, : 2 * TOK].reshape(2, 2, half_rows)
        marks_far = jnp.where(core == 0, marks_got, marks_got[:, ::-1]).reshape(2, TOK)
        projected_far = project(far_place, 1, first_far, qkv_weight, qkv_bias, marks_far)
        return first_turned, second_turned, slope_side, marks_far, *projected_far

    first_turned, second_turned, slope_side, marks_far, *projected_far = lax.cond(
        core == 0,
        far_step,
        far_step,
        hidden_got,
        send(hidden_got, "c"),
        first_turned,
        second_turned,
    )

    slope_side, projected_far, cot_got_too, branch, combined = after(
        (slope_side, projected_far, cot_got_too, branch, combined)
    )
    cot_far, cot_turned = norm_call(
        cot_far_kernel,
        128,
        (cot_got, cot_got_too, send(cot_got, "c"), send(cot_got_too, "c")),
        1,
        1,
        (),
        (cot_turned,),
    )
    branch = lax.psum(branch, "zh")
    combined = lax.psum(combined, "zh")
    grad_up_far = feed_back(at_side, cot_far, fc2_weight, slope_side)
    mixed_far, grad_packed_far = attend(
        far_place, 1, projected_far, cot_far, dense_weight, marks_far
    )
    joint_grad = joint(
        at_side,
        (second_turned, cot_turned, first_turned),
        (grad_up, grad_up_far, mixed_low, mixed_far, grad_packed, grad_packed_far),
    )
    joint_grad, down_sum = after((joint_grad, down_sum))
    joint_sum = after(lax.psum_scatter(joint_grad, ("x", "y"), scatter_dimension=0, tiled=True))
    _, norms, grad_packed, grad_up, cotangent, down_sum = after(
        (joint_grad, norms, grad_packed, grad_up, cotangent, down_sum)
    )

    norms = norms[:4].reshape(4, 32, 64).transpose(1, 0, 2).reshape(32, 256)
    norms = norms + send(norms, "c")
    norms = norms + send(norms, "zh")
    grad_out = cotangent.astype(F32)
    bias_sum = jnp.sum(grad_out, axis=0)
    qkv_bias_sum = jnp.sum(grad_packed.astype(F32), axis=0)
    up_bias_grad = jnp.sum(grad_up.astype(F32), axis=0)
    small = jnp.concatenate(
        [
            norms,
            bias_sum.reshape(32, 64),
            qkv_bias_sum.reshape(2, 32, 24).transpose(1, 0, 2).reshape(32, 48),
            up_bias_grad.reshape(16, 32, 4).transpose(1, 0, 2).reshape(32, 64),
            jnp.zeros((32, 80), F32),
        ],
        axis=1,
    )
    for axis in ("x", "y"):
        small = small + swap(small, axis, 1)
        small = small + swap(small, axis, 2)
    block = lax.axis_index("x") * 4 + lax.axis_index("y")
    own_small = lax.dynamic_slice_in_dim(small, side * 16 + block, 1, 0)
    far_small = lax.dynamic_slice_in_dim(small, (1 - side) * 16 + block, 1, 0)
    small = (own_small + send(far_small, "zl")).reshape(-1)

    small, branch, combined = after((small, branch, combined))
    norms = small[:256].reshape(4, 64)
    bias_total = small[256:320]
    hidden = hidden_in.astype(F32)
    output = both_cores(of_core(hidden, core) + branch + dense_bias + fc2_bias)
    own_stats = of_core(stats, core)
    average, inv_std = own_stats[:, 0:1], own_stats[:, 64:65]
    normed_half = (of_core(hidden, core) - average) * inv_std
    input_half = of_core(grad_out, core) + inv_std * (
        combined
        - jnp.mean(combined, axis=-1, keepdims=True)
        - normed_half * jnp.mean(combined * normed_half, axis=-1, keepdims=True)
    )
    input_grad = both_cores(input_half)

    def of_side(values, which):
        return lax.dynamic_slice_in_dim(values[0], which * 64, 64, 0)

    down_sum = of_side(down_sum, side) + send(of_side(down_sum, 1 - side), "zl")
    near = of_side(joint_sum, side)
    far = send(of_side(joint_sum, 1 - side), "zl")
    low = jnp.where(side == 0, near, far)
    high = jnp.where(side == 0, far, near)
    sums = []
    start = 0
    for width in (1024, 256, 768):
        stop = start + width
        sums.append(jnp.concatenate([low[:, start:stop], high[:, start:stop]], axis=1))
        start = stop
    up_sum, dense_sum, qkv_sum = sums
    return (
        output,
        input_grad,
        norms[0],
        norms[1],
        qkv_sum,
        small[320:368].reshape(2, 24),
        dense_sum.T,
        bias_total,
        norms[2],
        norms[3],
        up_sum,
        small[368:432].reshape(16, 4),
        down_sum.T,
        bias_total,
    )


def solution(mesh):
    fine = Mesh(mesh.devices.reshape(tuple(SIZES.values())), tuple(SIZES))
    return jax.shard_map(
        body,
        mesh=fine,
        in_specs=(
            P(DP, None),
            P(DP),
            P(DP),
            P(),
            P(),
            P(None, TENSOR),
            P(TENSOR, None),
            P(TENSOR, None),
            P(),
            P(),
            P(),
            P(None, TENSOR),
            P(TENSOR, None),
            P(TENSOR, None),
            P(),
            P(DP, None),
        ),
        out_specs=(
            P(DP, None),
            P(DP, None),
            P(DP),
            P(DP),
            P(DP, TENSOR),
            P(TENSOR, DP),
            P(TENSOR, DP),
            P(DP),
            P(DP),
            P(DP),
            P(DP, TENSOR),
            P(TENSOR, DP),
            P(TENSOR, DP),
            P(DP),
        ),
        check_vma=False,
    )
```

time: 325 us -> 333 us (1.025)
  Pallas kernels: 101 us -> 136 us
  matrix products: 32.1 us -> 0 us
  loops' own time: 0 us -> 9.17 us
  other arithmetic: 32.8 us -> 25.2 us
    pallas_call x2 -> x7, Pallas kernels: 20.6 us -> 63.9 us  [the longest x2 24.9 us: halves_call(): pl.pallas_call(kernel, grid_spec=pltpu.PrefetchScalarGridSpec(num_scalar_...]
    dot_general x6 -> x0, matrix products: 32.1 us -> none  [the longest x4 18.9 us: plain_dot(): return jnp.dot(left, right, preferred_element_type=F32)]
    psum x1, waiting for transfers between devices: 20.1 us -> 40.3 us  [body(): branch = lax.psum(branch, 'zh')]
    unnamed x5, waiting for transfers between devices: 20.7 us -> 4.87 us
    all_gather x1, waiting for transfers between devices: 10.5 us -> 0.02 us  [body(): hidden_pair = lax.all_gather(hidden_sent, 'zl')]
    pallas_call x2, Pallas kernels: 24.6 us -> 15.2 us  [attend(): pl.pallas_call(attend_kernel, grid_spec=pltpu.PrefetchScalarGridSpec(num_...]
    another operation x0 -> x2, loops' own time: none -> 9.17 us  [the longest x1 8.89 us: body(): lax.cond(core == 0, own_step, own_step, hidden_in, cotangent, act_low, sl...]
    ppermute x11 -> x14, waiting for transfers between devices: 24.3 us -> 31.3 us  [send(): return lax.ppermute(value, axis, [(i, (i + step) % n) for i in range(n)])]
  transfers between devices with their start and end apart: 19 -> 22, of which waited for: 11 -> 13; matrix products, arithmetic and copies ran while one was open for 24% -> 11% of each run, Pallas kernels for 31% -> 41%
where the time goes in v1:
time: 333 us; the launch traced here: 328 us
  Pallas kernels  136 us (41%)
  waiting for transfers between devices  93 us (28%)
  local copies, waits for them, and re-layouts  29.3 us (9%)
  other arithmetic  25.2 us (8%)
  starting transfers between devices  19.7 us (6%)
  between operations  16.1 us (5%)
  loops' own time  9.17 us (3%)
    psum x1, waiting for transfers between devices, body(): branch = lax.psum(branch, 'zh')  40.3 us
    ppermute x14, waiting for transfers between devices, send(): return lax.ppermute(value, axis, [(i, (i + step) % n) for i in range(n)])  31.3 us
    pallas_call x2, Pallas kernels, halves_call(): pl.pallas_call(kernel, grid_spec=pltpu.PrefetchScalarGridSpec(num_scalar_...  24.9 us
    pallas_call x4, Pallas kernels, norm_call(): pl.pallas_call(kernel, grid=(steps,), in_specs=specs + [whole((1, D))] *...  23.4 us
    pallas_call x2, Pallas kernels, feed_back(): pl.pallas_call(feed_back_kernel, grid_spec=pltpu.PrefetchScalarGridSpec(n...  17.4 us
    pallas_call x1, Pallas kernels, joint(): pl.pallas_call(joint_kernel, grid_spec=pltpu.PrefetchScalarGridSpec(num_s...  16.6 us
    pallas_call x1, Pallas kernels, feed(): pl.pallas_call(feed_kernel, grid=(units // width,), in_specs=[whole((TOK,...  16.6 us
    ppermute x4, waiting for transfers between devices, swap(): return lax.ppermute(value, axis, [(i, i ^ bit) for i in range(SIZES[axis])])  16.5 us
  transfers between devices with their start and end apart: 22, of which 13 were waited for; matrix products, arithmetic and copies ran while one was open for 11% of the time, Pallas kernels for 41%

profile of v1, /device:TPU:0, one launch (start us, length us, event | category | flops | bytes accessed | tf_op | source)
XLA Modules:
  0.0 328.3 jit_solution(17674543227510614189)
XLA Ops:
  12.7 4.6 %shard_map.281 = (bf16[512,2048]{1,0:T(8,128)(2,1)}, bf16[16,2,64,1024]{3,2,1,0:T(8,128)(2,1)}, f32[512,128]{1,0:T(8,128)S(1)}) custom-call(bf16[512,2048]{1,0:T(8,128)(2,1)} %hidden.1, bf16[512,2048]{1,0:T(8,128)(2,1)S(1)} %copy-done, f32[1,2048]{1,0:T(1,128)S(1)} %bitcast.69, f32[1,2048]{1,0:T(1,128)S(1)} %bitcast.83), custom_call_target="tpu_custom_call" | custom-call | flops 1000000 | bytes 1000000 | tf_op jit(solution)/shard_map/pallas_call | solution.py:134
  17.3 16.6 %shard_map.282 = (bf16[512,2048]{1,0:T(8,128)(2,1)}, f32[512,2048]{1,0:T(8,128)}, f32[16,128,2048]{2,1,0:T(8,128)}) custom-call(bf16[512,2048]{1,0:T(8,128)(2,1)} %get-tuple-element.327.second, bf16[16,2,64,1024]{3,2,1,0:T(8,128)(2,1)} %get-tuple-element.328.cot_turned.refs_4_, bf16[2048,2048]{1,0:T(8,128)(2,1)} %weight.2, f32[4,4,128]{2,1,0:T(4,128)S(1)} %bitcast.95), custom_call_target="tpu_custom_call" | custom-call | flops 1000000 | bytes 1000000 | tf_op jit(solution)/shard_map/pallas_call | solution.py:174
  38.9 69.3 %conditional.2 = (bf16[16,2,64,1024]{3,2,1,0:T(8,128)(2,1)}, bf16[16,2,64,1024]{3,2,1,0:T(8,128)(2,1)}, bf16[512,512]{1,0:T(8,128)(2,1)}, bf16[512,1536]{1,0:T(8...) conditional(s32[]{:T(128)} %convert_element_type.41, ...), branch_computations={%region_0.1_spmd, %region_1.2_spmd} | conditional | flops 6000000 | bytes 54234748 | solution.py:553
  47.7 6.1 %branch_1_fun.9 = (bf16[512,2048]{1,0:T(8,128)(2,1)}, bf16[16,2,64,1024]{3,2,1,0:T(8,128)(2,1)}, bf16[16,2,64,1024]{3,2,1,0:T(8,128)(2,1)}) custom-call(bf16[512,2048]{1,0:T(8,128)(2,1)} %get-tuple-element.170.hidden, f32[1,2048]{1,0:T(1,128)S(1)} %bitcast.78, f32[1,2048]{1,0:T(1,128)S(1)} %bitcast.89, f32[1,2048]{1,0:T(1,128)S(1)} %bitcast.72, ...), custom_call_target="tpu_custom_call" | custom-call | flops 1000000 | bytes 1000000 | tf_op jit(solution)/shard_map/cond/branch_1_fun/pallas_call | solution.py:134
  54.3 9.3 %branch_1_fun.10 = (bf16[512,512]{1,0:T(8,128)(2,1)}, bf16[512,512]{1,0:T(8,128)(2,1)}, bf16[512,512]{1,0:T(8,128)(2,1)}, f32[512,128]{1,0:T(8,128)}, f32[512,128]{1,0:T(8,128)}, /*index=5*/f32[512,128]{1,0:T(8,128)}) custom-call(s32[2]{0:T(128)} %broadcast_5_place.0.place, bf16[512,2048]{1,0:T(8,128)(2,1)} %get-tuple-element.177.first, ...), custom_call_target="tpu_custom_call" | custom-call | flops 1000000 | bytes 1000000 | tf_op jit(solution)/shard_map/cond/branch_1_fun/pallas_call | solution.py:283
  63.6 8.9 %branch_1_fun.11 = (bf16[512,512]{1,0:T(8,128)(2,1)}, bf16[512,1536]{1,0:T(8,128)(2,1)}) custom-call(s32[2]{0:T(128)} %broadcast_5_place.0.place, bf16[512,512]{1,0:T(8,128)(2,1)} %get-tuple-element.182.queries, bf16[512,512]{1,0:T(8,128)(2,1)} %get-tuple-element.183.keys, bf16[512,512]{1,0:T(8,128)(2,1)} %get-tuple-element.184.values, ...), custom_call_target="tpu_custom_call" | custom-call | flops 1000000 | bytes 1000000 | tf_op jit(solution)/shard_map/cond/branch_1_fun/pallas_call | solution.py:337
  72.5 10.8 %branch_1_fun.12.up_grad = bf16[512,2048]{1,0:T(8,128)(2,1)} custom-call(s32[1]{0:T(128)} %get-tuple-element.192.side, bf16[512,2048]{1,0:T(8,128)(2,1)} %copy-done.3, bf16[2048,2048]{1,0:T(8,128)(2,1)} %get-tuple-element.193.weight.down, f32[512,2048]{1,0:T(8,128)} %get-tuple-element.194.slope), custom_call_target="tpu_custom_call" | custom-call | flops 1000000 | bytes 1000000 | tf_op jit(solution)/shard_map/cond/branch_1_fun/pallas_call | solution.py:203
  83.3 13.8 %branch_1_fun.14 = (f32[256,2048]{1,0:T(8,128)}, f32[256,2048]{1,0:T(8,128)}, f32[8,2048]{1,0:T(8,128)S(1)}) custom-call(s32[1]{0:T(128)} %get-tuple-element.195.core, bf16[512,1536]{1,0:T(8,128)(2,1)S(1)} %copy-done.9, bf16[512,2048]{1,0:T(8,128)(2,1)} %branch_1_fun.12.up_grad, bf16[2048,1536]{1,0:T(8,128)(2,1)S(1)} %bitcast.62, ...), custom_call_target="tpu_custom_call" | custom-call | flops 1000000 | bytes 1000000 | tf_op jit(solution)/shard_map/cond/branch_1_fun/pallas_call | solution.py:384
  97.1 11.1 %branch_1_fun.13 = (f32[256,2048]{1,0:T(8,128)}, f32[256,2048]{1,0:T(8,128)}) custom-call(s32[1]{0:T(128)} %get-tuple-element.195.core, bf16[512,512]{1,0:T(8,128)(2,1)} %get-tuple-element.460.mixed, bf16[512,2048]{1,0:T(8,128)(2,1)} %get-tuple-element.196.act, bf16[512,2048]{1,0:T(8,128)(2,1)} %get-tuple-element.189.dense, ...), custom_call_target="tpu_custom_call" | custom-call | flops 1000000 | bytes 1000000 | tf_op jit(solution)/shard_map/cond/branch_1_fun/pallas_call | solution.py:384
  108.2 3.8 %dynamic-slice_bitcast_fusion = f32[264,2048]{1,0:T(8,128)} fusion(f32[2,264,2048]{2,1,0:T(8,128)} %bitcast.67, s32[]{:T(128)S(6)} %select_n.59), kind=kLoop, calls=%fused_computation.10 | loop fusion | bytes 4325380 | tf_op jit(solution)/shard_map/jit(dynamic_index_in_dim)/squeeze | solution.py:560
  113.8 5.6 %collective-permute-done.4 = f32[256,2048]{1,0:T(8,128)S(1)} collective-permute-done((f32[256,2048]{1,0:T(8,128)}, f32[256,2048]{1,0:T(8,128)S(1)}, u32[]{:S(2)}, u32[]{:S(2)}) %collective-permute-start.4) | collective-permute-done | bytes 2097184 | tf_op jit(solution)/shard_map/ppermute | solution.py:27
  119.4 3.2 add.107
  122.7 3.3 add.106
  125.9 21.4 %conditional.3 = (bf16[16,2,64,1024]{3,2,1,0:T(8,128)(2,1)}, bf16[16,2,64,1024]{3,2,1,0:T(8,128)(2,1)}, f32[512,1024]{1,0:T(8,128)}, f32[2,512]{1,0:T(2,128)S(1)...) conditional(s32[]{:T(128)} %convert_element_type.41, ...), branch_computations={%region_2.3_spmd, %region_3.4_spmd} | conditional | flops 3001025 | bytes 21952386 | solution.py:578
  127.1 7.9 %branch_1_fun.15 = (bf16[512,2048]{1,0:T(8,128)(2,1)}, bf16[512,2048]{1,0:T(8,128)(2,1)}, bf16[16,2,64,1024]{3,2,1,0:T(8,128)(2,1)}, bf16[16,2,64,1024]{3,2,1,0:T(8,128)(2,1)}) custom-call(f32[264,2048]{1,0:T(8,128)} %get-tuple-element.230.near, f32[264,2048]{1,0:T(8,128)} %get-tuple-element.231.other, ...), custom_call_target="tpu_custom_call", output_to_operand_aliasing={{2}: (6, {}), {3}: (7, {})} | custom-call | flops 1000000 | bytes 1000000 | tf_op jit(solution)/shard_map/cond/branch_1_fun/pallas_call | solution.py:134
  135.0 5.9 %branch_1_fun.17 = (bf16[512,256]{1,0:T(8,128)(2,1)}, bf16[512,256]{1,0:T(8,128)(2,1)}, bf16[512,256]{1,0:T(8,128)(2,1)}, f32[512,128]{1,0:T(8,128)}, f32[512,128]{1,0:T(8,128)}, /*index=5*/f32[512,128]{1,0:T(8,128)}) custom-call(s32[2]{0:T(128)S(1)} %get-tuple-element.245.place, bf16[512,2048]{1,0:T(8,128)(2,1)} %get-tuple-element.246.first, ...), custom_call_target="tpu_custom_call" | custom-call | flops 1000000 | bytes 1000000 | tf_op jit(solution)/shard_map/cond/branch_1_fun/pallas_call | solution.py:283
  140.9 6.4 %branch_1_fun.16 = f32[512,1024]{1,0:T(8,128)} custom-call(s32[1]{0:T(128)} %get-tuple-element.240.side, bf16[512,2048]{1,0:T(8,128)(2,1)} %get-tuple-element.241.second, bf16[2048,2048]{1,0:T(8,128)(2,1)} %get-tuple-element.242.weight, f32[4,4,128]{2,1,0:T(4,128)S(1)} %bitcast.97), custom_call_target="tpu_custom_call" | custom-call | flops 1000000 | bytes 1000000 | tf_op jit(solution)/shard_map/cond/branch_1_fun/pallas_call | solution.py:229
  152.8 4.9 %shard_map.283 = (bf16[512,2048]{1,0:T(8,128)(2,1)}, bf16[16,2,64,1024]{3,2,1,0:T(8,128)(2,1)}) custom-call(f32[128,2048]{1,0:T(8,128)} %collective-permute-done.refs_0_, f32[128,2048]{1,0:T(8,128)} %collective-permute-done.2.refs_1_, f32[128,2048]{1,0:T(8,128)} %copy-done.23, f32[128,2048]{1,0:T(8,128)} %copy-done.24, ...), custom_call_target="tpu_custom_call", output_to_operand_aliasing={{1}: (4, {})} | custom-call | flops 1000000 | bytes 1000000 | tf_op jit(solution)/shard_map/pallas_call | solution.py:134
  157.7 6.6 %shard_map.284.refs_4_ = bf16[512,1024]{1,0:T(8,128)(2,1)} custom-call(s32[1]{0:T(128)} %bitcast.21.side, bf16[512,2048]{1,0:T(8,128)(2,1)} %get-tuple-element.358.cot, bf16[2048,2048]{1,0:T(8,128)(2,1)} %weight.3, f32[512,1024]{1,0:T(8,128)} %get-tuple-element.359.slope), custom_call_target="tpu_custom_call" | custom-call | flops 1000000 | bytes 1000000 | tf_op jit(solution)/shard_map/pallas_call | solution.py:203
  164.3 6.3 %shard_map.285 = (bf16[512,256]{1,0:T(8,128)(2,1)}, bf16[512,768]{1,0:T(8,128)(2,1)}) custom-call(s32[2]{0:T(128)S(1)} %pad_add_fusion.place, bf16[512,256]{1,0:T(8,128)(2,1)} %get-tuple-element.361.queries, bf16[512,256]{1,0:T(8,128)(2,1)} %get-tuple-element.362.keys, bf16[512,256]{1,0:T(8,128)(2,1)} %get-tuple-element.363.values, ...), custom_call_target="tpu_custom_call" | custom-call | flops 1000000 | bytes 1000000 | tf_op jit(solution)/shard_map/pallas_call | solution.py:337
  170.6 16.6 %shard_map.286 = f32[16,128,2048]{2,1,0:T(8,128)} custom-call(s32[1]{0:T(128)} %bitcast.21.side, bf16[16,2,64,1024]{3,2,1,0:T(8,128)(2,1)} %get-tuple-element.340.refs_0_, bf16[16,2,64,1024]{3,2,1,0:T(8,128)(2,1)} %get-tuple-element.355.refs_1_, bf16[16,2,64,1024]{3,2,1,0:T(8,128)(2,1)} %get-tuple-element.356.refs_2_, ...), custom_call_target="tpu_custom_call" | custom-call | flops 1000000 | bytes 1000000 | tf_op jit(solution)/shard_map/pallas_call | solution.py:450
  190.3 3.6 %collective-permute-start.8 = (f32[32,256]{1,0:T(8,128)S(1)}, f32[32,256]{1,0:T(8,128)S(1)}, u32[]{:S(2)}, u32[]{:S(2)}) collective-permute-start(f32[32,256]{1,0:T(8,128)S(1)} %add.108), channel_id=1, source_target_pairs={{0,2},{2,0},{1,3},{3,1},{4,6},{6,4},{5,7},{7,5},{8,10},{10,8},{9,1... | collective-permute-start | bytes 98312 | tf_op jit(solution)/shard_map/ppermute | solution.py:27
  198.6 4.0 %collective-permute-done.9 = f32[32,512]{1,0:T(8,128)S(1)} collective-permute-done((f32[32,512]{1,0:T(8,128)S(1)}, f32[32,512]{1,0:T(8,128)S(1)}, u32[]{:S(2)}, u32[]{:S(2)}) %collective-permute-start.9) | collective-permute-done | bytes 65568 | tf_op jit(solution)/shard_map/ppermute | solution.py:31
  205.7 4.1 %collective-permute-done.10 = f32[32,512]{1,0:T(8,128)S(1)} collective-permute-done((f32[32,512]{1,0:T(8,128)S(1)}, f32[32,512]{1,0:T(8,128)S(1)}, u32[]{:S(2)}, u32[]{:S(2)}) %collective-permute-start.10) | collective-permute-done | bytes 65568 | tf_op jit(solution)/shard_map/ppermute | solution.py:31
  211.4 3.8 %collective-permute-done.11 = f32[32,512]{1,0:T(8,128)S(1)} collective-permute-done((f32[32,512]{1,0:T(8,128)S(1)}, f32[32,512]{1,0:T(8,128)S(1)}, u32[]{:S(2)}, u32[]{:S(2)}) %collective-permute-start.11) | collective-permute-done | bytes 65568 | tf_op jit(solution)/shard_map/ppermute | solution.py:31
  218.1 4.5 %collective-permute-done.12 = f32[32,512]{1,0:T(8,128)S(1)} collective-permute-done((f32[32,512]{1,0:T(8,128)S(1)}, f32[32,512]{1,0:T(8,128)S(1)}, u32[]{:S(2)}, u32[]{:S(2)}) %collective-permute-start.12) | collective-permute-done | bytes 65568 | tf_op jit(solution)/shard_map/ppermute | solution.py:31
  226.5 40.3 %all-reduce.6.cloned.1.call-done = (f32[256,2048]{1,0:T(8,128)}, f32[256,2048]{1,0:T(8,128)}) async-done(((f32[256,2048]{1,0:T(8,128)}, f32[256,2048]{1,0:T(8,128)}), (f32[256,2048]{1,0:T(8,128)}, f32[256,2048]{1,0:T(8,128)})) %all-reduce.6.cloned.1.call-update) | async-done | bytes 4194320 | tf_op jit(solution)/shard_map/psum | solution.py:600
  269.1 3.7 %fusion.11 = (f32[256]{0:T(256)S(1)}, f32[256]{0:T(256)S(1)}, f32[512,2048]{1,0:T(8,128)S(1)}, f32[256,2048]{1,0:T(8,128)}) fusion(f32[256,2048]{1,0:T(8,128)S(1)} %copy-done.16, f32[256]{0:T(256)S(1)} %get-tuple-element.428, f32[256]{0:T(256)S(1)} %get-tuple-element.429, bf16[512,2048]{1,0:T(8,128)(2,1)S(1)} %copy-done.4, s32[]{:T(128)S(6)} %select_n.58, ...), kind=kLoop, calls=%fused_computation.47 | loop fusion | flops 4718080 | bytes 9457668 | tf_op jit(solution)/shard_map/reduce_sum | solution.py:652
  285.1 11.5 %collective-permute-done.17 = f32[64,2048]{1,0:T(8,128)} collective-permute-done((f32[64,2048]{1,0:T(8,128)}, f32[64,2048]{1,0:T(8,128)}, u32[]{:S(2)}, u32[]{:S(2)}) %collective-permute-start.17) | collective-permute-done | bytes 524320 | tf_op jit(solution)/shard_map/ppermute | solution.py:27
  298.5 4.8 %reduce-scatter.9.cloned.1.call-done = f32[1,128,2048]{2,1,0:T(8,128)} async-done(((f32[16,128,2048]{2,1,0:T(8,128)}), f32[1,128,2048]{2,1,0:T(8,128)}) %reduce-scatter.9.cloned.1.call-update) | async-done | bytes 1048592
  305.9 3.3 %constant_dynamic-update-slice_fusion = f32[512,2048]{1,0:T(8,128)} fusion(f32[512,2048]{1,0:T(8,128)} %copy-done.17, f32[256,2048]{1,0:T(8,128)} %collective-permute-done.15, s32[]{:T(128)S(6)} %select_n.62), kind=kLoop, calls=%fused_computation.37 | loop fusion | bytes 4194308 | tf_op jit(solution)/shard_map/dynamic_update_slice | solution.py:500
  309.4 8.2 %collective-permute-done.16 = f32[64,2048]{1,0:T(8,128)S(1)} collective-permute-done((f32[64,2048]{1,0:T(8,128)S(1)}, f32[64,2048]{1,0:T(8,128)S(1)}, u32[]{:S(2)}, u32[]{:S(2)}) %collective-permute-start.16) | collective-permute-done | bytes 524320 | tf_op jit(solution)/shard_map/ppermute | solution.py:27
  (185 shorter events, 59.5 us)
Async XLA Ops:
  8.0 100.2 %all-gather.3.cloned.1.call-start = ((), (), s32[]{:S(2)}) async-start(), calls=%async_computation.2 | async-start | bytes 6488064 | tf_op jit(solution)/shard_map/all_gather | solution.py:506
  11.1 176.1 %reduce-scatter.7.cloned.1.call-start = ((), (), s32[]{:S(2)}) async-start(), calls=%async_computation.3 | async-start | bytes 17825792
  34.0 232.8 %all-reduce.6.cloned.1.call-start = ((), (), s32[]{:S(2)}) async-start(), calls=%async_computation.5 | async-start | bytes 8388608 | tf_op jit(solution)/shard_map/psum | solution.py:600
  36.8 71.4 %collective-permute-start = (f32[128,2048]{1,0:T(8,128)}, f32[128,2048]{1,0:T(8,128)}, u32[]{:S(2)}, u32[]{:S(2)}) collective-permute-start(f32[128,2048]{1,0:T(8,128)} %slice.98), channel_id=1, source_target_pairs={{0,64},{64,0},{1,65},{65,1},{2,66},{66,2},{3,67},{67,3},{4,68},{68... | collective-permute-start | bytes 3145736 | tf_op jit(solution)/shard_map/ppermute | solution.py:27
  47.7 15.8 %copy-start.3 = (bf16[512,2048]{1,0:T(8,128)(2,1)}, bf16[512,2048]{1,0:T(8,128)(2,1)S(1)}, u32[]{:S(2)}) copy-start(bf16[512,2048]{1,0:T(8,128)(2,1)S(1)} %get-tuple-element.188.cot) | copy-start | bytes 6291460 | tf_op jit(solution)/shard_map/cond
  72.4 10.8 %slice-start.2 = ((s8[6291456]{0:T(1024)(128)(4,1)}), s8[4194304]{0:T(1024)(128)(4,1)S(1)}, s32[]{:S(2)}) async-start(s8[6291456]{0:T(1024)(128)(4,1)} %bitcast.61), calls=%async_computation.8 | async-start | bytes 8388608 | tf_op jit(solution)/shard_map/cond
  72.4 10.8 %slice-start.3 = ((s8[6291456]{0:T(1024)(128)(4,1)}), s8[2097152]{0:T(1024)(128)(4,1)S(1)}, s32[]{:S(2)}) async-start(s8[6291456]{0:T(1024)(128)(4,1)} %bitcast.61), calls=%async_computation.9 | async-start | bytes 4194304 | tf_op jit(solution)/shard_map/cond
  72.4 10.8 %copy-start.9 = (bf16[512,1536]{1,0:T(8,128)(2,1)S(1)}, bf16[512,1536]{1,0:T(8,128)(2,1)}, u32[]{:S(2)}) copy-start(bf16[512,1536]{1,0:T(8,128)(2,1)} %get-tuple-element.461.packed) | copy-start | bytes 4718596 | tf_op jit(solution)/shard_map/cond
  97.1 11.1 %copy-start.10 = (bf16[512,1536]{1,0:T(8,128)(2,1)S(1)}, bf16[512,1536]{1,0:T(8,128)(2,1)}, u32[]{:S(2)}) copy-start(bf16[512,1536]{1,0:T(8,128)(2,1)} %get-tuple-element.461.packed) | copy-start | bytes 4718596 | tf_op jit(solution)/shard_map/cond
  108.2 62.4 %copy-start.11 = (bf16[512,1536]{1,0:T(8,128)(2,1)}, bf16[512,1536]{1,0:T(8,128)(2,1)S(1)}, u32[]{:S(2)}) copy-start(bf16[512,1536]{1,0:T(8,128)(2,1)S(1)} %get-tuple-element.376.refs_7_) | copy-start | bytes 4718596
  112.0 13.9 %collective-permute-start.1 = (f32[264,2048]{1,0:T(8,128)}, f32[264,2048]{1,0:T(8,128)}, u32[]{:S(2)}, u32[]{:S(2)}) collective-permute-start(f32[264,2048]{1,0:T(8,128)} %dynamic-slice_bitcast_fusion), channel_id=1, source_target_pairs={{0,1},{1,0},{2,3},{3,2},{4,5},{5,4},{6,7},{7,6},{8,9},{9,8},{10,11... | collective-permute-start | bytes 6488072 | tf_op jit(solution)/shard_map/ppermute | solution.py:27
  112.0 7.4 %collective-permute-start.4 = (f32[256,2048]{1,0:T(8,128)}, f32[256,2048]{1,0:T(8,128)S(1)}, u32[]{:S(2)}, u32[]{:S(2)}) collective-permute-start(f32[256,2048]{1,0:T(8,128)} %get-tuple-element.353), channel_id=1, source_target_pairs={{0,1},{1,0},{2,3},{3,2},{4,5},{5,4},{6,7},{7,6},{8,9},{9,8},{10,11... | collective-permute-start | bytes 6291464 | tf_op jit(solution)/shard_map/ppermute | solution.py:27
  112.5 10.1 %collective-permute-start.3 = (f32[256,2048]{1,0:T(8,128)}, f32[256,2048]{1,0:T(8,128)S(1)}, u32[]{:S(2)}, u32[]{:S(2)}) collective-permute-start(f32[256,2048]{1,0:T(8,128)} %get-tuple-element.351), channel_id=1, source_target_pairs={{0,1},{1,0},{2,3},{3,2},{4,5},{5,4},{6,7},{7,6},{8,9},{9,8},{10,11... | collective-permute-start | bytes 6291464 | tf_op jit(solution)/shard_map/ppermute | solution.py:27
  113.7 33.6 %collective-permute-start.2 = (f32[128,2048]{1,0:T(8,128)}, f32[128,2048]{1,0:T(8,128)}, u32[]{:S(2)}, u32[]{:S(2)}) collective-permute-start(f32[128,2048]{1,0:T(8,128)} %slice.80), channel_id=1, source_target_pairs={{0,64},{64,0},{1,65},{65,1},{2,66},{66,2},{3,67},{67,3},{4,68},{68... | collective-permute-start | bytes 3145736 | tf_op jit(solution)/shard_map/ppermute | solution.py:27
  147.3 155.9 %reduce-scatter.9.cloned.1.call-start = ((), (), s32[]{:S(2)}) async-start(), calls=%async_computation.4 | async-start | bytes 17825792
  147.4 3.0 collective-permute-start.5
  147.6 4.2 %collective-permute-start.6 = (f32[128,2048]{1,0:T(8,128)}, f32[128,2048]{1,0:T(8,128)S(1)}, u32[]{:S(2)}, u32[]{:S(2)}) collective-permute-start(f32[128,2048]{1,0:T(8,128)} %collective-permute-done.2.refs_1_), channel_id=1, source_target_pairs={{0,1},{1,0},{2,3},{3,2},{4,5},{5,4},{6,7},{7,6},{8,9},{9,8},{10,11... | collective-permute-start | bytes 3145736 | tf_op jit(solution)/shard_map/ppermute | solution.py:27
  187.6 2.8 collective-permute-start.7
  190.3 6.4 %collective-permute-start.8 = (f32[32,256]{1,0:T(8,128)S(1)}, f32[32,256]{1,0:T(8,128)S(1)}, u32[]{:S(2)}, u32[]{:S(2)}) collective-permute-start(f32[32,256]{1,0:T(8,128)S(1)} %add.108), channel_id=1, source_target_pairs={{0,2},{2,0},{1,3},{3,1},{4,6},{6,4},{5,7},{7,5},{8,10},{10,8},{9,1... | collective-permute-start | bytes 98312 | tf_op jit(solution)/shard_map/ppermute | solution.py:27
  196.9 5.7 %collective-permute-start.9 = (f32[32,512]{1,0:T(8,128)S(1)}, f32[32,512]{1,0:T(8,128)S(1)}, u32[]{:S(2)}, u32[]{:S(2)}) collective-permute-start(f32[32,512]{1,0:T(8,128)S(1)} %concatenate.36), channel_id=1, source_target_pairs={{0,16},{16,0},{32,48},{48,32},{1,17},{17,1},{33,49},{49,33},{2,18}... | collective-permute-start | bytes 196616 | tf_op jit(solution)/shard_map/ppermute | solution.py:31
  202.6 7.2 %collective-permute-start.10 = (f32[32,512]{1,0:T(8,128)S(1)}, f32[32,512]{1,0:T(8,128)S(1)}, u32[]{:S(2)}, u32[]{:S(2)}) collective-permute-start(f32[32,512]{1,0:T(8,128)S(1)} %add.110), channel_id=1, source_target_pairs={{0,32},{16,48},{32,0},{48,16},{1,33},{17,49},{33,1},{49,17},{2,34}... | collective-permute-start | bytes 196616 | tf_op jit(solution)/shard_map/ppermute | solution.py:31
  209.8 5.4 %collective-permute-start.11 = (f32[32,512]{1,0:T(8,128)S(1)}, f32[32,512]{1,0:T(8,128)S(1)}, u32[]{:S(2)}, u32[]{:S(2)}) collective-permute-start(f32[32,512]{1,0:T(8,128)S(1)} %add.111), channel_id=1, source_target_pairs={{0,4},{4,0},{8,12},{12,8},{1,5},{5,1},{9,13},{13,9},{2,6},{6,2},{1... | collective-permute-start | bytes 196616 | tf_op jit(solution)/shard_map/ppermute | solution.py:31
  215.2 7.4 %collective-permute-start.12 = (f32[32,512]{1,0:T(8,128)S(1)}, f32[32,512]{1,0:T(8,128)S(1)}, u32[]{:S(2)}, u32[]{:S(2)}) collective-permute-start(f32[32,512]{1,0:T(8,128)S(1)} %add.112), channel_id=1, source_target_pairs={{0,8},{4,12},{8,0},{12,4},{1,9},{5,13},{9,1},{13,5},{2,10},{6,14},... | collective-permute-start | bytes 196616 | tf_op jit(solution)/shard_map/ppermute | solution.py:31
  222.7 3.9 %collective-permute-start.13 = (f32[1,512]{1,0:T(1,128)S(1)}, f32[1,512]{1,0:T(1,128)S(1)}, u32[]{:S(2)}, u32[]{:S(2)}) collective-permute-start(f32[1,512]{1,0:T(1,128)S(1)} %constant_dynamic-slice_fusion), channel_id=1, source_target_pairs={{0,64},{64,0},{1,65},{65,1},{2,66},{66,2},{3,67},{67,3},{4,68},{68... | collective-permute-start | bytes 6152 | tf_op jit(solution)/shard_map/ppermute | solution.py:27
  223.2 44.1 %copy-start.36 = (f32[2048]{0:T(1024)S(1)}, f32[2048]{0:T(1024)}, u32[]{:S(2)}) copy-start(f32[2048]{0:T(1024)} %param.36) | copy-start | bytes 24580
  223.2 44.1 %copy-start.37 = (f32[2048]{0:T(1024)S(1)}, f32[2048]{0:T(1024)}, u32[]{:S(2)}) copy-start(f32[2048]{0:T(1024)} %param.30) | copy-start | bytes 24580
  281.1 24.8 %collective-permute-start.15 = (f32[256,2048]{1,0:T(8,128)}, f32[256,2048]{1,0:T(8,128)}, u32[]{:S(2)}, u32[]{:S(2)}) collective-permute-start(f32[256,2048]{1,0:T(8,128)} %get-tuple-element.433), channel_id=1, source_target_pairs={{0,1},{1,0},{2,3},{3,2},{4,5},{5,4},{6,7},{7,6},{8,9},{9,8},{10,11... | collective-permute-start | bytes 6291464 | tf_op jit(solution)/shard_map/ppermute | solution.py:27
  281.1 28.1 %collective-permute-start.14 = (f32[256,2048]{1,0:T(8,128)}, f32[256,2048]{1,0:T(8,128)S(1)}, u32[]{:S(2)}, u32[]{:S(2)}) collective-permute-start(f32[256,2048]{1,0:T(8,128)} %get-tuple-element.437), channel_id=1, source_target_pairs={{0,1},{1,0},{2,3},{3,2},{4,5},{5,4},{6,7},{7,6},{8,9},{9,8},{10,11... | collective-permute-start | bytes 6291464 | tf_op jit(solution)/shard_map/ppermute | solution.py:27
  282.4 14.1 %collective-permute-start.17 = (f32[64,2048]{1,0:T(8,128)}, f32[64,2048]{1,0:T(8,128)}, u32[]{:S(2)}, u32[]{:S(2)}) collective-permute-start(f32[64,2048]{1,0:T(8,128)} %dynamic-slice_bitcast_fusion.1), channel_id=1, source_target_pairs={{0,64},{64,0},{1,65},{65,1},{2,66},{66,2},{3,67},{67,3},{4,68},{68... | collective-permute-start | bytes 1572872 | tf_op jit(solution)/shard_map/ppermute | solution.py:27
  283.7 36.5 %copy-start.38 = (f32[64]{0:T(128)}, f32[64]{0:T(128)S(1)}, u32[]{:S(2)}) copy-start(f32[64]{0:T(128)S(1)} %get-tuple-element.515) | copy-start | bytes 772
  304.3 13.3 %collective-permute-start.16 = (f32[64,2048]{1,0:T(8,128)S(1)}, f32[64,2048]{1,0:T(8,128)S(1)}, u32[]{:S(2)}, u32[]{:S(2)}) collective-permute-start(f32[64,2048]{1,0:T(8,128)S(1)} %dynamic-slice_bitcast_fusion.2), channel_id=1, source_target_pairs={{0,64},{64,0},{1,65},{65,1},{2,66},{66,2},{3,67},{67,3},{4,68},{68... | collective-permute-start | bytes 1572872 | tf_op jit(solution)/shard_map/ppermute | solution.py:27
  309.4 11.2 %copy-start.20 = (f32[512,2048]{1,0:T(8,128)}, f32[512,2048]{1,0:T(8,128)S(1)}, u32[]{:S(2)}) copy-start(f32[512,2048]{1,0:T(8,128)S(1)} %constant_dynamic-update-slice_fusion.2) | copy-start | bytes 12582916
  (30 other events, 121.6 us)
Sparse Core Ops, SparseCore 0:
  11.2 85.7 all-gather.2
  147.4 119.3 all-reduce.5
Sparse Core Ops, SparseCore 1:
  34.0 112.7 reduce-scatter.6
  187.4 115.8 reduce-scatter.8

commit v2 on v1

--- a/solution.py
+++ b/solution.py
@@ -103,15 +103,20 @@
         step(other[...])
 
 
-def cot_far_kernel(*refs):
-    cot_out, cot_turned = refs[5:]
-    for k in range(4):
-
-        @pl.when(pl.program_id(0) == k)
-        def _(k=k):
-            rows = refs[k][...]
-            cot_out[...] = rows.astype(BF16)
-            put_turned(cot_turned, rows)
+def cot_far_kernel(near, other, *refs):
+    cot_out, cot_turned = refs[1:]
+
+    def step(rows):
+        cot_out[...] = rows.astype(BF16)
+        put_turned(cot_turned, rows)
+
+    @pl.when(pl.program_id(0) < 2)
+    def _():
+        step(near[...])
+
+    @pl.when(pl.program_id(0) >= 2)
+    def _():
+        step(other[...])
 
 
 TURNED = (16, 2, 64, 2 * TOK)
@@ -122,9 +127,7 @@
     plain = pl.BlockSpec((rows, D), lambda i: (i, 0))
     shift = steps if far else 0
     turned = pl.BlockSpec((16, 2, 64, rows), lambda i: (0, 0, 0, i + shift))
-    if len(n_rows) == 4:
-        specs = [whole((rows, D))] * 4
-    elif far:
+    if far:
         picks = (lambda i: (lax.min(i, 1), 0), lambda i: (lax.max(i - 2, 0), 0))
         specs = [pl.BlockSpec((rows, D), p) for p in picks]
     else:
@@ -261,12 +264,12 @@
 def project_kernel(place, first, weight, bias, marks, inverse, queries, keys, values, *tables):
     @pl.when(pl.program_id(0) == 0)
     def _():
-        lane = lax.broadcasted_iota(jnp.int32, (TOK, 128), 1)
-        angles = as_column(marks[1:2, :]) * inverse[...]
-        sine = jnp.sin(angles)
-        tables[0][...] = jnp.where(lane < ROT, jnp.cos(angles), 1.0)
-        tables[1][...] = jnp.where((lane >= ROT // 2) & (lane < ROT), sine, 0.0)
-        tables[2][...] = jnp.where(lane < ROT // 2, -sine, 0.0)
+        angles = inverse[...] * marks[1:2, :]
+        cosine, sine = jnp.cos(angles), jnp.sin(angles)
+        none, rest = jnp.zeros_like(sine), jnp.zeros((64, TOK), F32)
+        tables[0][...] = jnp.concatenate([cosine, cosine, rest + 1.0], axis=0).T
+        tables[1][...] = jnp.concatenate([none, sine, rest], axis=0).T
+        tables[2][...] = jnp.concatenate([-sine, none, rest], axis=0).T
 
     head = pl.program_id(0) + place[0] * (2 - pl.num_programs(0))
     packed = plain_dot(first[...], weight[...]) + bias[pl.ds(head, 1), :]
@@ -276,8 +279,7 @@
 
 
 def project(place, heads, first, weight, bias, marks):
-    inverse = (10000.0 ** (-2.0 * (np.arange(128) % (ROT // 2)) / ROT)).astype(np.float32)
-    inverse = jnp.asarray(inverse.reshape(1, 128))
+    inverse = jnp.asarray((10000.0 ** (-2.0 * np.arange(32) / ROT)).astype(np.float32).reshape(32, 1))
     at = (lambda h, s: h) if heads == 2 else (lambda h, s: s[0])
     column = pl.BlockSpec((TOK, HD), lambda h, s: (0, h))
     return pl.pallas_call(
@@ -290,7 +292,7 @@
                 pl.BlockSpec((D, 3 * HD), lambda h, s: (0, at(h, s))),
                 whole((2, 3 * HD)),
                 whole((2, TOK)),
-                whole((1, 128)),
+                whole((32, 1)),
             ],
             out_specs=[column] * 3 + [pl.BlockSpec((TOK, 128), lambda h, s: (0, 0))] * 3,
         ),
@@ -511,55 +513,21 @@
     act_low, slope, down_grad = feed(second_in, cot_turned, fc1_weight, fc1_bias)
     down_sum = after(lax.psum_scatter(down_grad, ("x", "y"), scatter_dimension=0, tiled=True))
     _, cotangent, hidden_in = after((down_grad, cotangent, hidden_in))
-    cot_sent = of_core(cotangent, core).astype(F32)
-    cot_got = send(cot_sent[:128], "zl")
 
     own_marks = marks.reshape(2, TOK)
-
-    def own_step(hidden_in, cotangent, act_low, slope):
-        first_in, first_turned, second_turned = norm_call(
-            first_kernel, 256, (hidden_in,), 1, 2, params
-        )
-        projected = project(own_place, 2, first_in, qkv_weight, qkv_bias, own_marks)
-        mixed_low, grad_packed = attend(
-            own_place, 2, projected, cotangent, dense_weight, own_marks
-        )
-        grad_up = feed_back(at_side, cotangent, fc2_weight, slope)
-        branches = branch_halves(at_core, mixed_low, act_low, dense_weight, fc2_weight)
-        backs = back_halves(
-            at_core,
-            grad_packed,
-            grad_up,
-            qkv_weight,
-            fc1_weight,
-            hidden_in,
-            stats,
-            ln1_gain,
-            ln2_gain,
-        )
-        return (first_turned, second_turned, mixed_low, grad_packed, grad_up, *branches, *backs)
-
-    (
-        first_turned,
-        second_turned,
-        mixed_low,
-        grad_packed,
-        grad_up,
-        branch,
-        branch_other,
-        combined,
-        combined_other,
-        norms,
-    ) = lax.cond(core == 0, own_step, own_step, hidden_in, cotangent, act_low, slope)
-    hidden_pair, branch_other, combined_other, cot_got, cot_sent = after(
-        (hidden_pair, branch_other, combined_other, cot_got, cot_sent)
-    )
-    cot_got_too = send(cot_sent[128:], "zl")
-    branch = branch + send(branch_other, "c")
-    combined = combined + send(combined_other, "c")
+    first_in, first_turned, second_turned = norm_call(first_kernel, 256, (hidden_in,), 1, 2, params)
+    projected = project(own_place, 2, first_in, qkv_weight, qkv_bias, own_marks)
+    mixed_low, grad_packed = attend(own_place, 2, projected, cotangent, dense_weight, own_marks)
+    grad_up = feed_back(at_side, cotangent, fc2_weight, slope)
+
+    hidden_pair, mixed_low, grad_packed, grad_up, cotangent = after(
+        (hidden_pair, mixed_low, grad_packed, grad_up, cotangent)
+    )
+    cot_got = send(of_core(cotangent, core).astype(F32), "zl")
     hidden_got = lax.dynamic_index_in_dim(hidden_pair, 1 - side, 0, keepdims=False)
-
-    def far_step(hidden_got, hidden_too, first_turned, second_turned):
+    hidden_too = send(hidden_got, "c")
+
+    def beside(hidden_got, hidden_too, first_turned, second_turned, mixed_low, grad_packed, grad_up):
         first_far, second_far, first_turned, second_turned = norm_call(
             first_far_kernel,
             128,
@@ -573,32 +541,56 @@
         marks_got = hidden_got[half_rows, : 2 * TOK].reshape(2, 2, half_rows)
         marks_far = jnp.where(core == 0, marks_got, marks_got[:, ::-1]).reshape(2, TOK)
         projected_far = project(far_place, 1, first_far, qkv_weight, qkv_bias, marks_far)
-        return first_turned, second_turned, slope_side, marks_far, *projected_far
-
-    first_turned, second_turned, slope_side, marks_far, *projected_far = lax.cond(
-        core == 0,
-        far_step,
-        far_step,
-        hidden_got,
-        send(hidden_got, "c"),
+        branches = branch_halves(at_core, mixed_low, act_low, dense_weight, fc2_weight)
+        backs = back_halves(
+            at_core,
+            grad_packed,
+            grad_up,
+            qkv_weight,
+            fc1_weight,
+            hidden_in,
+            stats,
+            ln1_gain,
+            ln2_gain,
+        )
+        return first_turned, second_turned, slope_side, marks_far, *branches, *backs, *projected_far
+
+    (
         first_turned,
         second_turned,
-    )
-
-    slope_side, projected_far, cot_got_too, branch, combined = after(
-        (slope_side, projected_far, cot_got_too, branch, combined)
+        slope_side,
+        marks_far,
+        branch,
+        branch_other,
+        combined,
+        combined_other,
+        norms,
+        *projected_far,
+    ) = lax.cond(
+        core == 0,
+        beside,
+        beside,
+        hidden_got,
+        hidden_too,
+        first_turned,
+        second_turned,
+        mixed_low,
+        grad_packed,
+        grad_up,
+    )
+
+    slope_side, projected_far, cot_got, branch_other, combined_other = after(
+        (slope_side, projected_far, cot_got, branch_other, combined_other)
     )
     cot_far, cot_turned = norm_call(
         cot_far_kernel,
         128,
-        (cot_got, cot_got_too, send(cot_got, "c"), send(cot_got_too, "c")),
+        (cot_got, send(cot_got, "c")),
         1,
         1,
         (),
         (cot_turned,),
     )
-    branch = lax.psum(branch, "zh")
-    combined = lax.psum(combined, "zh")
     grad_up_far = feed_back(at_side, cot_far, fc2_weight, slope_side)
     mixed_far, grad_packed_far = attend(
         far_place, 1, projected_far, cot_far, dense_weight, marks_far
@@ -610,13 +602,14 @@
     )
     joint_grad, down_sum = after((joint_grad, down_sum))
     joint_sum = after(lax.psum_scatter(joint_grad, ("x", "y"), scatter_dimension=0, tiled=True))
-    _, norms, grad_packed, grad_up, cotangent, down_sum = after(
-        (joint_grad, norms, grad_packed, grad_up, cotangent, down_sum)
-    )
+    _, norms, grad_packed, grad_up, cotangent, down_sum, branch, combined = after(
+        (joint_grad, norms, grad_packed, grad_up, cotangent, down_sum, branch, combined)
+    )
+    branch = branch + send(branch_other, "c")
+    combined = combined + send(combined_other, "c")
+    branch_too, combined_too = send(branch, "zh"), send(combined, "zh")
 
     norms = norms[:4].reshape(4, 32, 64).transpose(1, 0, 2).reshape(32, 256)
-    norms = norms + send(norms, "c")
-    norms = norms + send(norms, "zh")
     grad_out = cotangent.astype(F32)
     bias_sum = jnp.sum(grad_out, axis=0)
     qkv_bias_sum = jnp.sum(grad_packed.astype(F32), axis=0)
@@ -639,8 +632,12 @@
     far_small = lax.dynamic_slice_in_dim(small, (1 - side) * 16 + block, 1, 0)
     small = (own_small + send(far_small, "zl")).reshape(-1)
 
-    small, branch, combined = after((small, branch, combined))
-    norms = small[:256].reshape(4, 64)
+    small, branch_too, combined_too = after((small, branch_too, combined_too))
+    branch = branch + branch_too
+    combined = combined + combined_too
+    norms = small[:256]
+    norms = norms + send(norms, "c")
+    norms = (norms + send(norms, "zh")).reshape(4, 64)
     bias_total = small[256:320]
     hidden = hidden_in.astype(F32)
     output = both_cores(of_core(hidden, core) + branch + dense_bias + fc2_bias)

time: 333 us -> 332 us (level)
  starting transfers between devices: 19.7 us -> 30.8 us
  loops' own time: 9.17 us -> 0.33 us
  Pallas kernels: 136 us -> 130 us
  waiting for transfers between devices: 93 us -> 96.9 us
    ppermute x14, waiting for transfers between devices: 31.3 us -> 74 us  [send(): return lax.ppermute(value, axis, [(i, (i + step) % n) for i in range(n)])]
    psum x1 -> x0, waiting for transfers between devices: 40.3 us -> none  [body(): branch = lax.psum(branch, 'zh')]
    ppermute x14, starting transfers between devices: 10.3 us -> 20.3 us  [send(): return lax.ppermute(value, axis, [(i, (i + step) % n) for i in range(n)])]
    another operation x2 -> x1, loops' own time: 9.17 us -> 0.33 us  [body(): lax.cond(core == 0, beside, beside, hidden_got, hidden_too, first_turned,...]
    all_gather x1, waiting for transfers between devices: 0.02 us -> 7.38 us  [body(): hidden_pair = lax.all_gather(hidden_sent, 'zl')]
    unnamed x5 -> x4, waiting for transfers between devices: 4.87 us -> 0.05 us
    unnamed x62, local copies, waits for them, and re-layouts: 12.6 us -> 9.23 us
  transfers between devices with their start and end apart: 22 -> 21, of which waited for: 13 -> 14; matrix products, arithmetic and copies ran while one was open for 11% -> 12% of each run, Pallas kernels for 41% -> 40%
where the time goes in v2:
time: 332 us; the launch traced here: 327 us
  Pallas kernels  130 us (39%)
  waiting for transfers between devices  96.9 us (29%)
  starting transfers between devices  30.8 us (9%)
  local copies, waits for them, and re-layouts  26.7 us (8%)
  other arithmetic  25.9 us (8%)
  between operations  16.1 us (5%)
    ppermute x14, waiting for transfers between devices, send(): return lax.ppermute(value, axis, [(i, (i + step) % n) for i in range(n)])  74 us
    pallas_call x2, Pallas kernels, halves_call(): pl.pallas_call(kernel, grid_spec=pltpu.PrefetchScalarGridSpec(num_scalar_...  23.3 us
    pallas_call x4, Pallas kernels, norm_call(): pl.pallas_call(kernel, grid=(steps,), in_specs=specs + [whole((1, D))] *...  21.1 us
    ppermute x14, starting transfers between devices, send(): return lax.ppermute(value, axis, [(i, (i + step) % n) for i in range(n)])  20.3 us
    pallas_call x2, Pallas kernels, feed_back(): pl.pallas_call(feed_back_kernel, grid_spec=pltpu.PrefetchScalarGridSpec(n...  16.9 us
    pallas_call x1, Pallas kernels, feed(): pl.pallas_call(feed_kernel, grid=(units // width,), in_specs=[whole((TOK,...  16.6 us
    pallas_call x1, Pallas kernels, joint(): pl.pallas_call(joint_kernel, grid_spec=pltpu.PrefetchScalarGridSpec(num_s...  15.8 us
    pallas_call x2, Pallas kernels, attend(): pl.pallas_call(attend_kernel, grid_spec=pltpu.PrefetchScalarGridSpec(num_...  15.7 us
  transfers between devices with their start and end apart: 21, of which 14 were waited for; matrix products, arithmetic and copies ran while one was open for 12% of the time, Pallas kernels for 40%

profile of v2, /device:TPU:0, one launch (start us, length us, event | category | flops | bytes accessed | tf_op | source)
XLA Modules:
  0.0 326.7 jit_solution(2559498233296610934)
XLA Ops:
  13.3 4.6 %shard_map.281 = (bf16[512,2048]{1,0:T(8,128)(2,1)}, bf16[16,2,64,1024]{3,2,1,0:T(8,128)(2,1)}, f32[512,128]{1,0:T(8,128)S(1)}) custom-call(bf16[512,2048]{1,0:T(8,128)(2,1)S(1)} %copy-done.4, bf16[512,2048]{1,0:T(8,128)(2,1)} %cot.3, f32[1,2048]{1,0:T(1,128)S(1)} %bitcast.57, f32[1,2048]{1,0:T(1,128)S(1)} %bitcast.69), custom_call_target="tpu_custom_call" | custom-call | flops 1000000 | bytes 1000000 | tf_op jit(solution)/shard_map/pallas_call | solution.py:137
  17.9 16.6 %shard_map.282 = (bf16[512,2048]{1,0:T(8,128)(2,1)}, f32[512,2048]{1,0:T(8,128)}, f32[16,128,2048]{2,1,0:T(8,128)}) custom-call(bf16[512,2048]{1,0:T(8,128)(2,1)} %get-tuple-element.259.second, bf16[16,2,64,1024]{3,2,1,0:T(8,128)(2,1)} %get-tuple-element.260.cot_turned.refs_0_, bf16[2048,2048]{1,0:T(8,128)(2,1)} %weight.4, f32[4,4,128]{2,1,0:T(4,128)S(1)} %bitcast.79), custom_call_target="tpu_custom_call" | custom-call | flops 1000000 | bytes 1000000 | tf_op jit(solution)/shard_map/pallas_call | solution.py:177
  35.9 4.0 %shard_map.283 = (bf16[512,2048]{1,0:T(8,128)(2,1)}, bf16[16,2,64,1024]{3,2,1,0:T(8,128)(2,1)}, bf16[16,2,64,1024]{3,2,1,0:T(8,128)(2,1)}) custom-call(bf16[512,2048]{1,0:T(8,128)(2,1)S(1)} %copy-done.4, f32[1,2048]{1,0:T(1,128)S(1)} %bitcast.64, f32[1,2048]{1,0:T(1,128)S(1)} %bitcast.76, f32[1,2048]{1,0:T(1,128)S(1)} %bitcast.58, f32[1,2048]{1,0:T(1,128)S(1)} %bitcast.70), custom_call_target="tpu_custom_call" | custom-call | flops 1000000 | bytes 1000000 | tf_op jit(solution)/shard_map/pallas_call | solution.py:137
  39.9 10.8 %shard_map.286.refs_3_ = bf16[512,2048]{1,0:T(8,128)(2,1)} custom-call(s32[1]{0:T(128)} %bitcast.13.side, bf16[512,2048]{1,0:T(8,128)(2,1)} %cot.3, bf16[2048,2048]{1,0:T(8,128)(2,1)} %weight.7, f32[512,2048]{1,0:T(8,128)} %get-tuple-element.273.slope), custom_call_target="tpu_custom_call" | custom-call | flops 1000000 | bytes 1000000 | tf_op jit(solution)/shard_map/pallas_call | solution.py:206
  51.2 7.7 %shard_map.284 = (bf16[512,512]{1,0:T(8,128)(2,1)}, bf16[512,512]{1,0:T(8,128)(2,1)}, bf16[512,512]{1,0:T(8,128)(2,1)}, f32[512,128]{1,0:T(8,128)}, f32[512,128]{1,0:T(8,128)}, /*index=5*/f32[512,128]{1,0:T(8,128)}) custom-call(s32[2]{0:T(128)} %broadcast_5_place.2.place, bf16[512,2048]{1,0:T(8,128)(2,1)} %get-tuple-element.263.first, ...), custom_call_target="tpu_custom_call" | custom-call | flops 1000000 | bytes 1000000 | tf_op jit(solution)/shard_map/pallas_call | solution.py:285
  58.9 8.9 %shard_map.285 = (bf16[512,512]{1,0:T(8,128)(2,1)}, bf16[512,1536]{1,0:T(8,128)(2,1)S(1)}) custom-call(s32[2]{0:T(128)} %broadcast_5_place.2.place, bf16[512,512]{1,0:T(8,128)(2,1)} %get-tuple-element.264.queries, bf16[512,512]{1,0:T(8,128)(2,1)} %get-tuple-element.265.keys, bf16[512,512]{1,0:T(8,128)(2,1)} %get-tuple-element.266.values, ...), custom_call_target="tpu_custom_call" | custom-call | flops 1000000 | bytes 1000000 | tf_op jit(solution)/shard_map/pallas_call | solution.py:339
  67.8 7.4 %all-gather.3.cloned.1.call-done = f32[528,2048]{1,0:T(8,128)} async-done(((f32[264,2048]{1,0:T(8,128)}), f32[528,2048]{1,0:T(8,128)}) %all-gather.3.cloned.1.call-update) | async-done | bytes 4325392 | tf_op jit(solution)/shard_map/all_gather | solution.py:508
  75.2 3.4 %dynamic-slice_bitcast_fusion = f32[264,2048]{1,0:T(8,128)} fusion(f32[2,264,2048]{2,1,0:T(8,128)} %bitcast.55, s32[]{:T(128)S(6)} %select_n.59), kind=kLoop, calls=%fused_computation.10 | loop fusion | bytes 4325380 | tf_op jit(solution)/shard_map/jit(dynamic_index_in_dim)/squeeze | solution.py:527
  83.2 44.5 %conditional.1 = (bf16[16,2,64,1024]{3,2,1,0:T(8,128)(2,1)}, bf16[16,2,64,1024]{3,2,1,0:T(8,128)(2,1)}, f32[512,1024]{1,0:T(8,128)}, f32[2,512]{1,0:T(2,128)S(1)...) conditional(s32[]{:T(128)} %convert_element_type.40, ...), branch_computations={%region_0.1_spmd, %region_1.2_spmd} | conditional | flops 5001025 | bytes 49118312 | solution.py:569
  84.3 7.1 %branch_1_fun.5 = (bf16[512,2048]{1,0:T(8,128)(2,1)}, bf16[512,2048]{1,0:T(8,128)(2,1)}, bf16[16,2,64,1024]{3,2,1,0:T(8,128)(2,1)}, bf16[16,2,64,1024]{3,2,1,0:T(8,128)(2,1)}) custom-call(f32[264,2048]{1,0:T(8,128)} %get-tuple-element.140.near, f32[264,2048]{1,0:T(8,128)} %get-tuple-element.141.other, ...), custom_call_target="tpu_custom_call", output_to_operand_aliasing={{2}: (6, {}), {3}: (7, {})} | custom-call | flops 1000000 | bytes 1000000 | tf_op jit(solution)/shard_map/cond/branch_1_fun/pallas_call | solution.py:137
  91.6 6.2 %branch_1_fun.9 = (bf16[512,256]{1,0:T(8,128)(2,1)}, bf16[512,256]{1,0:T(8,128)(2,1)}, bf16[512,256]{1,0:T(8,128)(2,1)}, f32[512,128]{1,0:T(8,128)}, f32[512,128]{1,0:T(8,128)}, /*index=5*/f32[512,128]{1,0:T(8,128)}) custom-call(s32[2]{0:T(128)S(1)} %get-tuple-element.170.place, bf16[512,2048]{1,0:T(8,128)(2,1)} %get-tuple-element.171.first, ...), custom_call_target="tpu_custom_call" | custom-call | flops 1000000 | bytes 1000000 | tf_op jit(solution)/shard_map/cond/branch_1_fun/pallas_call | solution.py:285
  97.8 13.8 %branch_1_fun.8 = (f32[256,2048]{1,0:T(8,128)}, f32[256,2048]{1,0:T(8,128)}, f32[8,2048]{1,0:T(8,128)S(1)}) custom-call(s32[1]{0:T(128)} %get-tuple-element.155.core, bf16[512,1536]{1,0:T(8,128)(2,1)S(1)} %get-tuple-element.162.packed, bf16[512,2048]{1,0:T(8,128)(2,1)} %get-tuple-element.163.up_grad, bf16[2048,1536]{1,0:T(8,128)(2,1)S(1)} %copy-done.1, ...), custom_call_target="tpu_custom_call" | custom-call | flops 1000000 | bytes 1000000 | tf_op jit(solution)/shard_map/cond/branch_1_fun/pallas_call | solution.py:386
  111.6 6.6 %branch_1_fun.6 = f32[512,1024]{1,0:T(8,128)} custom-call(s32[1]{0:T(128)} %get-tuple-element.150.side, bf16[512,2048]{1,0:T(8,128)(2,1)} %get-tuple-element.151.second, bf16[2048,2048]{1,0:T(8,128)(2,1)} %get-tuple-element.152.weight.up, f32[4,4,128]{2,1,0:T(4,128)S(1)} %bitcast.81), custom_call_target="tpu_custom_call" | custom-call | flops 1000000 | bytes 1000000 | tf_op jit(solution)/shard_map/cond/branch_1_fun/pallas_call | solution.py:232
  118.2 9.5 %branch_1_fun.7 = (f32[256,2048]{1,0:T(8,128)}, f32[256,2048]{1,0:T(8,128)}) custom-call(s32[1]{0:T(128)} %get-tuple-element.155.core, bf16[512,512]{1,0:T(8,128)(2,1)S(1)} %copy-done.16, bf16[512,2048]{1,0:T(8,128)(2,1)S(1)} %copy-done.14, bf16[512,2048]{1,0:T(8,128)(2,1)S(1)} %copy-done.10, bf16[2048,2048]{1,0:T(8,128)(2,1)} %get-tuple-element.159.down), custom_call_target="tpu_custom_call" | custom-call | flops 1000000 | bytes 1000000 | tf_op jit(solution)/shard_map/cond/branch_1_fun/pallas_call | solution.py:386
  128.5 8.5 %collective-permute-start.2 = (f32[256,2048]{1,0:T(8,128)}, f32[256,2048]{1,0:T(8,128)S(1)}, u32[]{:S(2)}, u32[]{:S(2)}) collective-permute-start(f32[256,2048]{1,0:T(8,128)} %collective-permute-done.1.near), channel_id=1, source_target_pairs={{0,1},{1,0},{2,3},{3,2},{4,5},{5,4},{6,7},{7,6},{8,9},{9,8},{10,11... | collective-permute-start | bytes 6291464 | tf_op jit(solution)/shard_map/ppermute | solution.py:27
  137.1 4.4 %collective-permute-done.2.other = f32[256,2048]{1,0:T(8,128)S(1)} collective-permute-done((f32[256,2048]{1,0:T(8,128)}, f32[256,2048]{1,0:T(8,128)S(1)}, u32[]{:S(2)}, u32[]{:S(2)}) %collective-permute-start.2) | collective-permute-done | bytes 2097184 | tf_op jit(solution)/shard_map/ppermute | solution.py:27
  142.8 5.4 %shard_map.287 = (bf16[512,2048]{1,0:T(8,128)(2,1)}, bf16[16,2,64,1024]{3,2,1,0:T(8,128)(2,1)}) custom-call(f32[256,2048]{1,0:T(8,128)} %collective-permute-done.1.near, f32[256,2048]{1,0:T(8,128)} %copy-done.21, bf16[16,2,64,1024]{3,2,1,0:T(8,128)(2,1)} %get-tuple-element.260.cot_turned.refs_0_), custom_call_target="tpu_custom_call", output_to_operand_aliasing={{1}: (2, {})} | custom-call | flops 1000000 | bytes 1000000 | tf_op jit(solution)/shard_map/pallas_call | solution.py:137
  148.2 6.1 %shard_map.288.refs_4_ = bf16[512,1024]{1,0:T(8,128)(2,1)} custom-call(s32[1]{0:T(128)} %bitcast.13.side, bf16[512,2048]{1,0:T(8,128)(2,1)} %get-tuple-element.296.cot, bf16[2048,2048]{1,0:T(8,128)(2,1)} %weight.7, f32[512,1024]{1,0:T(8,128)} %get-tuple-element.297.slope), custom_call_target="tpu_custom_call" | custom-call | flops 1000000 | bytes 1000000 | tf_op jit(solution)/shard_map/pallas_call | solution.py:206
  154.3 6.8 %shard_map.289 = (bf16[512,256]{1,0:T(8,128)(2,1)}, bf16[512,768]{1,0:T(8,128)(2,1)}) custom-call(s32[2]{0:T(128)S(1)} %pad_add_fusion.place, bf16[512,256]{1,0:T(8,128)(2,1)} %get-tuple-element.298.queries, bf16[512,256]{1,0:T(8,128)(2,1)} %get-tuple-element.299.keys, bf16[512,256]{1,0:T(8,128)(2,1)} %get-tuple-element.300.values, ...), custom_call_target="tpu_custom_call" | custom-call | flops 1000000 | bytes 1000000 | tf_op jit(solution)/shard_map/pallas_call | solution.py:339
  161.1 15.8 %shard_map.290 = f32[16,128,2048]{2,1,0:T(8,128)} custom-call(s32[1]{0:T(128)} %bitcast.13.side, bf16[16,2,64,1024]{3,2,1,0:T(8,128)(2,1)} %get-tuple-element.282.refs_0_, bf16[16,2,64,1024]{3,2,1,0:T(8,128)(2,1)} %get-tuple-element.294.refs_1_, bf16[16,2,64,1024]{3,2,1,0:T(8,128)(2,1)S(1)} %copy-done.8, bf16[512,2048]{1,0:T(8,128)(2,1)S(1)} %copy-done.6, ...), custom_call_target="tpu_custom_call" | custom-call | flops 1000000 | bytes 1000000 | tf_op jit(solution)/shard_map/pallas_call | solution.py:452
  177.6 3.9 %collective-permute-done.3 = f32[256,2048]{1,0:T(8,128)S(1)} collective-permute-done((f32[256,2048]{1,0:T(8,128)}, f32[256,2048]{1,0:T(8,128)S(1)}, u32[]{:S(2)}, u32[]{:S(2)}) %collective-permute-start.3) | collective-permute-done | bytes 2097184 | tf_op jit(solution)/shard_map/ppermute | solution.py:27
  181.4 3.2 add.108
  187.5 3.4 %add.119 = f32[256,2048]{1,0:T(8,128)} add(f32[256,2048]{1,0:T(8,128)} %get-tuple-element.318, f32[256,2048]{1,0:T(8,128)S(1)} %collective-permute-done.10) | non-fusion elementwise | flops 524288 | bytes 6291456 | tf_op jit(solution)/shard_map/add | solution.py:609
  197.1 4.3 %collective-permute-done.4 = f32[32,512]{1,0:T(8,128)S(1)} collective-permute-done((f32[32,512]{1,0:T(8,128)S(1)}, f32[32,512]{1,0:T(8,128)S(1)}, u32[]{:S(2)}, u32[]{:S(2)}) %collective-permute-start.4) | collective-permute-done | bytes 65568 | tf_op jit(solution)/shard_map/ppermute | solution.py:31
  204.6 4.2 %collective-permute-done.5 = f32[32,512]{1,0:T(8,128)S(1)} collective-permute-done((f32[32,512]{1,0:T(8,128)S(1)}, f32[32,512]{1,0:T(8,128)S(1)}, u32[]{:S(2)}, u32[]{:S(2)}) %collective-permute-start.5) | collective-permute-done | bytes 65568 | tf_op jit(solution)/shard_map/ppermute | solution.py:31
  210.6 3.4 %collective-permute-done.6 = f32[32,512]{1,0:T(8,128)S(1)} collective-permute-done((f32[32,512]{1,0:T(8,128)S(1)}, f32[32,512]{1,0:T(8,128)S(1)}, u32[]{:S(2)}, u32[]{:S(2)}) %collective-permute-start.6) | collective-permute-done | bytes 65568 | tf_op jit(solution)/shard_map/ppermute | solution.py:31
  214.0 3.8 %collective-permute-start.7 = (f32[32,512]{1,0:T(8,128)S(1)}, f32[32,512]{1,0:T(8,128)S(1)}, u32[]{:S(2)}, u32[]{:S(2)}) collective-permute-start(f32[32,512]{1,0:T(8,128)S(1)} %add.111), channel_id=1, source_target_pairs={{0,8},{4,12},{8,0},{12,4},{1,9},{5,13},{9,1},{13,5},{2,10},{6,14},... | collective-permute-start | bytes 196616 | tf_op jit(solution)/shard_map/ppermute | solution.py:31
  218.1 3.6 %collective-permute-done.7 = f32[32,512]{1,0:T(8,128)S(1)} collective-permute-done((f32[32,512]{1,0:T(8,128)S(1)}, f32[32,512]{1,0:T(8,128)S(1)}, u32[]{:S(2)}, u32[]{:S(2)}) %collective-permute-start.7) | collective-permute-done | bytes 65568 | tf_op jit(solution)/shard_map/ppermute | solution.py:31
  226.5 52.8 %collective-permute-done.8 = f32[1,512]{1,0:T(1,128)S(1)} collective-permute-done((f32[1,512]{1,0:T(1,128)S(1)}, f32[1,512]{1,0:T(1,128)S(1)}, u32[]{:S(2)}, u32[]{:S(2)}) %collective-permute-start.8) | collective-permute-done | bytes 2080 | tf_op jit(solution)/shard_map/ppermute | solution.py:27
  281.5 4.6 %fusion.11 = (f32[256]{0:T(256)S(1)}, f32[256]{0:T(256)S(1)}, f32[256,2048]{1,0:T(8,128)S(1)}, f32[512,2048]{1,0:T(8,128)S(1)}, f32[256,2048]{1,0:T(8,128)S(1)}) fusion(f32[256]{0:T(256)S(1)} %get-tuple-element.368, f32[256]{0:T(256)S(1)} %get-tuple-element.369, bf16[512,2048]{1,0:T(8,128)(2,1)S(1)} %copy-done.5, s32[]{:T(128)S(6)} %select_n.58, ...), kind=kLoop, calls=%fused_computation.48 | loop fusion | flops 5766656 | bytes 15749124 | tf_op jit(solution)/shard_map/reduce_sum | solution.py:649
  304.2 3.3 %constant_dynamic-update-slice_fusion.2 = f32[512,2048]{1,0:T(8,128)} fusion(f32[512,2048]{1,0:T(8,128)} %copy-done.20, f32[256,2048]{1,0:T(8,128)} %collective-permute-done.12, s32[]{:T(128)S(6)} %select_n.62), kind=kLoop, calls=%fused_computation.39 | loop fusion | bytes 4194308 | tf_op jit(solution)/shard_map/dynamic_update_slice | solution.py:502
  309.4 6.7 %collective-permute-done.16 = f32[64,2048]{1,0:T(8,128)S(1)} collective-permute-done((f32[64,2048]{1,0:T(8,128)S(1)}, f32[64,2048]{1,0:T(8,128)S(1)}, u32[]{:S(2)}, u32[]{:S(2)}) %collective-permute-start.16) | collective-permute-done | bytes 524320 | tf_op jit(solution)/shard_map/ppermute | solution.py:27
  (172 shorter events, 59.5 us)
Async XLA Ops:
  8.0 67.2 %all-gather.3.cloned.1.call-start = ((), (), s32[]{:S(2)}) async-start(), calls=%async_computation.2 | async-start | bytes 6488064 | tf_op jit(solution)/shard_map/all_gather | solution.py:508
  11.7 165.2 %reduce-scatter.7.cloned.1.call-start = ((), (), s32[]{:S(2)}) async-start(), calls=%async_computation.3 | async-start | bytes 17825792
  34.6 267.1 %reduce-scatter.9.cloned.1.call-start = ((), (), s32[]{:S(2)}) async-start(), calls=%async_computation.4 | async-start | bytes 17825792
  39.9 11.3 %slice-start = ((s8[6291456]{0:T(1024)(128)(4,1)}), s8[4194304]{0:T(1024)(128)(4,1)S(1)}, s32[]{:S(2)}) async-start(s8[6291456]{0:T(1024)(128)(4,1)} %bitcast.53), calls=%async_computation.5 | async-start | bytes 8388608
  39.9 11.3 %slice-start.1 = ((s8[6291456]{0:T(1024)(128)(4,1)}), s8[2097152]{0:T(1024)(128)(4,1)S(1)}, s32[]{:S(2)}) async-start(s8[6291456]{0:T(1024)(128)(4,1)} %bitcast.53), calls=%async_computation.6 | async-start | bytes 4194304
  39.9 11.3 %copy-start.26 = (f32[32,1]{1,0:T(8,128)S(1)}, f32[32,1]{1,0:T(8,128)}, u32[]{:S(2)}) copy-start(f32[32,1]{1,0:T(8,128)} %constant.61.clone.inverse) | copy-start | bytes 388
  39.9 11.3 %copy-start.32 = (f32[2,768]{1,0:T(2,128)S(1)}, f32[2,768]{1,0:T(2,128)}, u32[]{:S(2)}) copy-start(f32[2,768]{1,0:T(2,128)} %bias.1) | copy-start | bytes 18436
  67.8 15.4 %copy-start.11 = (bf16[512,1536]{1,0:T(8,128)(2,1)}, bf16[512,1536]{1,0:T(8,128)(2,1)S(1)}, u32[]{:S(2)}) copy-start(bf16[512,1536]{1,0:T(8,128)(2,1)S(1)} %get-tuple-element.316.refs_7_) | copy-start | bytes 4718596
  78.6 4.6 %collective-permute-start = (f32[264,2048]{1,0:T(8,128)}, f32[264,2048]{1,0:T(8,128)}, u32[]{:S(2)}, u32[]{:S(2)}) collective-permute-start(f32[264,2048]{1,0:T(8,128)} %dynamic-slice_bitcast_fusion), channel_id=1, source_target_pairs={{0,1},{1,0},{2,3},{3,2},{4,5},{5,4},{6,7},{7,6},{8,9},{9,8},{10,11... | collective-permute-start | bytes 6488072 | tf_op jit(solution)/shard_map/ppermute | solution.py:27
  80.2 48.4 %collective-permute-start.1 = (f32[256,2048]{1,0:T(8,128)}, f32[256,2048]{1,0:T(8,128)}, u32[]{:S(2)}, u32[]{:S(2)}) collective-permute-start(f32[256,2048]{1,0:T(8,128)} %dynamic-slice_convert_fusion), channel_id=1, source_target_pairs={{0,64},{64,0},{1,65},{65,1},{2,66},{66,2},{3,67},{67,3},{4,68},{68... | collective-permute-start | bytes 6291464 | tf_op jit(solution)/shard_map/ppermute | solution.py:27
  118.2 9.5 %copy-start.31 = (f32[1,2,2,256]{3,1,2,0:T(2,128)S(1)}, f32[1,2,2,256]{3,1,2,0:T(2,128)}, u32[]{:S(2)}) copy-start(f32[1,2,2,256]{3,1,2,0:T(2,128)} %copy-done.30) | copy-start | bytes 12292 | tf_op jit(solution)/shard_map/cond
  128.5 12.9 %collective-permute-start.2 = (f32[256,2048]{1,0:T(8,128)}, f32[256,2048]{1,0:T(8,128)S(1)}, u32[]{:S(2)}, u32[]{:S(2)}) collective-permute-start(f32[256,2048]{1,0:T(8,128)} %collective-permute-done.1.near), channel_id=1, source_target_pairs={{0,1},{1,0},{2,3},{3,2},{4,5},{5,4},{6,7},{7,6},{8,9},{9,8},{10,11... | collective-permute-start | bytes 6291464 | tf_op jit(solution)/shard_map/ppermute | solution.py:27
  148.2 12.9 %copy-start.8 = (bf16[16,2,64,1024]{3,2,1,0:T(8,128)(2,1)S(1)}, bf16[16,2,64,1024]{3,2,1,0:T(8,128)(2,1)}, u32[]{:S(2)}) copy-start(bf16[16,2,64,1024]{3,2,1,0:T(8,128)(2,1)} %get-tuple-element.295.refs_2_) | copy-start | bytes 12582916
  177.0 4.5 %collective-permute-start.3 = (f32[256,2048]{1,0:T(8,128)}, f32[256,2048]{1,0:T(8,128)S(1)}, u32[]{:S(2)}, u32[]{:S(2)}) collective-permute-start(f32[256,2048]{1,0:T(8,128)} %get-tuple-element.313), channel_id=1, source_target_pairs={{0,1},{1,0},{2,3},{3,2},{4,5},{5,4},{6,7},{7,6},{8,9},{9,8},{10,11... | collective-permute-start | bytes 6291464 | tf_op jit(solution)/shard_map/ppermute | solution.py:27
  177.2 10.3 %collective-permute-start.10 = (f32[256,2048]{1,0:T(8,128)}, f32[256,2048]{1,0:T(8,128)S(1)}, u32[]{:S(2)}, u32[]{:S(2)}) collective-permute-start(f32[256,2048]{1,0:T(8,128)} %get-tuple-element.319), channel_id=1, source_target_pairs={{0,1},{1,0},{2,3},{3,2},{4,5},{5,4},{6,7},{7,6},{8,9},{9,8},{10,11... | collective-permute-start | bytes 6291464 | tf_op jit(solution)/shard_map/ppermute | solution.py:27
  184.6 7.1 %copy-start.7 = (bf16[512,2048]{1,0:T(8,128)(2,1)S(1)}, bf16[512,2048]{1,0:T(8,128)(2,1)}, u32[]{:S(2)}) copy-start(bf16[512,2048]{1,0:T(8,128)(2,1)} %shard_map.286.refs_3_) | copy-start | bytes 6291460
  184.6 94.7 %collective-permute-start.9 = (f32[256,2048]{1,0:T(8,128)}, f32[256,2048]{1,0:T(8,128)}, u32[]{:S(2)}, u32[]{:S(2)}) collective-permute-start(f32[256,2048]{1,0:T(8,128)} %add.108), channel_id=1, source_target_pairs={{0,2},{2,0},{1,3},{3,1},{4,6},{6,4},{5,7},{7,5},{8,10},{10,8},{9,1... | collective-permute-start | bytes 6291464 | tf_op jit(solution)/shard_map/ppermute | solution.py:27
  190.9 89.0 %collective-permute-start.11 = (f32[256,2048]{1,0:T(8,128)}, f32[256,2048]{1,0:T(8,128)}, u32[]{:S(2)}, u32[]{:S(2)}) collective-permute-start(f32[256,2048]{1,0:T(8,128)} %add.119), channel_id=1, source_target_pairs={{0,2},{2,0},{1,3},{3,1},{4,6},{6,4},{5,7},{7,5},{8,10},{10,8},{9,1... | collective-permute-start | bytes 6291464 | tf_op jit(solution)/shard_map/ppermute | solution.py:27
  195.4 6.0 %collective-permute-start.4 = (f32[32,512]{1,0:T(8,128)S(1)}, f32[32,512]{1,0:T(8,128)S(1)}, u32[]{:S(2)}, u32[]{:S(2)}) collective-permute-start(f32[32,512]{1,0:T(8,128)S(1)} %concatenate.36), channel_id=1, source_target_pairs={{0,16},{16,0},{32,48},{48,32},{1,17},{17,1},{33,49},{49,33},{2,18}... | collective-permute-start | bytes 196616 | tf_op jit(solution)/shard_map/ppermute | solution.py:31
  201.4 7.4 %collective-permute-start.5 = (f32[32,512]{1,0:T(8,128)S(1)}, f32[32,512]{1,0:T(8,128)S(1)}, u32[]{:S(2)}, u32[]{:S(2)}) collective-permute-start(f32[32,512]{1,0:T(8,128)S(1)} %add.109), channel_id=1, source_target_pairs={{0,32},{16,48},{32,0},{48,16},{1,33},{17,49},{33,1},{49,17},{2,34}... | collective-permute-start | bytes 196616 | tf_op jit(solution)/shard_map/ppermute | solution.py:31
  208.8 5.1 %collective-permute-start.6 = (f32[32,512]{1,0:T(8,128)S(1)}, f32[32,512]{1,0:T(8,128)S(1)}, u32[]{:S(2)}, u32[]{:S(2)}) collective-permute-start(f32[32,512]{1,0:T(8,128)S(1)} %add.110), channel_id=1, source_target_pairs={{0,4},{4,0},{8,12},{12,8},{1,5},{5,1},{9,13},{13,9},{2,6},{6,2},{1... | collective-permute-start | bytes 196616 | tf_op jit(solution)/shard_map/ppermute | solution.py:31
  214.0 7.7 %collective-permute-start.7 = (f32[32,512]{1,0:T(8,128)S(1)}, f32[32,512]{1,0:T(8,128)S(1)}, u32[]{:S(2)}, u32[]{:S(2)}) collective-permute-start(f32[32,512]{1,0:T(8,128)S(1)} %add.111), channel_id=1, source_target_pairs={{0,8},{4,12},{8,0},{12,4},{1,9},{5,13},{9,1},{13,5},{2,10},{6,14},... | collective-permute-start | bytes 196616 | tf_op jit(solution)/shard_map/ppermute | solution.py:31
  221.7 57.6 %collective-permute-start.8 = (f32[1,512]{1,0:T(1,128)S(1)}, f32[1,512]{1,0:T(1,128)S(1)}, u32[]{:S(2)}, u32[]{:S(2)}) collective-permute-start(f32[1,512]{1,0:T(1,128)S(1)} %constant_dynamic-slice_fusion), channel_id=1, source_target_pairs={{0,64},{64,0},{1,65},{65,1},{2,66},{66,2},{3,67},{67,3},{4,68},{68... | collective-permute-start | bytes 6152 | tf_op jit(solution)/shard_map/ppermute | solution.py:27
  225.0 67.8 %collective-permute-start.17 = (f32[64,2048]{1,0:T(8,128)}, f32[64,2048]{1,0:T(8,128)}, u32[]{:S(2)}, u32[]{:S(2)}) collective-permute-start(f32[64,2048]{1,0:T(8,128)} %dynamic-slice_bitcast_fusion.1), channel_id=1, source_target_pairs={{0,64},{64,0},{1,65},{65,1},{2,66},{66,2},{3,67},{67,3},{4,68},{68... | collective-permute-start | bytes 1572872 | tf_op jit(solution)/shard_map/ppermute | solution.py:27
  286.1 18.0 %collective-permute-start.12 = (f32[256,2048]{1,0:T(8,128)S(1)}, f32[256,2048]{1,0:T(8,128)}, u32[]{:S(2)}, u32[]{:S(2)}) collective-permute-start(f32[256,2048]{1,0:T(8,128)S(1)} %get-tuple-element.376), channel_id=1, source_target_pairs={{0,1},{1,0},{2,3},{3,2},{4,5},{5,4},{6,7},{7,6},{8,9},{9,8},{10,11... | collective-permute-start | bytes 6291464 | tf_op jit(solution)/shard_map/ppermute | solution.py:27
  292.2 15.2 %collective-permute-start.13 = (f32[256,2048]{1,0:T(8,128)}, f32[256,2048]{1,0:T(8,128)}, u32[]{:S(2)}, u32[]{:S(2)}) collective-permute-start(f32[256,2048]{1,0:T(8,128)} %get-tuple-element.371), channel_id=1, source_target_pairs={{0,1},{1,0},{2,3},{3,2},{4,5},{5,4},{6,7},{7,6},{8,9},{9,8},{10,11... | collective-permute-start | bytes 6291464 | tf_op jit(solution)/shard_map/ppermute | solution.py:27
  292.2 3.8 %collective-permute-start.14 = (f32[256]{0:T(256)S(1)}, f32[256]{0:T(256)S(1)}, u32[]{:S(2)}, u32[]{:S(2)}) collective-permute-start(f32[256]{0:T(256)S(1)} %slice.74), channel_id=1, source_target_pairs={{0,1},{1,0},{2,3},{3,2},{4,5},{5,4},{6,7},{7,6},{8,9},{9,8},{10,11... | collective-permute-start | bytes 3080 | tf_op jit(solution)/shard_map/ppermute | solution.py:27
  296.0 5.1 %collective-permute-start.15 = (f32[256]{0:T(256)S(1)}, f32[256]{0:T(256)S(1)}, u32[]{:S(2)}, u32[]{:S(2)}) collective-permute-start(f32[256]{0:T(256)S(1)} %slice_add_fusion), channel_id=1, source_target_pairs={{0,2},{2,0},{1,3},{3,1},{4,6},{6,4},{5,7},{7,5},{8,10},{10,8},{9,1... | collective-permute-start | bytes 3080 | tf_op jit(solution)/shard_map/ppermute | solution.py:27
  298.9 19.6 %copy-start.37 = (f32[64]{0:T(128)}, f32[64]{0:T(128)S(1)}, u32[]{:S(2)}) copy-start(f32[64]{0:T(128)S(1)} %get-tuple-element.444) | copy-start | bytes 772
  302.8 13.3 %collective-permute-start.16 = (f32[64,2048]{1,0:T(8,128)S(1)}, f32[64,2048]{1,0:T(8,128)S(1)}, u32[]{:S(2)}, u32[]{:S(2)}) collective-permute-start(f32[64,2048]{1,0:T(8,128)S(1)} %dynamic-slice_bitcast_fusion.2), channel_id=1, source_target_pairs={{0,64},{64,0},{1,65},{65,1},{2,66},{66,2},{3,67},{67,3},{4,68},{68... | collective-permute-start | bytes 1572872 | tf_op jit(solution)/shard_map/ppermute | solution.py:27
  307.5 8.6 %copy-start.23 = (f32[1,128,2048]{2,1,0:T(8,128)S(1)}, f32[1,128,2048]{2,1,0:T(8,128)}, u32[]{:S(2)}) copy-start(f32[1,128,2048]{2,1,0:T(8,128)} %reduce-scatter.9.cloned.1.call-done) | copy-start | bytes 3145732
  309.3 9.7 %copy-start.19 = (f32[512,2048]{1,0:T(8,128)}, f32[512,2048]{1,0:T(8,128)S(1)}, u32[]{:S(2)}) copy-start(f32[512,2048]{1,0:T(8,128)S(1)} %constant_dynamic-update-slice_fusion) | copy-start | bytes 12582916
  (25 other events, 88.0 us)
Sparse Core Ops, SparseCore 0:
  11.9 63.2 all-gather.2
Sparse Core Ops, SparseCore 1:
  34.7 112.8 reduce-scatter.6
  177.0 115.0 reduce-scatter.8

commit v3 on v2

--- a/solution.py
+++ b/solution.py
@@ -93,22 +93,6 @@
         second_out[...] = second.astype(BF16)
         put_turned(first_turned, first)
         put_turned(second_turned, second)
-
-    @pl.when(pl.program_id(0) < 2)
-    def _():
-        step(near[...])
-
-    @pl.when(pl.program_id(0) >= 2)
-    def _():
-        step(other[...])
-
-
-def cot_far_kernel(near, other, *refs):
-    cot_out, cot_turned = refs[1:]
-
-    def step(rows):
-        cot_out[...] = rows.astype(BF16)
-        put_turned(cot_turned, rows)
 
     @pl.when(pl.program_id(0) < 2)
     def _():
@@ -194,31 +178,82 @@
     )(second, cot_turned, weight, bias.reshape(-1, width // 128, 128))
 
 
-def feed_back_kernel(side, cot, weight, slope, up_grad):
+def feed_back_kernel(cot, weight, slope, dense, up_grad, grad_mixed):
     up_grad[...] = (contract_cols(cot[...], weight[...]) * slope[...]).astype(BF16)
 
-
-def feed_back(side, cot, weight, slope):
+    @pl.when(pl.program_id(0) == 0)
+    def _():
+        grad_mixed[...] = contract_cols(cot[...], dense[...]).astype(BF16)
+
+
+def feed_back(cot, weight, slope, dense):
     units, width = slope.shape[1], 512
-    steps = units // width
-    far = units < weight.shape[0]
-    column = pl.BlockSpec((TOK, width), lambda j, s: (0, j))
+    column = pl.BlockSpec((TOK, width), lambda j: (0, j))
+    mixed = dense.shape[0]
     return pl.pallas_call(
         feed_back_kernel,
+        grid=(units // width,),
+        in_specs=[
+            whole((TOK, D)),
+            pl.BlockSpec((width, D), lambda j: (j, 0)),
+            column,
+            whole(dense.shape),
+        ],
+        out_specs=[column, pl.BlockSpec((TOK, mixed), lambda j: (0, 0))],
+        out_shape=[
+            jax.ShapeDtypeStruct((TOK, units), BF16),
+            jax.ShapeDtypeStruct((TOK, mixed), BF16),
+        ],
+        compiler_params=pltpu.CompilerParams(vmem_limit_bytes=VMEM),
+        cost_estimate=COST,
+    )(cot, weight, slope, dense)
+
+
+def cot_far_kernel(n, side, rows, weight, slope, dense, *refs):
+    up_grad, grad_mixed, cot_turned, low = refs[n:]
+
+    @pl.when(pl.program_id(0) == 0)
+    def _():
+        low[...] = rows[...].astype(BF16)
+        put_turned(cot_turned, rows[...])
+        grad_mixed[...] = contract_cols(low[...], dense[...]).astype(BF16)
+
+    up_grad[...] = (contract_cols(low[...], weight[...]) * slope[...]).astype(BF16)
+
+
+def cot_far_half(k, side, rows, weight, slope, dense, held):
+    half, width = TOK // 2, 256
+    steps = slope.shape[1] // width
+    first = len(held) == 1
+    shapes = [
+        jax.ShapeDtypeStruct((TOK, slope.shape[1]), BF16),
+        jax.ShapeDtypeStruct((TOK, HD), BF16),
+        jax.ShapeDtypeStruct(TURNED, BF16),
+    ]
+    return pl.pallas_call(
+        partial(cot_far_kernel, len(held)),
         grid_spec=pltpu.PrefetchScalarGridSpec(
             num_scalar_prefetch=1,
             grid=(steps,),
             in_specs=[
-                whole((TOK, D)),
-                pl.BlockSpec((width, D), lambda j, s: (s[0] * steps * far + j, 0)),
-                column,
+                whole((half, D)),
+                pl.BlockSpec((width, D), lambda j, s: (s[0] * steps + j, 0)),
+                pl.BlockSpec((half, width), lambda j, s: (k, j)),
+                pl.BlockSpec((HD, D), lambda j, s: (s[0], 0)),
+            ]
+            + [pl.BlockSpec(memory_space=pl.ANY)] * len(held),
+            out_specs=[
+                pl.BlockSpec((half, width), lambda j, s: (k, j)),
+                pl.BlockSpec((half, HD), lambda j, s: (k, 0)),
+                pl.BlockSpec((16, 2, 64, half), lambda j, s: (0, 0, 0, 2 + k)),
             ],
-            out_specs=column,
+            scratch_shapes=[pltpu.VMEM((half, D), BF16)],
         ),
-        out_shape=jax.ShapeDtypeStruct((TOK, units), BF16),
-        compiler_params=pltpu.CompilerParams(vmem_limit_bytes=VMEM),
-        cost_estimate=COST,
-    )(side, cot, weight, slope)
+        out_shape=shapes,
+        input_output_aliases={5: 2} if first else {5: 0, 6: 1, 7: 2},
+        compiler_params=pltpu.CompilerParams(vmem_limit_bytes=VMEM),
+        cost_estimate=COST,
+    )(side, rows, weight, slope, dense, *held)
 
 
 def slope_far_kernel(side, second, weight, bias, slope):
@@ -261,11 +296,28 @@
     return jnp.broadcast_to(row, (8, row.shape[1])).T[:, 0:1]
 
 
+def cosine_and_sine(angles):
+    turns = jnp.floor(angles * (2.0 / math.pi) + 0.5)
+    rest = ((angles - turns * 1.5703125) - turns * 4.837512969970703e-4) - turns * 7.549789954891882e-8
+    square = rest * rest
+    sine = ((-1.9515295891e-4 * square + 8.3321608736e-3) * square - 1.6666654611e-1) * square
+    sine = sine * rest + rest
+    cosine = (2.443315711809948e-5 * square - 1.388731625493765e-3) * square + 4.166664568298827e-2
+    cosine = cosine * (square * square) - 0.5 * square + 1.0
+    quarter = turns.astype(jnp.int32) & 3
+    odd = (quarter & 1) == 1
+    flipped = jnp.where(odd, sine, cosine), jnp.where(odd, cosine, sine)
+    return (
+        jnp.where((quarter == 1) | (quarter == 2), -flipped[0], flipped[0]),
+        jnp.where(quarter >= 2, -flipped[1], flipped[1]),
+    )
+
+
 def project_kernel(place, first, weight, bias, marks, inverse, queries, keys, values, *tables):
     @pl.when(pl.program_id(0) == 0)
     def _():
         angles = inverse[...] * marks[1:2, :]
-        cosine, sine = jnp.cos(angles), jnp.sin(angles)
+        cosine, sine = cosine_and_sine(angles)
         none, rest = jnp.zeros_like(sine), jnp.zeros((64, TOK), F32)
         tables[0][...] = jnp.concatenate([cosine, cosine, rest + 1.0], axis=0).T
         tables[1][...] = jnp.concatenate([none, sine, rest], axis=0).T
@@ -304,7 +356,7 @@
 
 
 def attend_kernel(
-    place, queries, keys, values, cosine, rising, falling, cot, dense, marks, mixed_out, grad_out
+    place, queries, keys, values, cosine, rising, falling, grad_mixed, marks, mixed_out, grad_out
 ):
     tables = (cosine, rising, falling)
     scale = 1.0 / math.sqrt(HD)
@@ -321,20 +373,18 @@
     probs = weights / jnp.sum(weights, axis=-1, keepdims=True)
     probs_low = probs.astype(BF16)
     mixed_out[...] = plain_dot(probs_low, values).astype(BF16)
-    grad_mixed = contract_cols(cot[...], dense[...]).astype(BF16)
-    grad_probs = contract_cols(grad_mixed, values)
+    grad_probs = contract_cols(grad_mixed[...], values)
     along = jnp.sum(probs * grad_probs, axis=-1, keepdims=True)
     grad_scores = (probs * (grad_probs - along)).astype(BF16)
     grad_query = plain_dot(grad_scores, keys) * scale
     grad_key = plain_dot(grad_scores.T, queries) * scale
-    grad_value = plain_dot(probs_low.T, grad_mixed)
+    grad_value = plain_dot(probs_low.T, grad_mixed[...])
     grad_out[:, :HD] = turn(grad_query, tables, -1.0).astype(BF16)
     grad_out[:, HD : 2 * HD] = turn(grad_key, tables, -1.0).astype(BF16)
     grad_out[:, 2 * HD :] = grad_value.astype(BF16)
 
 
-def attend(place, heads, projected, cot, dense, marks):
-    at = (lambda h, s: h) if heads == 2 else (lambda h, s: s[0])
+def attend(place, heads, projected, grad_mixed, marks):
     column = pl.BlockSpec((TOK, HD), lambda h, s: (0, h))
     return pl.pallas_call(
         attend_kernel,
@@ -343,7 +393,7 @@
             grid=(heads,),
             in_specs=[column] * 3
             + [whole((TOK, 128))] * 3
-            + [whole((TOK, D)), pl.BlockSpec((HD, D), lambda h, s: (at(h, s), 0)), whole((2, TOK))],
+            + [column, whole((2, TOK))],
             out_specs=[column, pl.BlockSpec((TOK, 3 * HD), lambda h, s: (0, h))],
         ),
         out_shape=[
@@ -352,7 +402,7 @@
         ],
         compiler_params=pltpu.CompilerParams(vmem_limit_bytes=VMEM),
         cost_estimate=COST,
-    )(place, *projected, cot, dense, marks)
+    )(place, *projected, grad_mixed, marks)
 
 
 def put_halves(core, values, scratch, mine, other):
@@ -517,17 +567,21 @@
     own_marks = marks.reshape(2, TOK)
     first_in, first_turned, second_turned = norm_call(first_kernel, 256, (hidden_in,), 1, 2, params)
     projected = project(own_place, 2, first_in, qkv_weight, qkv_bias, own_marks)
-    mixed_low, grad_packed = attend(own_place, 2, projected, cotangent, dense_weight, own_marks)
-    grad_up = feed_back(at_side, cotangent, fc2_weight, slope)
-
-    hidden_pair, mixed_low, grad_packed, grad_up, cotangent = after(
-        (hidden_pair, mixed_low, grad_packed, grad_up, cotangent)
-    )
-    cot_got = send(of_core(cotangent, core).astype(F32), "zl")
+    grad_up, grad_mixed = feed_back(cotangent, fc2_weight, slope, dense_weight)
+    mixed_low, grad_packed = attend(own_place, 2, projected, grad_mixed, own_marks)
+    branch, branch_other = branch_halves(at_core, mixed_low, act_low, dense_weight, fc2_weight)
+    cot_sent = of_core(cotangent, core).astype(F32)
+
+    hidden_pair, branch_other, cot_sent, grad_up = after(
+        (hidden_pair, branch_other, cot_sent, grad_up)
+    )
+    cot_got = send(cot_sent, "zl")
     hidden_got = lax.dynamic_index_in_dim(hidden_pair, 1 - side, 0, keepdims=False)
     hidden_too = send(hidden_got, "c")
-
-    def beside(hidden_got, hidden_too, first_turned, second_turned, mixed_low, grad_packed, grad_up):
+    branch = branch + send(branch_other, "c")
+    hidden_too, branch = after((hidden_too, branch))
+
+    def beside(hidden_got, hidden_too, first_turned, second_turned, grad_packed, grad_up):
         first_far, second_far, first_turned, second_turned = norm_call(
             first_far_kernel,
             128,
@@ -541,7 +595,6 @@
         marks_got = hidden_got[half_rows, : 2 * TOK].reshape(2, 2, half_rows)
         marks_far = jnp.where(core == 0, marks_got, marks_got[:, ::-1]).reshape(2, TOK)
         projected_far = project(far_place, 1, first_far, qkv_weight, qkv_bias, marks_far)
-        branches = branch_halves(at_core, mixed_low, act_low, dense_weight, fc2_weight)
         backs = back_halves(
             at_core,
             grad_packed,
@@ -553,15 +606,13 @@
             ln1_gain,
             ln2_gain,
         )
-        return first_turned, second_turned, slope_side, marks_far, *branches, *backs, *projected_far
+        return first_turned, second_turned, slope_side, marks_far, *backs, *projected_far
 
     (
         first_turned,
         second_turned,
         slope_side,
         marks_far,
-        branch,
-        branch_other,
         combined,
         combined_other,
         norms,
@@ -574,27 +625,22 @@
         hidden_too,
         first_turned,
         second_turned,
-        mixed_low,
         grad_packed,
         grad_up,
     )
 
-    slope_side, projected_far, cot_got, branch_other, combined_other = after(
-        (slope_side, projected_far, cot_got, branch_other, combined_other)
-    )
-    cot_far, cot_turned = norm_call(
-        cot_far_kernel,
-        128,
-        (cot_got, send(cot_got, "c")),
-        1,
-        1,
-        (),
-        (cot_turned,),
-    )
-    grad_up_far = feed_back(at_side, cot_far, fc2_weight, slope_side)
-    mixed_far, grad_packed_far = attend(
-        far_place, 1, projected_far, cot_far, dense_weight, marks_far
-    )
+    slope_side, cot_got, combined_other = after((slope_side, cot_got, combined_other))
+    cot_too = send(cot_got, "c")
+    combined_too = send(combined_other, "c")
+    held = cot_far_half(0, at_side, cot_got, fc2_weight, slope_side, dense_weight, (cot_turned,))
+    *held, cot_too, combined_too = after((*held, cot_too, combined_too))
+    combined = combined + combined_too
+    branch = lax.psum(branch, "zh")
+    combined = lax.psum(combined, "zh")
+    grad_up_far, grad_mixed_far, cot_turned = cot_far_half(
+        1, at_side, cot_too, fc2_weight, slope_side, dense_weight, held
+    )
+    mixed_far, grad_packed_far = attend(far_place, 1, projected_far, grad_mixed_far, marks_far)
     joint_grad = joint(
         at_side,
         (second_turned, cot_turned, first_turned),
@@ -602,12 +648,9 @@
     )
     joint_grad, down_sum = after((joint_grad, down_sum))
     joint_sum = after(lax.psum_scatter(joint_grad, ("x", "y"), scatter_dimension=0, tiled=True))
-    _, norms, grad_packed, grad_up, cotangent, down_sum, branch, combined = after(
-        (joint_grad, norms, grad_packed, grad_up, cotangent, down_sum, branch, combined)
-    )
-    branch = branch + send(branch_other, "c")
-    combined = combined + send(combined_other, "c")
-    branch_too, combined_too = send(branch, "zh"), send(combined, "zh")
+    _, norms, grad_packed, grad_up, cotangent, down_sum = after(
+        (joint_grad, norms, grad_packed, grad_up, cotangent, down_sum)
+    )
 
     norms = norms[:4].reshape(4, 32, 64).transpose(1, 0, 2).reshape(32, 256)
     grad_out = cotangent.astype(F32)
@@ -632,10 +675,8 @@
     far_small = lax.dynamic_slice_in_dim(small, (1 - side) * 16 + block, 1, 0)
     small = (own_small + send(far_small, "zl")).reshape(-1)
 
-    small, branch_too, combined_too = after((small, branch_too, combined_too))
-    branch = branch + branch_too
-    combined = combined + combined_too
-    norms = small[:256]
+    small, branch, combined = after((small, branch, combined))
+    norms, joint_sum = after((small[:256], joint_sum))
     norms = norms + send(norms, "c")
     norms = (norms + send(norms, "zh")).reshape(4, 64)
     bias_total = small[256:320]

time: 332 us -> 322 us (0.970)
  starting transfers between devices: 30.8 us -> 16.9 us
    psum x0 -> x1, waiting for transfers between devices: none -> 54.1 us  [body(): branch = lax.psum(branch, 'zh')]
    ppermute x14 -> x12, waiting for transfers between devices: 74 us -> 30.9 us  [send(): return lax.ppermute(value, axis, [(i, (i + step) % n) for i in range(n)])]
    ppermute x14 -> x12, starting transfers between devices: 20.3 us -> 6.84 us  [send(): return lax.ppermute(value, axis, [(i, (i + step) % n) for i in range(n)])]
    pallas_call x2 -> x3, Pallas kernels: 16.9 us -> 25.7 us  [the longest x2 13.4 us: cot_far_half(): pl.pallas_call(partial(cot_far_kernel, len(held)), grid_spec=pltpu.Prefet...]
    all_gather x1, waiting for transfers between devices: 7.38 us -> 0.01 us  [body(): hidden_pair = lax.all_gather(hidden_sent, 'zl')]
    pallas_call x4 -> x3, Pallas kernels: 21.1 us -> 15.9 us  [norm_call(): pl.pallas_call(kernel, grid=(steps,), in_specs=specs + [whole((1, D))] *...]
    pallas_call x2, Pallas kernels: 15.7 us -> 10.9 us  [attend(): pl.pallas_call(attend_kernel, grid_spec=pltpu.PrefetchScalarGridSpec(num_...]
    unnamed x62 -> x64, local copies, waits for them, and re-layouts: 9.23 us -> 11.8 us
  transfers between devices with their start and end apart: 21 -> 20, of which waited for: 14 -> 10; matrix products, arithmetic and copies ran while one was open for 12% -> 12% of each run, Pallas kernels for 40% -> 41%
where the time goes in v3:
time: 322 us; the launch traced here: 318 us
  Pallas kernels  129 us (40%)
  waiting for transfers between devices  100 us (31%)
  other arithmetic  28.5 us (9%)
  local copies, waits for them, and re-layouts  26.2 us (8%)
  starting transfers between devices  16.9 us (5%)
  between operations  16.1 us (5%)
    psum x1, waiting for transfers between devices, body(): branch = lax.psum(branch, 'zh')  54.1 us
    ppermute x12, waiting for transfers between devices, send(): return lax.ppermute(value, axis, [(i, (i + step) % n) for i in range(n)])  30.9 us
    pallas_call x2, Pallas kernels, halves_call(): pl.pallas_call(kernel, grid_spec=pltpu.PrefetchScalarGridSpec(num_scalar_...  25.2 us
    pallas_call x1, Pallas kernels, feed(): pl.pallas_call(feed_kernel, grid=(units // width,), in_specs=[whole((TOK,...  16.6 us
    pallas_call x3, Pallas kernels, norm_call(): pl.pallas_call(kernel, grid=(steps,), in_specs=specs + [whole((1, D))] *...  15.9 us
    pallas_call x1, Pallas kernels, joint(): pl.pallas_call(joint_kernel, grid_spec=pltpu.PrefetchScalarGridSpec(num_s...  15.8 us
    ppermute x4, waiting for transfers between devices, swap(): return lax.ppermute(value, axis, [(i, i ^ bit) for i in range(SIZES[axis])])  15.4 us
    pallas_call x2, Pallas kernels, project(): pl.pallas_call(project_kernel, grid_spec=pltpu.PrefetchScalarGridSpec(num...  13.7 us
  transfers between devices with their start and end apart: 20, of which 10 were waited for; matrix products, arithmetic and copies ran while one was open for 12% of the time, Pallas kernels for 41%

profile of v3, /device:TPU:0, one launch (start us, length us, event | category | flops | bytes accessed | tf_op | source)
XLA Modules:
  0.0 317.8 jit_solution(15304218245513442019)
XLA Ops:
  13.3 4.7 %shard_map.281 = (bf16[512,2048]{1,0:T(8,128)(2,1)}, bf16[16,2,64,1024]{3,2,1,0:T(8,128)(2,1)}, f32[512,128]{1,0:T(8,128)S(1)}) custom-call(bf16[512,2048]{1,0:T(8,128)(2,1)S(1)} %copy-done.2, bf16[512,2048]{1,0:T(8,128)(2,1)} %cot.2, f32[1,2048]{1,0:T(1,128)S(1)} %bitcast.57, f32[1,2048]{1,0:T(1,128)S(1)} %bitcast.69), custom_call_target="tpu_custom_call" | custom-call | flops 1000000 | bytes 1000000 | tf_op jit(solution)/shard_map/pallas_call | solution.py:121
  18.0 16.6 %shard_map.282 = (bf16[512,2048]{1,0:T(8,128)(2,1)}, f32[512,2048]{1,0:T(8,128)}, f32[16,128,2048]{2,1,0:T(8,128)}) custom-call(bf16[512,2048]{1,0:T(8,128)(2,1)} %get-tuple-element.236.second, bf16[16,2,64,1024]{3,2,1,0:T(8,128)(2,1)} %get-tuple-element.237.cot_turned.refs_0_, bf16[2048,2048]{1,0:T(8,128)(2,1)} %weight.5, f32[4,4,128]{2,1,0:T(4,128)S(1)} %bitcast.79), custom_call_target="tpu_custom_call" | custom-call | flops 1000000 | bytes 1000000 | tf_op jit(solution)/shard_map/pallas_call | solution.py:161
  35.9 3.9 %shard_map.283 = (bf16[512,2048]{1,0:T(8,128)(2,1)}, bf16[16,2,64,1024]{3,2,1,0:T(8,128)(2,1)}, bf16[16,2,64,1024]{3,2,1,0:T(8,128)(2,1)}) custom-call(bf16[512,2048]{1,0:T(8,128)(2,1)S(1)} %copy-done.2, f32[1,2048]{1,0:T(1,128)S(1)} %bitcast.64, f32[1,2048]{1,0:T(1,128)S(1)} %bitcast.76, f32[1,2048]{1,0:T(1,128)S(1)} %bitcast.58, f32[1,2048]{1,0:T(1,128)S(1)} %bitcast.70), custom_call_target="tpu_custom_call" | custom-call | flops 1000000 | bytes 1000000 | tf_op jit(solution)/shard_map/pallas_call | solution.py:121
  39.9 12.3 %shard_map.285 = (bf16[512,2048]{1,0:T(8,128)(2,1)}, bf16[512,512]{1,0:T(8,128)(2,1)}) custom-call(bf16[512,2048]{1,0:T(8,128)(2,1)} %cot.2, bf16[2048,2048]{1,0:T(8,128)(2,1)} %weight.9, f32[512,2048]{1,0:T(8,128)} %get-tuple-element.248.slope, bf16[512,2048]{1,0:T(8,128)(2,1)} %dense.7), custom_call_target="tpu_custom_call" | custom-call | flops 1000000 | bytes 1000000 | tf_op jit(solution)/shard_map/pallas_call | solution.py:193
  52.7 7.5 %shard_map.284 = (bf16[512,512]{1,0:T(8,128)(2,1)}, bf16[512,512]{1,0:T(8,128)(2,1)}, bf16[512,512]{1,0:T(8,128)(2,1)}, f32[512,128]{1,0:T(8,128)}, f32[512,128]{1,0:T(8,128)}, /*index=5*/f32[512,128]{1,0:T(8,128)}) custom-call(s32[2]{0:T(128)} %broadcast_5_place.2.place, bf16[512,2048]{1,0:T(8,128)(2,1)} %get-tuple-element.240.first, ...), custom_call_target="tpu_custom_call" | custom-call | flops 1000000 | bytes 1000000 | tf_op jit(solution)/shard_map/pallas_call | solution.py:337
  60.2 6.3 %shard_map.286 = (bf16[512,512]{1,0:T(8,128)(2,1)}, bf16[512,1536]{1,0:T(8,128)(2,1)S(1)}) custom-call(s32[2]{0:T(128)} %broadcast_5_place.2.place, bf16[512,512]{1,0:T(8,128)(2,1)} %get-tuple-element.241.queries, bf16[512,512]{1,0:T(8,128)(2,1)} %get-tuple-element.242.keys, bf16[512,512]{1,0:T(8,128)(2,1)} %get-tuple-element.243.values, ...), custom_call_target="tpu_custom_call" | custom-call | flops 1000000 | bytes 1000000 | tf_op jit(solution)/shard_map/pallas_call | solution.py:389
  66.5 11.7 %shard_map.287 = (f32[256,2048]{1,0:T(8,128)}, f32[256,2048]{1,0:T(8,128)}) custom-call(s32[1]{0:T(128)} %bitcast.17.core, bf16[512,512]{1,0:T(8,128)(2,1)} %get-tuple-element.250.mixed.refs_5_, bf16[512,2048]{1,0:T(8,128)(2,1)} %get-tuple-element.251.act, bf16[512,2048]{1,0:T(8,128)(2,1)} %dense.7, bf16[2048,2048]{1,0:T(8,128)(2,1)} %weight.9), custom_call_target="tpu_custom_call" | custom-call | flops 1000000 | bytes 1000000 | tf_op jit(solution)/shard_map/pallas_call | solution.py:436
  79.8 3.2 %dynamic-slice_bitcast_fusion = f32[264,2048]{1,0:T(8,128)} fusion(f32[2,264,2048]{2,1,0:T(8,128)} %bitcast.55, s32[]{:T(128)S(6)} %select_n.59), kind=kLoop, calls=%fused_computation.10 | loop fusion | bytes 4325380 | tf_op jit(solution)/shard_map/jit(dynamic_index_in_dim)/squeeze | solution.py:579
  85.4 5.2 %collective-permute-done.1 = f32[256,2048]{1,0:T(8,128)} collective-permute-done((f32[256,2048]{1,0:T(8,128)}, f32[256,2048]{1,0:T(8,128)}, u32[]{:S(2)}, u32[]{:S(2)}) %collective-permute-start.1) | collective-permute-done | bytes 2097184 | tf_op jit(solution)/shard_map/ppermute | solution.py:27
  90.7 4.0 %add.106 = f32[256,2048]{1,0:T(8,128)} add(f32[256,2048]{1,0:T(8,128)} %get-tuple-element.255, f32[256,2048]{1,0:T(8,128)} %collective-permute-done.1) | non-fusion elementwise | flops 524288 | bytes 6291456 | tf_op jit(solution)/shard_map/add | solution.py:581
  94.7 33.5 %conditional.1 = (bf16[16,2,64,1024]{3,2,1,0:T(8,128)(2,1)}, bf16[16,2,64,1024]{3,2,1,0:T(8,128)(2,1)}, f32[512,1024]{1,0:T(8,128)S(1)}, f32[2,512]{1,0:T(2,128)...) conditional(s32[]{:T(128)} %convert_element_type.40, ...), branch_computations={%region_0.1_spmd, %region_1.2_spmd} | conditional | flops 4001025 | bytes 29243846 | solution.py:620
  95.6 7.3 %branch_1_fun.4 = (bf16[512,2048]{1,0:T(8,128)(2,1)}, bf16[512,2048]{1,0:T(8,128)(2,1)}, bf16[16,2,64,1024]{3,2,1,0:T(8,128)(2,1)}, bf16[16,2,64,1024]{3,2,1,0:T(8,128)(2,1)}) custom-call(f32[264,2048]{1,0:T(8,128)} %get-tuple-element.118.near, f32[264,2048]{1,0:T(8,128)} %get-tuple-element.119.other, ...), custom_call_target="tpu_custom_call", output_to_operand_aliasing={{2}: (6, {}), {3}: (7, {})} | custom-call | flops 1000000 | bytes 1000000 | tf_op jit(solution)/shard_map/cond/branch_1_fun/pallas_call | solution.py:121
  103.1 6.2 %branch_1_fun.7 = (bf16[512,256]{1,0:T(8,128)(2,1)}, bf16[512,256]{1,0:T(8,128)(2,1)}, bf16[512,256]{1,0:T(8,128)(2,1)}, f32[512,128]{1,0:T(8,128)}, f32[512,128]{1,0:T(8,128)}, /*index=5*/f32[512,128]{1,0:T(8,128)}) custom-call(s32[2]{0:T(128)S(1)} %get-tuple-element.142.place, bf16[512,2048]{1,0:T(8,128)(2,1)} %get-tuple-element.143.first, ...), custom_call_target="tpu_custom_call" | custom-call | flops 1000000 | bytes 1000000 | tf_op jit(solution)/shard_map/cond/branch_1_fun/pallas_call | solution.py:337
  109.2 13.5 %branch_1_fun.6 = (f32[256,2048]{1,0:T(8,128)}, f32[256,2048]{1,0:T(8,128)}, f32[8,2048]{1,0:T(8,128)S(1)}) custom-call(s32[1]{0:T(128)} %get-tuple-element.133.core, bf16[512,1536]{1,0:T(8,128)(2,1)S(1)} %get-tuple-element.134.packed, bf16[512,2048]{1,0:T(8,128)(2,1)} %get-tuple-element.135.up_grad, bf16[2048,1536]{1,0:T(8,128)(2,1)S(1)} %copy-done.1, ...), custom_call_target="tpu_custom_call" | custom-call | flops 1000000 | bytes 1000000 | tf_op jit(solution)/shard_map/cond/branch_1_fun/pallas_call | solution.py:436
  122.7 5.5 %branch_1_fun.5 = f32[512,1024]{1,0:T(8,128)S(1)} custom-call(s32[1]{0:T(128)} %get-tuple-element.128.side, bf16[512,2048]{1,0:T(8,128)(2,1)} %get-tuple-element.129.second, bf16[2048,2048]{1,0:T(8,128)(2,1)} %get-tuple-element.130.weight.up, f32[4,4,128]{2,1,0:T(4,128)S(1)} %bitcast.81), custom_call_target="tpu_custom_call" | custom-call | flops 1000000 | bytes 1000000 | tf_op jit(solution)/shard_map/cond/branch_1_fun/pallas_call | solution.py:267
  128.2 3.3 %collective-permute-done.2.rows = f32[256,2048]{1,0:T(8,128)} collective-permute-done((f32[256,2048]{1,0:T(8,128)}, f32[256,2048]{1,0:T(8,128)}, u32[]{:S(2)}, u32[]{:S(2)}) %collective-permute-start.2) | collective-permute-done | bytes 2097184 | tf_op jit(solution)/shard_map/ppermute | solution.py:27
  132.2 6.5 %shard_map.288 = (bf16[512,1024]{1,0:T(8,128)(2,1)}, bf16[512,256]{1,0:T(8,128)(2,1)}, bf16[16,2,64,1024]{3,2,1,0:T(8,128)(2,1)}) custom-call(s32[1]{0:T(128)} %bitcast.13.side, f32[256,2048]{1,0:T(8,128)} %collective-permute-done.2.rows, bf16[2048,2048]{1,0:T(8,128)(2,1)} %weight.9, ...), custom_call_target="tpu_custom_call", output_to_operand_aliasing={{2}: (5, {})} | custom-call | flops 1000000 | bytes 1000000 | tf_op jit(solution)/shard_map/pallas_call | solution.py:233
  140.8 7.0 %shard_map.289 = (bf16[512,1024]{1,0:T(8,128)(2,1)}, bf16[512,256]{1,0:T(8,128)(2,1)}, bf16[16,2,64,1024]{3,2,1,0:T(8,128)(2,1)}) custom-call(s32[1]{0:T(128)} %bitcast.13.side, f32[256,2048]{1,0:T(8,128)} %collective-permute-done.3.rows, bf16[2048,2048]{1,0:T(8,128)(2,1)} %weight.9, ...), custom_call_target="tpu_custom_call", output_to_operand_aliasing={{0}: (5, {}), {1}: (6, {}), {2}: (7, {})} | custom-call | flops 1000000 | bytes 1000000 | tf_op jit(solution)/shard_map/pallas_call | solution.py:233
  147.7 4.7 %shard_map.290 = (bf16[512,256]{1,0:T(8,128)(2,1)}, bf16[512,768]{1,0:T(8,128)(2,1)}) custom-call(s32[2]{0:T(128)S(1)} %pad_add_fusion.place, bf16[512,256]{1,0:T(8,128)(2,1)} %get-tuple-element.280.queries, bf16[512,256]{1,0:T(8,128)(2,1)} %get-tuple-element.281.keys, bf16[512,256]{1,0:T(8,128)(2,1)} %get-tuple-element.282.values, ...), custom_call_target="tpu_custom_call" | custom-call | flops 1000000 | bytes 1000000 | tf_op jit(solution)/shard_map/pallas_call | solution.py:389
  152.4 15.8 %shard_map.291 = f32[16,128,2048]{2,1,0:T(8,128)} custom-call(s32[1]{0:T(128)} %bitcast.13.side, bf16[16,2,64,1024]{3,2,1,0:T(8,128)(2,1)} %get-tuple-element.263.refs_0_, bf16[16,2,64,1024]{3,2,1,0:T(8,128)(2,1)} %get-tuple-element.277.refs_1_, bf16[16,2,64,1024]{3,2,1,0:T(8,128)(2,1)S(1)} %copy-done.6, bf16[512,2048]{1,0:T(8,128)(2,1)S(1)} %copy-done.7, ...), custom_call_target="tpu_custom_call" | custom-call | flops 1000000 | bytes 1000000 | tf_op jit(solution)/shard_map/pallas_call | solution.py:502
  169.8 2.4 convert_reduce_fusion
  176.8 2.7 collective-permute-done.5
  179.5 3.1 collective-permute-start.6
  182.7 4.2 %collective-permute-done.6 = f32[32,512]{1,0:T(8,128)S(1)} collective-permute-done((f32[32,512]{1,0:T(8,128)S(1)}, f32[32,512]{1,0:T(8,128)S(1)}, u32[]{:S(2)}, u32[]{:S(2)}) %collective-permute-start.6) | collective-permute-done | bytes 65568 | tf_op jit(solution)/shard_map/ppermute | solution.py:31
  188.5 4.1 %collective-permute-done.7 = f32[32,512]{1,0:T(8,128)S(1)} collective-permute-done((f32[32,512]{1,0:T(8,128)S(1)}, f32[32,512]{1,0:T(8,128)S(1)}, u32[]{:S(2)}, u32[]{:S(2)}) %collective-permute-start.7) | collective-permute-done | bytes 65568 | tf_op jit(solution)/shard_map/ppermute | solution.py:31
  192.6 3.0 collective-permute-start.8
  195.6 4.4 %collective-permute-done.8 = f32[32,512]{1,0:T(8,128)S(1)} collective-permute-done((f32[32,512]{1,0:T(8,128)S(1)}, f32[32,512]{1,0:T(8,128)S(1)}, u32[]{:S(2)}, u32[]{:S(2)}) %collective-permute-start.8) | collective-permute-done | bytes 65568 | tf_op jit(solution)/shard_map/ppermute | solution.py:31
  202.2 2.5 convert_element_type.46
  204.8 54.1 %all-reduce.6.cloned.1.call-done = (f32[256,2048]{1,0:T(8,128)}, f32[256,2048]{1,0:T(8,128)}) async-done(((f32[256,2048]{1,0:T(8,128)}, f32[256,2048]{1,0:T(8,128)}), (f32[256,2048]{1,0:T(8,128)}, f32[256,2048]{1,0:T(8,128)})) %all-reduce.6.cloned.1.call-update) | async-done | bytes 4194320 | tf_op jit(solution)/shard_map/psum | solution.py:638
  261.1 4.3 %fusion.11 = (f32[256]{0:T(256)S(1)}, f32[256]{0:T(256)S(1)}, f32[512,2048]{1,0:T(8,128)S(1)}, f32[256,2048]{1,0:T(8,128)}) fusion(f32[256,2048]{1,0:T(8,128)S(1)} %copy-done.11, f32[256]{0:T(256)S(1)} %get-tuple-element.350, f32[256]{0:T(256)S(1)} %get-tuple-element.351, bf16[512,2048]{1,0:T(8,128)(2,1)S(1)} %copy-done.3, s32[]{:T(128)S(6)} %select_n.58, ...), kind=kLoop, calls=%fused_computation.47 | loop fusion | flops 4718080 | bytes 9457668 | tf_op jit(solution)/shard_map/reduce_sum | solution.py:690
  276.1 13.1 %collective-permute-done.15 = f32[64,2048]{1,0:T(8,128)} collective-permute-done((f32[64,2048]{1,0:T(8,128)}, f32[64,2048]{1,0:T(8,128)}, u32[]{:S(2)}, u32[]{:S(2)}) %collective-permute-start.15) | collective-permute-done | bytes 524320 | tf_op jit(solution)/shard_map/ppermute | solution.py:27
  297.5 8.9 %collective-permute-done.13 = f32[256]{0:T(256)S(1)} collective-permute-done((f32[256]{0:T(256)S(1)}, f32[256]{0:T(256)S(1)}, u32[]{:S(2)}, u32[]{:S(2)}) %collective-permute-start.13) | collective-permute-done | bytes 1056 | tf_op jit(solution)/shard_map/ppermute | solution.py:27
  (167 shorter events, 49.5 us)
Async XLA Ops:
  8.0 71.8 %all-gather.3.cloned.1.call-start = ((), (), s32[]{:S(2)}) async-start(), calls=%async_computation.2 | async-start | bytes 6488064 | tf_op jit(solution)/shard_map/all_gather | solution.py:558
  11.7 156.5 %reduce-scatter.7.cloned.1.call-start = ((), (), s32[]{:S(2)}) async-start(), calls=%async_computation.3 | async-start | bytes 17825792
  34.7 224.2 %all-reduce.6.cloned.1.call-start = ((), (), s32[]{:S(2)}) async-start(), calls=%async_computation.5 | async-start | bytes 8388608 | tf_op jit(solution)/shard_map/psum | solution.py:638
  39.9 12.8 %slice-start = ((s8[6291456]{0:T(1024)(128)(4,1)}), s8[4194304]{0:T(1024)(128)(4,1)S(1)}, s32[]{:S(2)}) async-start(s8[6291456]{0:T(1024)(128)(4,1)} %bitcast.53), calls=%async_computation.6 | async-start | bytes 8388608
  39.9 12.8 %slice-start.1 = ((s8[6291456]{0:T(1024)(128)(4,1)}), s8[2097152]{0:T(1024)(128)(4,1)S(1)}, s32[]{:S(2)}) async-start(s8[6291456]{0:T(1024)(128)(4,1)} %bitcast.53), calls=%async_computation.7 | async-start | bytes 4194304
  39.9 12.8 %copy-start.21 = (f32[32,1]{1,0:T(8,128)S(1)}, f32[32,1]{1,0:T(8,128)}, u32[]{:S(2)}) copy-start(f32[32,1]{1,0:T(8,128)} %constant.61.clone.inverse) | copy-start | bytes 388
  39.9 12.8 %copy-start.27 = (f32[2,768]{1,0:T(2,128)S(1)}, f32[2,768]{1,0:T(2,128)}, u32[]{:S(2)}) copy-start(f32[2,768]{1,0:T(2,128)} %bias.1) | copy-start | bytes 18436
  66.5 86.0 %copy-start.8 = (bf16[512,1536]{1,0:T(8,128)(2,1)}, bf16[512,1536]{1,0:T(8,128)(2,1)S(1)}, u32[]{:S(2)}) copy-start(bf16[512,1536]{1,0:T(8,128)(2,1)S(1)} %get-tuple-element.295.refs_7_) | copy-start | bytes 4718596
  66.5 11.7 %copy-start.4 = (bf16[512,2048]{1,0:T(8,128)(2,1)S(1)}, bf16[512,2048]{1,0:T(8,128)(2,1)}, u32[]{:S(2)}) copy-start(bf16[512,2048]{1,0:T(8,128)(2,1)} %cot.2) | copy-start | bytes 6291460
  83.1 11.6 %collective-permute-start = (f32[264,2048]{1,0:T(8,128)}, f32[264,2048]{1,0:T(8,128)}, u32[]{:S(2)}, u32[]{:S(2)}) collective-permute-start(f32[264,2048]{1,0:T(8,128)} %dynamic-slice_bitcast_fusion), channel_id=1, source_target_pairs={{0,1},{1,0},{2,3},{3,2},{4,5},{5,4},{6,7},{7,6},{8,9},{9,8},{10,11... | collective-permute-start | bytes 6488072 | tf_op jit(solution)/shard_map/ppermute | solution.py:27
  83.1 7.6 %collective-permute-start.1 = (f32[256,2048]{1,0:T(8,128)}, f32[256,2048]{1,0:T(8,128)}, u32[]{:S(2)}, u32[]{:S(2)}) collective-permute-start(f32[256,2048]{1,0:T(8,128)} %get-tuple-element.256), channel_id=1, source_target_pairs={{0,1},{1,0},{2,3},{3,2},{4,5},{5,4},{6,7},{7,6},{8,9},{9,8},{10,11... | collective-permute-start | bytes 6291464 | tf_op jit(solution)/shard_map/ppermute | solution.py:27
  83.6 47.9 %collective-permute-start.2 = (f32[256,2048]{1,0:T(8,128)}, f32[256,2048]{1,0:T(8,128)}, u32[]{:S(2)}, u32[]{:S(2)}) collective-permute-start(f32[256,2048]{1,0:T(8,128)} %dynamic-slice_convert_fusion), channel_id=1, source_target_pairs={{0,64},{64,0},{1,65},{65,1},{2,66},{66,2},{3,67},{67,3},{4,68},{68... | collective-permute-start | bytes 6291464 | tf_op jit(solution)/shard_map/ppermute | solution.py:27
  131.5 7.2 %collective-permute-start.4 = (f32[256,2048]{1,0:T(8,128)}, f32[256,2048]{1,0:T(8,128)S(1)}, u32[]{:S(2)}, u32[]{:S(2)}) collective-permute-start(f32[256,2048]{1,0:T(8,128)} %get-tuple-element.272), channel_id=1, source_target_pairs={{0,1},{1,0},{2,3},{3,2},{4,5},{5,4},{6,7},{7,6},{8,9},{9,8},{10,11... | collective-permute-start | bytes 6291464 | tf_op jit(solution)/shard_map/ppermute | solution.py:27
  131.5 7.5 %collective-permute-start.3 = (f32[256,2048]{1,0:T(8,128)}, f32[256,2048]{1,0:T(8,128)}, u32[]{:S(2)}, u32[]{:S(2)}) collective-permute-start(f32[256,2048]{1,0:T(8,128)} %collective-permute-done.2.rows), channel_id=1, source_target_pairs={{0,1},{1,0},{2,3},{3,2},{4,5},{5,4},{6,7},{7,6},{8,9},{9,8},{10,11... | collective-permute-start | bytes 6291464 | tf_op jit(solution)/shard_map/ppermute | solution.py:27
  140.7 150.5 %reduce-scatter.9.cloned.1.call-start = ((), (), s32[]{:S(2)}) async-start(), calls=%async_computation.4 | async-start | bytes 17825792
  140.7 11.7 %copy-start.6 = (bf16[16,2,64,1024]{3,2,1,0:T(8,128)(2,1)S(1)}, bf16[16,2,64,1024]{3,2,1,0:T(8,128)(2,1)}, u32[]{:S(2)}) copy-start(bf16[16,2,64,1024]{3,2,1,0:T(8,128)(2,1)} %get-tuple-element.278.refs_2_) | copy-start | bytes 12582916
  140.7 11.7 %copy-start.7 = (bf16[512,2048]{1,0:T(8,128)(2,1)S(1)}, bf16[512,2048]{1,0:T(8,128)(2,1)}, u32[]{:S(2)}) copy-start(bf16[512,2048]{1,0:T(8,128)(2,1)} %get-tuple-element.296.refs_3_) | copy-start | bytes 6291460
  175.2 4.3 %collective-permute-start.5 = (f32[32,512]{1,0:T(8,128)S(1)}, f32[32,512]{1,0:T(8,128)S(1)}, u32[]{:S(2)}, u32[]{:S(2)}) collective-permute-start(f32[32,512]{1,0:T(8,128)S(1)} %concatenate.36), channel_id=1, source_target_pairs={{0,16},{16,0},{32,48},{48,32},{1,17},{17,1},{33,49},{49,33},{2,18}... | collective-permute-start | bytes 196616 | tf_op jit(solution)/shard_map/ppermute | solution.py:31
  179.5 7.3 %collective-permute-start.6 = (f32[32,512]{1,0:T(8,128)S(1)}, f32[32,512]{1,0:T(8,128)S(1)}, u32[]{:S(2)}, u32[]{:S(2)}) collective-permute-start(f32[32,512]{1,0:T(8,128)S(1)} %add.107), channel_id=1, source_target_pairs={{0,32},{16,48},{32,0},{48,16},{1,33},{17,49},{33,1},{49,17},{2,34}... | collective-permute-start | bytes 196616 | tf_op jit(solution)/shard_map/ppermute | solution.py:31
  186.8 5.7 %collective-permute-start.7 = (f32[32,512]{1,0:T(8,128)S(1)}, f32[32,512]{1,0:T(8,128)S(1)}, u32[]{:S(2)}, u32[]{:S(2)}) collective-permute-start(f32[32,512]{1,0:T(8,128)S(1)} %add.108), channel_id=1, source_target_pairs={{0,4},{4,0},{8,12},{12,8},{1,5},{5,1},{9,13},{13,9},{2,6},{6,2},{1... | collective-permute-start | bytes 196616 | tf_op jit(solution)/shard_map/ppermute | solution.py:31
  192.6 7.4 %collective-permute-start.8 = (f32[32,512]{1,0:T(8,128)S(1)}, f32[32,512]{1,0:T(8,128)S(1)}, u32[]{:S(2)}, u32[]{:S(2)}) collective-permute-start(f32[32,512]{1,0:T(8,128)S(1)} %add.109), channel_id=1, source_target_pairs={{0,8},{4,12},{8,0},{12,4},{1,9},{5,13},{9,1},{13,5},{2,10},{6,14},... | collective-permute-start | bytes 196616 | tf_op jit(solution)/shard_map/ppermute | solution.py:31
  200.0 4.7 %collective-permute-start.9 = (f32[1,512]{1,0:T(1,128)S(1)}, f32[1,512]{1,0:T(1,128)S(1)}, u32[]{:S(2)}, u32[]{:S(2)}) collective-permute-start(f32[1,512]{1,0:T(1,128)S(1)} %constant_dynamic-slice_fusion), channel_id=1, source_target_pairs={{0,64},{64,0},{1,65},{65,1},{2,66},{66,2},{3,67},{67,3},{4,68},{68... | collective-permute-start | bytes 6152 | tf_op jit(solution)/shard_map/ppermute | solution.py:27
  202.2 57.2 %copy-start.30 = (f32[2048]{0:T(1024)S(1)}, f32[2048]{0:T(1024)}, u32[]{:S(2)}) copy-start(f32[2048]{0:T(1024)} %param.34) | copy-start | bytes 24580
  202.2 57.2 %copy-start.31 = (f32[2048]{0:T(1024)S(1)}, f32[2048]{0:T(1024)}, u32[]{:S(2)}) copy-start(f32[2048]{0:T(1024)} %param.28) | copy-start | bytes 24580
  265.4 27.2 %collective-permute-start.10 = (f32[256,2048]{1,0:T(8,128)}, f32[256,2048]{1,0:T(8,128)S(1)}, u32[]{:S(2)}, u32[]{:S(2)}) collective-permute-start(f32[256,2048]{1,0:T(8,128)} %get-tuple-element.359), channel_id=1, source_target_pairs={{0,1},{1,0},{2,3},{3,2},{4,5},{5,4},{6,7},{7,6},{8,9},{9,8},{10,11... | collective-permute-start | bytes 6291464 | tf_op jit(solution)/shard_map/ppermute | solution.py:27
  273.8 21.9 %collective-permute-start.11 = (f32[256,2048]{1,0:T(8,128)}, f32[256,2048]{1,0:T(8,128)}, u32[]{:S(2)}, u32[]{:S(2)}) collective-permute-start(f32[256,2048]{1,0:T(8,128)} %get-tuple-element.355), channel_id=1, source_target_pairs={{0,1},{1,0},{2,3},{3,2},{4,5},{5,4},{6,7},{7,6},{8,9},{9,8},{10,11... | collective-permute-start | bytes 6291464 | tf_op jit(solution)/shard_map/ppermute | solution.py:27
  274.6 14.7 %collective-permute-start.15 = (f32[64,2048]{1,0:T(8,128)}, f32[64,2048]{1,0:T(8,128)}, u32[]{:S(2)}, u32[]{:S(2)}) collective-permute-start(f32[64,2048]{1,0:T(8,128)} %dynamic-slice_bitcast_fusion.1), channel_id=1, source_target_pairs={{0,64},{64,0},{1,65},{65,1},{2,66},{66,2},{3,67},{67,3},{4,68},{68... | collective-permute-start | bytes 1572872 | tf_op jit(solution)/shard_map/ppermute | solution.py:27
  275.4 34.2 %copy-start.32 = (f32[64]{0:T(128)}, f32[64]{0:T(128)S(1)}, u32[]{:S(2)}) copy-start(f32[64]{0:T(128)S(1)} %get-tuple-element.423) | copy-start | bytes 772
  291.1 2.9 collective-permute-start.12
  292.2 14.8 %collective-permute-start.14 = (f32[64,2048]{1,0:T(8,128)S(1)}, f32[64,2048]{1,0:T(8,128)S(1)}, u32[]{:S(2)}, u32[]{:S(2)}) collective-permute-start(f32[64,2048]{1,0:T(8,128)S(1)} %dynamic-slice_bitcast_fusion.2), channel_id=1, source_target_pairs={{0,64},{64,0},{1,65},{65,1},{2,66},{66,2},{3,67},{67,3},{4,68},{68... | collective-permute-start | bytes 1572872 | tf_op jit(solution)/shard_map/ppermute | solution.py:27
  294.1 12.4 %collective-permute-start.13 = (f32[256]{0:T(256)S(1)}, f32[256]{0:T(256)S(1)}, u32[]{:S(2)}, u32[]{:S(2)}) collective-permute-start(f32[256]{0:T(256)S(1)} %add.125), channel_id=1, source_target_pairs={{0,2},{2,0},{1,3},{3,1},{4,6},{6,4},{5,7},{7,5},{8,10},{10,8},{9,1... | collective-permute-start | bytes 3080 | tf_op jit(solution)/shard_map/ppermute | solution.py:27
  297.5 12.6 %copy-start.14 = (f32[512,2048]{1,0:T(8,128)}, f32[512,2048]{1,0:T(8,128)S(1)}, u32[]{:S(2)}) copy-start(f32[512,2048]{1,0:T(8,128)S(1)} %constant_dynamic-update-slice_fusion) | copy-start | bytes 12582916
  (22 other events, 79.5 us)
Sparse Core Ops, SparseCore 0:
  11.9 63.2 all-gather.2
  140.8 118.0 all-reduce.5
Sparse Core Ops, SparseCore 1:
  34.8 112.8 reduce-scatter.6
  168.4 114.9 reduce-scatter.8
